TPU v7x, 256 devices: a whole 4x4x8 slice. The times are simulated.
256 devices in a mesh: tm: 64 (over z, y, x_lo), space: 4 (over x_hi, core).
Axes of the slice: x: 4 (x_hi: 2, x_lo: 2; x = x_hi * 2 + x_lo), y: 4, z: 8, core: 2. Of those that a mesh axis runs over, the one named last changes fastest.
Arguments:
- qkv: bfloat16 [3, 256, 128, 4096], P(None, 'tm', 'space'), may hold values from -32 to 32
- clip_lengths: int32 [16], replicated, may hold values from 1 to 40, 256 in all
- wo: bfloat16 [4096, 4096], P(None, 'space'), may hold values from -0.09375 to 0.09375
Outputs:
- mixed: bfloat16 [256, 128, 4096], P('tm', 'space')
Inputs may be any that keep to these rules, and one draw needn't show every extreme that they name: `clip_lengths`: the lengths sum to 256; the longest is exactly 40.
All inputs are finite; a program needn't handle non-finite values.
Results may differ from a plain program's by a relative error of at most 0.013.
Values may be sent and summed in bfloat16 or wider, within the bound.
No kernel may reach another device: no remote copies, remote signals or barrier semaphores. Data moves between devices by JAX's collectives and lax.ppermute only.
A program may use at most 128 MiB of HBM per device.

v0:
```python
import jax
import jax.numpy as jnp
from jax import lax
from jax.sharding import PartitionSpec as P

HS = 128


def passed_along(block, axis, distance):
    devices = range(lax.axis_size(axis))
    route = [(i - distance, i) for i in devices if i - distance in devices]
    return lax.ppermute(block, axis, route)


def clip_ids(clip_lengths, frames):
    clip_ends = jnp.cumsum(clip_lengths)
    starts = clip_ends - clip_lengths
    return jnp.sum((starts[None, :] <= frames[:, None]).astype(jnp.int32), axis=1) - 1


def weights_of(scores, allowed):
    masked = jnp.where(allowed, scores, -1e30)
    top_score = jnp.max(masked, axis=-1, keepdims=True)
    raised = jnp.where(allowed, jnp.exp(masked - top_score), 0.0)
    return (raised / jnp.sum(raised, axis=-1, keepdims=True)).astype(jnp.bfloat16)


def spatial_attend(queries, key_rows, values, score_scale):
    scores = (
        jnp.einsum("fthd,fshd->fhts", queries, key_rows, preferred_element_type=jnp.float32)
        * score_scale
    )
    allowed = jnp.ones(scores.shape[-1:], dtype=bool)
    weights = weights_of(scores, allowed)
    return jnp.einsum(
        "fhts,fshd->fthd", weights, values, preferred_element_type=jnp.float32
    ).astype(jnp.bfloat16)


def on_device(qkv, clip_lengths, wo):
    frames_dev = qkv.shape[1]
    tok_dev = qkv.shape[2]
    model_width = qkv.shape[3]
    half_width = model_width // 2
    head_count = half_width // HS
    score_scale = HS ** (-0.5)
    time_count = lax.axis_size("tm")
    time_place = lax.axis_index("tm")
    frames_all = frames_dev * time_count
    own_frames = time_place * frames_dev + jnp.arange(frames_dev, dtype=jnp.int32)
    spatial = qkv[:, :, :, :half_width]
    keyvals = lax.all_gather(spatial[1:], "space", axis=2, tiled=True)
    queries = spatial[0].reshape(frames_dev, tok_dev, head_count, HS)
    key_rows = keyvals[0].reshape(frames_dev, -1, head_count, HS)
    values = keyvals[1].reshape(frames_dev, -1, head_count, HS)
    spatial_out = spatial_attend(queries, key_rows, values, score_scale)
    spatial_out = spatial_out.reshape(frames_dev, tok_dev, half_width)
    temporal = qkv[:, :, :, half_width:]
    longest = min(40, frames_all // 2)
    reach_devices = min((longest + frames_dev - 2) // frames_dev, time_count - 1)
    local_kv = temporal[1:]
    pieces = [local_kv]
    key_frames = [own_frames]
    for offset in range(1, reach_devices + 1):
        pieces.append(passed_along(local_kv, "tm", offset))
        key_frames.append(own_frames - offset * frames_dev)
    stacked = jnp.concatenate(pieces, axis=1)
    frames_key = jnp.concatenate(key_frames)
    clip_query = clip_ids(clip_lengths, own_frames)
    clip_key = clip_ids(clip_lengths, frames_key)
    allowed = (
        (clip_key[None, :] == clip_query[:, None])
        & (frames_key[None, :] <= own_frames[:, None])
        & (frames_key[None, :] >= 0)
    )
    queries = temporal[0].reshape(frames_dev, tok_dev, head_count, HS)
    key_rows = stacked[0].reshape(-1, tok_dev, head_count, HS)
    values = stacked[1].reshape(-1, tok_dev, head_count, HS)
    scores = (
        jnp.einsum("fthd,gthd->thfg", queries, key_rows, preferred_element_type=jnp.float32)
        * score_scale
    )
    weights = weights_of(scores, allowed)
    temporal_out = jnp.einsum(
        "thfg,gthd->fthd", weights, values, preferred_element_type=jnp.float32
    ).astype(jnp.bfloat16)
    temporal_out = temporal_out.reshape(frames_dev, tok_dev, half_width)
    attention = jnp.concatenate([spatial_out, temporal_out], axis=-1).reshape(
        frames_dev * tok_dev, model_width
    )
    columns = jnp.dot(
        lax.all_gather(attention, "space", axis=0, tiled=True),
        wo,
        preferred_element_type=jnp.float32,
    ).astype(jnp.bfloat16)
    projected = lax.all_to_all(columns, "space", split_axis=0, concat_axis=1, tiled=True)
    return projected.reshape(frames_dev, tok_dev, model_width)


def solution(mesh):
    return jax.shard_map(
        on_device,
        mesh=mesh,
        in_specs=(P(None, "tm", "space", None), P(), P(None, "space")),
        out_specs=P("tm", "space", None),
        check_vma=False,
    )
```

profile of v0, /device:TPU:2, one launch (start us, length us, event | category | flops | bytes accessed | tf_op | source)
XLA Modules:
  0.0 514.0 jit_solution(9894083017115072418)
XLA Ops:
  6.5 2.8 fusion.35
  9.4 3.4 collective-permute-start
  12.8 4.5 collective-permute-start.1
  17.3 4.7 collective-permute-start.2
  22.0 3.0 collective-permute-start.3
  25.0 4.9 collective-permute-start.4
  29.9 1.8 copy.45
  31.7 0.0 all-gather.3.cloned.1.call-update
  31.7 0.0 all-gather.5.cloned.1.call-start
  31.9 0.1 copy.37
  32.0 0.1 reduce
  32.1 0.1 concatenate.20
  32.2 1.3 fusion.34
  33.5 0.1 convert_reduce_fusion
  33.6 0.2 convert_reduce_fusion.1
  33.8 0.1 and_and_fusion
  33.8 0.9 copy.52
  34.7 0.9 copy.48
  35.7 1.7 collective-permute-done
  37.4 38.8 %collective-permute-start.5 = (bf16[2,4,32,2048]{3,2,1,0:T(8,128)(2,1)S(1)}, bf16[2,4,32,2048]{3,2,1,0:T(8,128)(2,1)S(1)}, u32[]{:S(2)}, u32[]{:S(2)}) collective-permute-start(bf16[2,4,32,2048]{3,2,1,0:T(8,128)(2,1)S(1)} %get-tuple-element.13), channel_id=1, source_target_pairs={{0,24},{4,28},{8,32},{12,36},{16,40},{20,44},{24,48},{28,52},{32,5... | collective-permute-start | bytes 3145736 | tf_op jit(solution)/shard_map/ppermute | solution.py:12
  76.2 2.3 constant_dynamic-update-slice_fusion.9
  78.5 0.0 collective-permute-done.1
  78.5 61.1 %collective-permute-start.6 = (bf16[2,4,32,2048]{3,2,1,0:T(8,128)(2,1)S(1)}, bf16[2,4,32,2048]{3,2,1,0:T(8,128)(2,1)S(1)}, u32[]{:S(2)}, u32[]{:S(2)}) collective-permute-start(bf16[2,4,32,2048]{3,2,1,0:T(8,128)(2,1)S(1)} %get-tuple-element.13), channel_id=1, source_target_pairs={{0,28},{4,32},{8,36},{12,40},{16,44},{20,48},{24,52},{28,56},{32,6... | collective-permute-start | bytes 3145736 | tf_op jit(solution)/shard_map/ppermute | solution.py:12
  139.6 2.3 constant_dynamic-update-slice_fusion.8
  142.0 0.0 collective-permute-done.2
  142.0 12.3 %collective-permute-start.7 = (bf16[2,4,32,2048]{3,2,1,0:T(8,128)(2,1)S(1)}, bf16[2,4,32,2048]{3,2,1,0:T(8,128)(2,1)S(1)}, u32[]{:S(2)}, u32[]{:S(2)}) collective-permute-start(bf16[2,4,32,2048]{3,2,1,0:T(8,128)(2,1)S(1)} %get-tuple-element.13), channel_id=1, source_target_pairs={{0,32},{4,36},{8,40},{12,44},{16,48},{20,52},{24,56},{28,60},{32,6... | collective-permute-start | bytes 3145736 | tf_op jit(solution)/shard_map/ppermute | solution.py:12
  154.3 2.3 constant_dynamic-update-slice_fusion.7
  156.6 0.0 collective-permute-done.3
  156.6 51.6 %collective-permute-start.8 = (bf16[2,4,32,2048]{3,2,1,0:T(8,128)(2,1)S(1)}, bf16[2,4,32,2048]{3,2,1,0:T(8,128)(2,1)S(1)}, u32[]{:S(2)}, u32[]{:S(2)}) collective-permute-start(bf16[2,4,32,2048]{3,2,1,0:T(8,128)(2,1)S(1)} %get-tuple-element.13), channel_id=1, source_target_pairs={{0,36},{4,40},{8,44},{12,48},{16,52},{20,56},{24,60},{28,64},{32,6... | collective-permute-start | bytes 3145736 | tf_op jit(solution)/shard_map/ppermute | solution.py:12
  208.1 1.1 constant_dynamic-update-slice_fusion.6
  209.2 0.0 collective-permute-done.4
  209.2 41.2 %collective-permute-start.9 = (bf16[2,4,32,2048]{3,2,1,0:T(8,128)(2,1)S(1)}, bf16[2,4,32,2048]{3,2,1,0:T(8,128)(2,1)S(1)}, u32[]{:S(2)}, u32[]{:S(2)}) collective-permute-start(bf16[2,4,32,2048]{3,2,1,0:T(8,128)(2,1)S(1)} %get-tuple-element.13), channel_id=1, source_target_pairs={{0,40},{4,44},{8,48},{12,52},{16,56},{20,60},{24,64},{28,68},{32,7... | collective-permute-start | bytes 3145736 | tf_op jit(solution)/shard_map/ppermute | solution.py:12
  250.4 1.1 constant_dynamic-update-slice_fusion.5
  251.6 0.0 collective-permute-done.5
  251.6 1.1 constant_dynamic-update-slice_fusion.4
  252.7 0.0 collective-permute-done.6
  252.7 1.0 constant_dynamic-update-slice_fusion.3
  253.7 0.0 collective-permute-done.7
  253.7 1.0 constant_dynamic-update-slice_fusion.2
  254.7 1.1 constant_dynamic-update-slice_fusion.1
  255.8 13.7 %collective-permute-done.9 = bf16[2,4,32,2048]{3,2,1,0:T(8,128)(2,1)S(1)} collective-permute-done((bf16[2,4,32,2048]{3,2,1,0:T(8,128)(2,1)S(1)}, bf16[2,4,32,2048]{3,2,1,0:T(8,128)(2,1)S(1)}, u32[]{:S(2)}, u32[]{:S(2)}) %collective-permute-start.9) | collective-permute-done | bytes 1048608 | tf_op jit(solution)/shard_map/ppermute | solution.py:12
  269.5 1.1 constant_dynamic-update-slice_fusion
  270.5 11.0 %fusion.32 = (bf16[1,44,32,2048]{3,2,1,0:T(8,128)(2,1)}, bf16[1,44,32,2048]{3,2,1,0:T(8,128)(2,1)}) fusion(bf16[2,44,32,2048]{3,2,1,0:T(8,128)(2,1)} %constant_dynamic-update-slice_fusion), kind=kLoop, calls=%fused_computation.58 | loop fusion | bytes 23068672 | tf_op jit(solution)/shard_map/slice | solution.py:77
  281.5 7.4 %copy.50 = bf16[176,8,16,128]{3,2,1,0:T(8,128)(2,1)} copy(bf16[176,8,16,128]{3,1,2,0:T(8,128)(2,1)} %bitcast.54) | data formatting | bytes 11534336
  289.0 4.7 copy.51
  293.7 7.7 %fusion.36 = (f32[32,16,4]{2,1,0:T(8,128)S(1)}, f32[32,16,4,44]{3,2,1,0:T(4,128)S(1)}) fusion(pred[4,44]{1,0:T(4,128)(4,1)S(1)} %and_and_fusion, bf16[44,32,16,128]{3,2,1,0:T(8,128)(2,1)} %bitcast.57, bf16[4,32,16,128]{3,2,1,0:T(8,128)(2,1)S(1)} %bitcast.68), kind=kOutput, calls=%fused_computation.62 | convolution fusion | flops 23519276 | bytes 6660272 | tf_op jit(solution)/shard_map/sub | solution.py:24
  301.4 6.5 %fusion.20 = bf16[4,32,16,128]{3,0,2,1:T(4,128)(2,1)S(1)} fusion(bf16[44,32,16,128]{3,2,1,0:T(8,128)(2,1)} %bitcast.56, f32[32,16,4,44]{3,2,1,0:T(4,128)S(1)} %get-tuple-element.15, f32[32,16,4]{2,1,0:T(8,128)S(1)} %get-tuple-element.14), kind=kOutput, calls=%fused_computation.17 | convolution fusion | flops 23511040 | bytes 6660096 | tf_op jit(solution)/shard_map/thfg,gthd->fthd/dot_general | solution.py:84
  307.8 0.1 copy.41
  307.9 0.9 copy.78
  308.9 4.6 fusion.33
  313.5 3.0 copy.47
  316.5 3.4 copy.46
  319.9 1.7 convolution_multiply_fusion
  321.6 0.6 fusion.37
  322.2 5.2 %fusion.23 = bf16[4,32,16,128]{3,1,2,0:T(8,128)(2,1)S(1)} fusion(bf16[4,128,16,128]{1,3,2,0:T(8,128)(2,1)} %bitcast.60, f32[4,16,32]{2,1,0:T(8,128)S(1)} %fusion.37, f32[4,16,32,128]{3,2,1,0:T(8,128)S(1)} %convolution_multiply_fusion), kind=kOutput, calls=%fused_computation.18 | convolution fusion | flops 68159616 | bytes 3678208 | tf_op jit(solution)/shard_map/fhts,fshd->fthd/dot_general | solution.py:35
  327.4 0.2 copy.36
  327.6 0.1 copy.79
  327.8 2.1 pad_maximum_fusion
  329.9 0.0 all-gather.5.cloned.1.call-update
  329.9 147.2 %all-gather.5.cloned.1.call-done = bf16[512,4096]{1,0:T(8,128)(2,1)} async-done(((bf16[128,4096]{1,0:T(8,128)(2,1)}), bf16[512,4096]{1,0:T(8,128)(2,1)}) %all-gather.5.cloned.1.call-update) | async-done | bytes 4194320 | tf_op jit(solution)/shard_map/all_gather | solution.py:92
  477.1 9.1 %convolution_convert_fusion = bf16[512,1024]{1,0:T(8,128)(2,1)S(1)} fusion(bf16[512,4096]{1,0:T(8,128)(2,1)} %all-gather.5.cloned.1.call-done, bf16[4096,1024]{1,0:T(8,128)(2,1)} %param.5), kind=kOutput, calls=%fused_computation.6 | convolution fusion | flops 4295491584 | bytes 13631488 | tf_op jit(solution)/shard_map/dot_general | solution.py:91
  486.3 18.5 %all_to_all.16 = bf16[4,128,1024]{2,1,0:T(8,128)(2,1)S(1)} all-to-all(bf16[4,128,1024]{2,1,0:T(8,128)(2,1)S(1)} %bitcast.67), channel_id=1, replica_groups=mesh['tm'=64,'space'=4] {'space'}, dimensions={0} | all-to-all | bytes 2097152 | tf_op jit(solution)/shard_map/all_to_all | solution.py:96
  504.7 0.8 copy.42
  505.6 1.6 reshape.127
  (23 shorter events, 0.1 us)
Async XLA Ops:
  6.5 25.3 %copy-start.1 = (s32[16]{0:T(128)S(1)}, s32[16]{0:T(128)}, u32[]{:S(2)}) copy-start(s32[16]{0:T(128)} %param.4) | copy-start | bytes 196
  6.5 302.3 %all-gather.3.cloned.1.call-start = ((), (), s32[]{:S(2)}) async-start(), calls=%async_computation.1 | async-start | bytes 5242880 | tf_op jit(solution)/shard_map/all_gather | solution.py:52
  9.4 28.0 %collective-permute-start = (bf16[2,4,32,2048]{3,2,1,0:T(8,128)(2,1)S(1)}, bf16[2,4,32,2048]{3,2,1,0:T(8,128)(2,1)}, u32[]{:S(2)}, u32[]{:S(2)}) collective-permute-start(bf16[2,4,32,2048]{3,2,1,0:T(8,128)(2,1)S(1)} %get-tuple-element.13), channel_id=1, source_target_pairs={{0,4},{4,8},{8,12},{12,16},{16,20},{20,24},{24,28},{28,32},{32,36}... | collective-permute-start | bytes 3145736 | tf_op jit(solution)/shard_map/ppermute | solution.py:12
  12.8 65.7 %collective-permute-start.1 = (bf16[2,4,32,2048]{3,2,1,0:T(8,128)(2,1)S(1)}, bf16[2,4,32,2048]{3,2,1,0:T(8,128)(2,1)}, u32[]{:S(2)}, u32[]{:S(2)}) collective-permute-start(bf16[2,4,32,2048]{3,2,1,0:T(8,128)(2,1)S(1)} %get-tuple-element.13), channel_id=1, source_target_pairs={{0,8},{4,12},{8,16},{12,20},{16,24},{20,28},{24,32},{28,36},{32,40... | collective-permute-start | bytes 3145736 | tf_op jit(solution)/shard_map/ppermute | solution.py:12
  17.3 124.6 %collective-permute-start.2 = (bf16[2,4,32,2048]{3,2,1,0:T(8,128)(2,1)S(1)}, bf16[2,4,32,2048]{3,2,1,0:T(8,128)(2,1)}, u32[]{:S(2)}, u32[]{:S(2)}) collective-permute-start(bf16[2,4,32,2048]{3,2,1,0:T(8,128)(2,1)S(1)} %get-tuple-element.13), channel_id=1, source_target_pairs={{0,12},{4,16},{8,20},{12,24},{16,28},{20,32},{24,36},{28,40},{32,4... | collective-permute-start | bytes 3145736 | tf_op jit(solution)/shard_map/ppermute | solution.py:12
  22.0 134.5 %collective-permute-start.3 = (bf16[2,4,32,2048]{3,2,1,0:T(8,128)(2,1)S(1)}, bf16[2,4,32,2048]{3,2,1,0:T(8,128)(2,1)S(1)}, u32[]{:S(2)}, u32[]{:S(2)}) collective-permute-start(bf16[2,4,32,2048]{3,2,1,0:T(8,128)(2,1)S(1)} %get-tuple-element.13), channel_id=1, source_target_pairs={{0,16},{4,20},{8,24},{12,28},{16,32},{20,36},{24,40},{28,44},{32,4... | collective-permute-start | bytes 3145736 | tf_op jit(solution)/shard_map/ppermute | solution.py:12
  25.0 184.2 %collective-permute-start.4 = (bf16[2,4,32,2048]{3,2,1,0:T(8,128)(2,1)S(1)}, bf16[2,4,32,2048]{3,2,1,0:T(8,128)(2,1)S(1)}, u32[]{:S(2)}, u32[]{:S(2)}) collective-permute-start(bf16[2,4,32,2048]{3,2,1,0:T(8,128)(2,1)S(1)} %get-tuple-element.13), channel_id=1, source_target_pairs={{0,20},{4,24},{8,28},{12,32},{16,36},{20,40},{24,44},{28,48},{32,5... | collective-permute-start | bytes 3145736 | tf_op jit(solution)/shard_map/ppermute | solution.py:12
  31.7 445.4 %all-gather.5.cloned.1.call-start = ((), (), s32[]{:S(2)}) async-start(), calls=%async_computation.2 | async-start | bytes 5242880 | tf_op jit(solution)/shard_map/all_gather | solution.py:92
  37.4 214.1 %collective-permute-start.5 = (bf16[2,4,32,2048]{3,2,1,0:T(8,128)(2,1)S(1)}, bf16[2,4,32,2048]{3,2,1,0:T(8,128)(2,1)S(1)}, u32[]{:S(2)}, u32[]{:S(2)}) collective-permute-start(bf16[2,4,32,2048]{3,2,1,0:T(8,128)(2,1)S(1)} %get-tuple-element.13), channel_id=1, source_target_pairs={{0,24},{4,28},{8,32},{12,36},{16,40},{20,44},{24,48},{28,52},{32,5... | collective-permute-start | bytes 3145736 | tf_op jit(solution)/shard_map/ppermute | solution.py:12
  78.5 174.2 %collective-permute-start.6 = (bf16[2,4,32,2048]{3,2,1,0:T(8,128)(2,1)S(1)}, bf16[2,4,32,2048]{3,2,1,0:T(8,128)(2,1)S(1)}, u32[]{:S(2)}, u32[]{:S(2)}) collective-permute-start(bf16[2,4,32,2048]{3,2,1,0:T(8,128)(2,1)S(1)} %get-tuple-element.13), channel_id=1, source_target_pairs={{0,28},{4,32},{8,36},{12,40},{16,44},{20,48},{24,52},{28,56},{32,6... | collective-permute-start | bytes 3145736 | tf_op jit(solution)/shard_map/ppermute | solution.py:12
  142.0 111.7 %collective-permute-start.7 = (bf16[2,4,32,2048]{3,2,1,0:T(8,128)(2,1)S(1)}, bf16[2,4,32,2048]{3,2,1,0:T(8,128)(2,1)S(1)}, u32[]{:S(2)}, u32[]{:S(2)}) collective-permute-start(bf16[2,4,32,2048]{3,2,1,0:T(8,128)(2,1)S(1)} %get-tuple-element.13), channel_id=1, source_target_pairs={{0,32},{4,36},{8,40},{12,44},{16,48},{20,52},{24,56},{28,60},{32,6... | collective-permute-start | bytes 3145736 | tf_op jit(solution)/shard_map/ppermute | solution.py:12
  156.6 98.2 %collective-permute-start.8 = (bf16[2,4,32,2048]{3,2,1,0:T(8,128)(2,1)S(1)}, bf16[2,4,32,2048]{3,2,1,0:T(8,128)(2,1)S(1)}, u32[]{:S(2)}, u32[]{:S(2)}) collective-permute-start(bf16[2,4,32,2048]{3,2,1,0:T(8,128)(2,1)S(1)} %get-tuple-element.13), channel_id=1, source_target_pairs={{0,36},{4,40},{8,44},{12,48},{16,52},{20,56},{24,60},{28,64},{32,6... | collective-permute-start | bytes 3145736 | tf_op jit(solution)/shard_map/ppermute | solution.py:12
  209.2 60.3 %collective-permute-start.9 = (bf16[2,4,32,2048]{3,2,1,0:T(8,128)(2,1)S(1)}, bf16[2,4,32,2048]{3,2,1,0:T(8,128)(2,1)S(1)}, u32[]{:S(2)}, u32[]{:S(2)}) collective-permute-start(bf16[2,4,32,2048]{3,2,1,0:T(8,128)(2,1)S(1)} %get-tuple-element.13), channel_id=1, source_target_pairs={{0,40},{4,44},{8,48},{12,52},{16,56},{20,60},{24,64},{28,68},{32,7... | collective-permute-start | bytes 3145736 | tf_op jit(solution)/shard_map/ppermute | solution.py:12
  281.5 7.4 %slice-start = ((s8[5767168]{0:T(1024)(128)(4,1)}), s8[4194304]{0:T(1024)(128)(4,1)S(1)}, s32[]{:S(2)}) async-start(s8[5767168]{0:T(1024)(128)(4,1)} %bitcast.51), calls=%async_computation.3 | async-start | bytes 8388608
  281.5 7.4 %slice-start.1 = ((s8[5767168]{0:T(1024)(128)(4,1)}), s8[1572864]{0:T(1024)(128)(4,1)S(1)}, s32[]{:S(2)}) async-start(s8[5767168]{0:T(1024)(128)(4,1)} %bitcast.51), calls=%async_computation.4 | async-start | bytes 3145728
  289.0 4.7 copy-start
Sparse Core Ops, SparseCore 0:
  31.8 63.8 all-gather.2
  330.0 147.0 all-gather.4
where the time goes:
time: 516 us; the launch traced here: 514 us
  starting transfers between devices  225 us (44%)
  waiting for transfers between devices  163 us (32%)
  local copies, waits for them, and re-layouts  60.3 us (12%)
  matrix products  30.2 us (6%)
  blocking collectives  18.5 us (4%)
  between operations  13.6 us (3%)
    ppermute x10, starting transfers between devices, passed_along(): return lax.ppermute(block, axis, route)  225 us
    all_gather x1, waiting for transfers between devices, on_device(): lax.all_gather(attention, 'space', axis=0, tiled=True)  147 us
    unnamed x26, local copies, waits for them, and re-layouts  36.6 us
    all_to_all x1, blocking collectives, on_device(): lax.all_to_all(columns, 'space', split_axis=0, concat_axis=1, tiled=True)  18.5 us
    ppermute x10, waiting for transfers between devices, passed_along(): return lax.ppermute(block, axis, route)  15.4 us
    slice x1, local copies, waits for them, and re-layouts, on_device(): key_rows = stacked[0].reshape(-1, tok_dev, head_count, HS)  11 us
  transfers between devices with their start and end apart: 12, of which 3 were waited for; matrix products, arithmetic and copies ran while one was open for 11% of the time, Pallas kernels for 0%

commit v1 on v0

v1 whole, which is shorter than its diff:
```python
import jax
import jax.numpy as jnp
import numpy as np
from jax import lax
from jax.experimental import pallas as pl
from jax.experimental.pallas import tpu as pltpu
from jax.sharding import Mesh, PartitionSpec as P

HS = 128
Z, Y, XL, XH, C = 8, 4, 2, 2, 2
PLANE = Y * XL
SWAP = [(0, 1), (1, 0)]
SCALE = HS ** (-0.5)
VMEM = 56 * 1024 * 1024
F32 = jnp.float32
BF16 = jnp.bfloat16
GROUP = 8


def softmax_parts(scores):
    top = jnp.max(scores, axis=-1, keepdims=True)
    raised = jnp.exp(scores - top)
    return raised.astype(BF16), jnp.sum(raised, axis=-1, keepdims=True)


def spatial_kernel(heads, place, own, queries_far, keyvals_far, mate_own, mate_far, out):
    for head in range(heads):
        cols = slice(head * HS, (head + 1) * HS)
        queries = jnp.concatenate([own[0, 0, :, cols], queries_far[0, :, cols]], axis=0)
        key_rows = jnp.concatenate(
            [own[1, 0, :, cols], keyvals_far[0, 0, :, cols], mate_own[0, 0, :, cols], mate_far[0, 0, :, cols]], axis=0
        )
        values = jnp.concatenate(
            [own[2, 0, :, cols], keyvals_far[1, 0, :, cols], mate_own[1, 0, :, cols], mate_far[1, 0, :, cols]], axis=0
        )
        scores = lax.dot_general(queries, key_rows, (((1,), (1,)), ((), ())), preferred_element_type=F32) * SCALE
        raised, total = softmax_parts(scores)
        result = (jnp.dot(raised, values, preferred_element_type=F32) / total).astype(BF16)
        rows = result.shape[0] // 2
        out[0, 0, :, cols] = result[:rows]
        out[1, 0, :, cols] = result[rows:]


def spatial_attend(place, qkv, queries_far, keyvals_far, mate_own, mate_far):
    _, frames, tok, width = keyvals_far.shape
    heads = width // HS

    def body(*refs):
        spatial_kernel(heads, *refs)

    pair = pl.BlockSpec((2, 1, tok, width), lambda f, place: (0, f, 0, 0))
    return pl.pallas_call(
        body,
        grid_spec=pltpu.PrefetchScalarGridSpec(
            num_scalar_prefetch=1,
            grid=(frames,),
            in_specs=[
                pl.BlockSpec((3, 1, tok, width), lambda f, place: (0, f, 0, place[1])),
                pl.BlockSpec((1, tok, width), lambda f, place: (f, 0, 0)),
                pair,
                pair,
                pair,
            ],
            out_specs=pair,
        ),
        out_shape=jax.ShapeDtypeStruct((2, frames, tok, width), BF16),
        compiler_params=pltpu.CompilerParams(vmem_limit_bytes=VMEM),
        name="spatial",
    )(place, qkv, queries_far, keyvals_far, mate_own, mate_far)


def temporal_kernel(clips, place, lengths, queries, own, before, before2, out, bias):
    sources, _, groups, rows, _ = queries.shape
    frames_dev = rows // GROUP
    query_rows = sources * rows
    past_frames = (sources + before2.shape[0]) * frames_dev
    key_count = query_rows + past_frames * GROUP

    @pl.when(pl.program_id(0) == 0)
    def _():
        row = lax.broadcasted_iota(jnp.int32, (query_rows, 1), 0)
        first = place[0] * (sources * frames_dev)
        frame = first + row // GROUP
        start = jnp.zeros_like(frame)
        begin = jnp.int32(0)
        for clip in range(clips):
            start = jnp.where(frame >= begin, begin, start)
            begin = begin + lengths[clip]
        token = (row % GROUP) * 4096
        low = token + start - first + past_frames
        high = token + frame - first + past_frames
        col = lax.broadcasted_iota(jnp.int32, (1, key_count), 1)
        code = (col % GROUP) * 4096 + col // GROUP
        bias[...] = jnp.where((code >= low) & (code <= high), 0.0, -1e30)

    pieces = []
    for group in range(groups):
        def rows_of(ref, which):
            return ref[:, which, 0, group].reshape(-1, HS)

        key_rows = jnp.concatenate([rows_of(before2, 0), rows_of(before, 0), rows_of(own, 0)], axis=0)
        values = jnp.concatenate([rows_of(before2, 1), rows_of(before, 1), rows_of(own, 1)], axis=0)
        scores = lax.dot_general(
            queries[:, 0, group].reshape(-1, HS), key_rows, (((1,), (1,)), ((), ())), preferred_element_type=F32
        )
        raised, total = softmax_parts(scores * SCALE + bias[...])
        result = jnp.dot(raised, values, preferred_element_type=F32) / total
        pieces.append(result.reshape(sources * frames_dev, 1, GROUP, HS))
    joined = jnp.concatenate(pieces, axis=1).reshape(sources, frames_dev * groups * GROUP, HS)
    out[...] = joined.astype(BF16)


def temporal_attend(place, lengths, queries, own, before, before2):
    sources, heads, groups, rows, _ = queries.shape
    clips = lengths.shape[0]
    tok_rows = groups * rows

    def body(*refs):
        temporal_kernel(clips, *refs)

    def keyvals_spec(count):
        return pl.BlockSpec((count, 2, 1, groups, rows, HS), lambda h, place, lengths: (0, 0, h, 0, 0, 0))

    key_count = (2 * sources + before2.shape[0]) * rows
    return pl.pallas_call(
        body,
        grid_spec=pltpu.PrefetchScalarGridSpec(
            num_scalar_prefetch=2,
            grid=(heads,),
            in_specs=[
                pl.BlockSpec((sources, 1, groups, rows, HS), lambda h, place, lengths: (0, h, 0, 0, 0)),
                keyvals_spec(sources),
                keyvals_spec(sources),
                keyvals_spec(before2.shape[0]),
            ],
            out_specs=pl.BlockSpec((sources, tok_rows, HS), lambda h, place, lengths: (0, 0, h)),
            scratch_shapes=[pltpu.VMEM((sources * rows, key_count), F32)],
        ),
        out_shape=jax.ShapeDtypeStruct((sources, tok_rows, heads * HS), BF16),
        compiler_params=pltpu.CompilerParams(vmem_limit_bytes=VMEM),
        name="temporal",
    )(place, lengths, queries, own, before, before2)


def project_spatial(place, near, far, wo, wo_mate):
    _, rows, width = near.shape
    cols = wo.shape[1]
    block = 512
    per = width // block

    def body(place, near, far, wo, wo_mate, out):
        step = pl.program_id(0)

        def add(first, own_rows, far_rows):
            for weights, side in ((wo, 0), (wo_mate, 1)):
                for which, lhs in ((0, own_rows), (1, far_rows)):
                    part = jnp.dot(lhs, weights[...], preferred_element_type=F32)
                    out[which, :, side] = part if first else out[which, :, side] + part

        @pl.when(step == 0)
        def _():
            add(True, near[0], near[1])

        @pl.when((step > 0) & (step < per))
        def _():
            add(False, near[0], near[1])

        @pl.when(step >= per)
        def _():
            add(False, far[1], far[0])

    weights = pl.BlockSpec(
        (block, cols), lambda k, place: (jnp.where(k < per, place[1] * per + k, (1 - place[1]) * per + k - per), 0)
    )
    return pl.pallas_call(
        body,
        grid_spec=pltpu.PrefetchScalarGridSpec(
            num_scalar_prefetch=1,
            grid=(2 * per,),
            in_specs=[
                pl.BlockSpec((2, rows, block), lambda k, place: (0, 0, jnp.minimum(k, per - 1))),
                pl.BlockSpec((2, rows, block), lambda k, place: (0, 0, jnp.maximum(k - per, 0))),
                weights,
                weights,
            ],
            out_specs=pl.BlockSpec((2, rows, 2, cols), lambda k, place: (0, 0, 0, 0)),
        ),
        out_shape=jax.ShapeDtypeStruct((2, rows, 2, cols), F32),
        compiler_params=pltpu.CompilerParams(vmem_limit_bytes=VMEM),
        name="project_spatial",
    )(place, near, far, wo, wo_mate)


def project_temporal(place, which, partial, returned, wo, wo_mate):
    _, rows, _, cols = partial.shape
    sources, _, _, width = returned.shape
    per = 2
    block = per * width
    steps = sources // per
    skip = wo.shape[0] // block - steps

    def body(place, partial, returned, wo, wo_mate, out, total):
        step = pl.program_id(0)
        lhs = jnp.concatenate([returned[i, 0] for i in range(per)], axis=1)

        @pl.when(step == 0)
        def _():
            total[...] = partial[0]

        for weights, side in ((wo, 0), (wo_mate, 1)):
            total[:, side] = total[:, side] + jnp.dot(lhs, weights[...], preferred_element_type=F32)

        @pl.when(step == steps - 1)
        def _():
            out[...] = total[...].astype(BF16)

    weights = pl.BlockSpec((block, cols), lambda k, place: (skip + k, 0))
    return pl.pallas_call(
        body,
        grid_spec=pltpu.PrefetchScalarGridSpec(
            num_scalar_prefetch=1,
            grid=(steps,),
            in_specs=[
                pl.BlockSpec((1, rows, 2, cols), lambda k, place: (which, 0, 0, 0)),
                pl.BlockSpec(
                    (per, 1, rows, width),
                    lambda k, place: (k, (1 - place[1]) if which else place[1], 0, 0),
                ),
                weights,
                weights,
            ],
            out_specs=pl.BlockSpec((rows, 2, cols), lambda k, place: (0, 0, 0)),
            scratch_shapes=[pltpu.VMEM((rows, 2, cols), F32)],
        ),
        out_shape=jax.ShapeDtypeStruct((rows, 2, cols), BF16),
        compiler_params=pltpu.CompilerParams(vmem_limit_bytes=VMEM),
        name="project_far" if which else "project_own",
    )(place, partial, returned, wo, wo_mate)


def on_device(qkv, clip_lengths, wo):
    _, frames, tok, model_width = qkv.shape
    half = model_width // 2
    quarter = half // 2
    z_place = lax.axis_index("z")
    x_place = lax.axis_index("xh")
    c_place = lax.axis_index("c")
    place = jnp.stack([z_place, x_place]).astype(jnp.int32)

    heads = half // HS // PLANE
    groups = tok // GROUP
    rows = frames * GROUP

    def by_plane(block):
        count = block.shape[0]
        split = block.reshape(count, frames, groups, GROUP, PLANE, heads, HS)
        return split.transpose(4, 0, 5, 2, 1, 3, 6).reshape(PLANE, count, heads, groups, rows, HS)

    keyvals = lax.all_to_all(by_plane(qkv[1:, :, :, half:]), ("y", "xl"), 0, 0, tiled=True)
    queries = lax.all_to_all(by_plane(qkv[:1, :, :, half:]), ("y", "xl"), 0, 0, tiled=True)[:, 0]
    before = lax.ppermute(keyvals, "z", [(i, (i + 1) % Z) for i in range(Z)])
    before2 = lax.ppermute(keyvals[PLANE - 2 :], "z", [(i, (i + 2) % Z) for i in range(Z)])

    own_cols = x_place * quarter
    far_cols = (1 - x_place) * quarter
    keyvals_far = lax.ppermute(
        lax.dynamic_slice(qkv, (1, 0, 0, far_cols), (2, frames, tok, quarter)), "xh", SWAP
    )
    queries_far = lax.ppermute(
        lax.dynamic_slice(qkv, (0, 0, 0, far_cols), (1, frames, tok, quarter)), "xh", SWAP
    )[0]
    mate_own = lax.ppermute(
        lax.dynamic_slice(qkv, (1, 0, 0, own_cols), (2, frames, tok, quarter)), "c", SWAP
    )
    mate_far = lax.ppermute(keyvals_far, "c", SWAP)
    wo_mate = lax.ppermute(wo, "c", SWAP)

    near = spatial_attend(place, qkv, queries_far, keyvals_far, mate_own, mate_far)
    near = near.reshape(2, frames * tok, quarter)
    far = lax.ppermute(near, "xh", SWAP)
    partial = project_spatial(place, near, far, wo, wo_mate)

    temporal = temporal_attend(place, clip_lengths, queries, keyvals, before, before2)
    sent = jnp.broadcast_to(temporal[:, None], (PLANE, XH) + temporal.shape[1:])
    sent = sent.reshape((PLANE * XH,) + temporal.shape[1:])
    returned = lax.all_to_all(sent, ("y", "xl", "xh"), 0, 0, tiled=True)
    returned = returned.reshape((PLANE, XH) + temporal.shape[1:])

    cols = wo.shape[1]
    for_partner = project_temporal(place, 1, partial, returned, wo, wo_mate)
    arrived = lax.ppermute(for_partner, "xh", SWAP)
    own = project_temporal(place, 0, partial, returned, wo, wo_mate)
    mixed = jnp.zeros((frames * tok, model_width), BF16)
    for block, place_x in ((own, x_place), (arrived, 1 - x_place)):
        mixed = lax.dynamic_update_slice(mixed, block[:, 0], (0, (place_x * C + c_place) * cols))
        mixed = lax.dynamic_update_slice(mixed, block[:, 1], (0, (place_x * C + 1 - c_place) * cols))
    return mixed.reshape(frames, tok, model_width)


def solution(mesh):
    fine = Mesh(mesh.devices.reshape(Z, Y, XL, XH, C), ("z", "y", "xl", "xh", "c"))
    return jax.shard_map(
        on_device,
        mesh=fine,
        in_specs=(P(None, ("z", "y", "xl"), ("xh", "c"), None), P(), P(None, ("xh", "c"))),
        out_specs=P(("z", "y", "xl"), ("xh", "c"), None),
        check_vma=False,
    )
```

time: 516 us -> 156 us (0.30)
  the two profiles are of different devices: /device:TPU:2 before, /device:TPU:42 now
where the time goes in v1:
time: 156 us; the launch traced here: 155 us
  waiting for transfers between devices  54.7 us (35%)
  Pallas kernels  41.7 us (27%)
  starting transfers between devices  24.1 us (15%)
  blocking collectives  20.1 us (13%)
  local copies, waits for them, and re-layouts  14.1 us (9%)
    all_to_all x1, blocking collectives, on_device(): lax.all_to_all(by_plane(qkv[1:, :, :, half:]), ('y', 'xl'), 0, 0, tiled=T...  20.1 us
    ppermute x1, waiting for transfers between devices, on_device(): lax.ppermute(lax.dynamic_slice(qkv, (0, 0, 0, far_cols), (1, frames, tok,...  17.8 us
    ppermute x1, waiting for transfers between devices, on_device(): lax.ppermute(keyvals[PLANE - 2:], 'z', [(i, (i + 2) % Z) for i in range(Z)])  16.2 us
    pallas_call x2, Pallas kernels, project_temporal(): pl.pallas_call(body, grid_spec=pltpu.PrefetchScalarGridSpec(num_scalar_pr...  15.4 us
    ppermute x1, waiting for transfers between devices, on_device(): far = lax.ppermute(near, 'xh', SWAP)  13.8 us
    pallas_call x1, Pallas kernels, spatial_attend(): pl.pallas_call(body, grid_spec=pltpu.PrefetchScalarGridSpec(num_scalar_pr...  10.7 us
    pallas_call x1, Pallas kernels, project_spatial(): pl.pallas_call(body, grid_spec=pltpu.PrefetchScalarGridSpec(num_scalar_pr...  9.11 us
    all_to_all x1, starting transfers between devices, on_device(): lax.all_to_all(by_plane(qkv[:1, :, :, half:]), ('y', 'xl'), 0, 0, tiled=T...  6.72 us
  transfers between devices with their start and end apart: 11, of which 6 were waited for; matrix products, arithmetic and copies ran while one was open for 7% of the time, Pallas kernels for 22%

profile of v1, /device:TPU:42, one launch (start us, length us, event | category | flops | bytes accessed | tf_op | source)
XLA Modules:
  0.0 155.5 jit_solution(16112056515714508346)
XLA Ops:
  0.0 0.0 copy-start
  0.0 0.0 collective-permute-start.5
  0.0 1.4 slice.22
  1.5 0.3 copy.20
  1.7 20.1 %all_to_all.15.refs_3_ = bf16[8,2,2,4,32,128]{5,4,3,2,1,0:T(8,128)(2,1)} all-to-all(bf16[8,2,2,4,32,128]{5,4,3,2,1,0:T(8,128)(2,1)S(1)} %bitcast.29), channel_id=1, replica_groups=mesh['z'=8,'y'=4,'xl'=2,'xh'=2,'c'=2] {'y','xl'}, dimensions={0} | all-to-all | bytes 2097152 | tf_op jit(solution)/shard_map/all_to_all | solution.py:259
  21.9 1.9 %collective-permute-start.6 = (bf16[8,2,2,4,32,128]{5,4,3,2,1,0:T(8,128)(2,1)}, bf16[8,2,2,4,32,128]{5,4,3,2,1,0:T(8,128)(2,1)}, u32[]{:S(2)}, u32[]{:S(2)}) collective-permute-start(bf16[8,2,2,4,32,128]{5,4,3,2,1,0:T(8,128)(2,1)} %all_to_all.15.refs_3_), channel_id=1, source_target_pairs={{0,32},{32,64},{64,96},{96,128},{128,160},{160,192},{192,224},{224... | collective-permute-start | bytes 3145736 | tf_op jit(solution)/shard_map/ppermute | solution.py:261
  23.8 0.0 copy-done
  23.8 1.1 constant_dynamic-slice_fusion
  24.9 2.1 %collective-permute-start.1 = (bf16[2,4,32,1024]{3,2,1,0:T(8,128)(2,1)}, bf16[2,4,32,1024]{3,2,1,0:T(8,128)(2,1)}, u32[]{:S(2)}, u32[]{:S(2)}) collective-permute-start(bf16[2,4,32,1024]{3,2,1,0:T(8,128)(2,1)} %get-tuple-element.6), channel_id=1, source_target_pairs={{0,2},{2,0},{1,3},{3,1},{4,6},{6,4},{5,7},{7,5},{8,10},{10,8},{9,1... | collective-permute-start | bytes 1572872 | tf_op jit(solution)/shard_map/ppermute | solution.py:266
  27.0 0.9 copy.21
  28.0 6.7 %all-to-all-start = ((bf16[8,1,2,4,32,128]{5,4,3,2,1,0:T(8,128)(2,1)}), bf16[8,1,2,4,32,128]{5,4,3,2,1,0:T(8,128)(2,1)}, u32[]{:S(2)}, u32[]{:S(2)}) async-start(bf16[8,1,2,4,32,128]{5,4,3,2,1,0:T(8,128)(2,1)} %bitcast.31), calls=%async_computation | async-start | bytes 1048576 | tf_op jit(solution)/shard_map/all_to_all | solution.py:260
  34.7 1.7 %slice.28 = bf16[2,2,2,4,32,128]{5,4,3,2,1,0:T(8,128)(2,1)} slice(bf16[8,2,2,4,32,128]{5,4,3,2,1,0:T(8,128)(2,1)} %all_to_all.15.refs_3_), slice={[6:8], [0:2], [0:2], [0:4], [0:32], [0:128]} | slice | bytes 524288 | tf_op jit(solution)/shard_map/slice | solution.py:262
  36.3 4.5 %collective-permute-start.7 = (bf16[2,2,2,4,32,128]{5,4,3,2,1,0:T(8,128)(2,1)}, bf16[2,2,2,4,32,128]{5,4,3,2,1,0:T(8,128)(2,1)S(1)}, u32[]{:S(2)}, u32[]{:S(2)}) collective-permute-start(bf16[2,2,2,4,32,128]{5,4,3,2,1,0:T(8,128)(2,1)} %slice.28), channel_id=1, source_target_pairs={{0,64},{32,96},{64,128},{96,160},{128,192},{160,224},{192,0},{224,... | collective-permute-start | bytes 786440 | tf_op jit(solution)/shard_map/ppermute | solution.py:262
  40.8 0.0 collective-permute-start.2
  40.8 0.7 collective-permute-done.1.refs_3_
  41.5 0.0 collective-permute-start.3
  41.5 0.6 pad_add_fusion.refs_0_.place
  42.2 3.5 %all-to-all-done = bf16[8,1,2,4,32,128]{5,4,3,2,1,0:T(8,128)(2,1)} async-done(((bf16[8,1,2,4,32,128]{5,4,3,2,1,0:T(8,128)(2,1)}), bf16[8,1,2,4,32,128]{5,4,3,2,1,0:T(8,128)(2,1)}, u32[]{:S(2)}, u32[]{:S(2)}) %all-to-all-start) | async-done | bytes 524320 | tf_op jit(solution)/shard_map/all_to_all | solution.py:260
  45.6 16.2 %collective-permute-done.7.refs_5_ = bf16[2,2,2,4,32,128]{5,4,3,2,1,0:T(8,128)(2,1)S(1)} collective-permute-done((bf16[2,2,2,4,32,128]{5,4,3,2,1,0:T(8,128)(2,1)}, bf16[2,2,2,4,32,128]{5,4,3,2,1,0:T(8,128)(2,1)S(1)}, u32[]{:S(2)}, u32[]{:S(2)}) %collective-permute-start.7) | collective-permute-done | bytes 262176 | tf_op jit(solution)/shard_map/ppermute | solution.py:262
  61.9 0.0 copy-start.3
  61.9 0.0 collective-permute-done.6.refs_4_
  61.9 0.7 copy-done.3
  62.6 6.6 %temporal.1 = bf16[8,128,256]{2,1,0:T(8,128)(2,1)} custom-call(s32[2]{0:T(128)} %pad_add_fusion.refs_0_.place, s32[16]{0:T(128)} %refs_1_.3, bf16[8,2,4,32,128]{4,3,2,1,0:T(8,128)(2,1)} %bitcast.7.refs_2_, bf16[8,2,2,4,32,128]{5,4,3,2,1,0:T(8,128)(2,1)} %all_to_all.15.refs_3_, bf16[8,2,2,4,32,128]{5,4,3,2,1,0:T(8,128)(2,1)} %collective-permute-done.6.refs_4_, ...), custom_call_target="tpu_custom_call" | custom-call | tf_op jit(solution)/shard_map/temporal/pallas_call | solution.py:125
  69.2 2.1 %broadcast_in_dim.10 = bf16[8,2,128,256]{3,2,1,0:T(8,128)(2,1)} broadcast(bf16[8,128,256]{2,1,0:T(8,128)(2,1)} %temporal.1), dimensions={0,2,3} | broadcast | bytes 1572864 | tf_op jit(solution)/shard_map/broadcast_in_dim | solution.py:284
  71.3 6.1 %all-to-all-start.2 = ((bf16[16,128,256]{2,1,0:T(8,128)(2,1)}), bf16[16,128,256]{2,1,0:T(8,128)(2,1)}, u32[]{:S(2)}, u32[]{:S(2)}) async-start(bf16[16,128,256]{2,1,0:T(8,128)(2,1)} %bitcast.28), calls=%async_computation.2 | async-start | bytes 2097152 | tf_op jit(solution)/shard_map/all_to_all | solution.py:286
  77.4 2.2 %collective-permute-start = (bf16[1,4,32,1024]{3,2,1,0:T(8,128)(2,1)S(1)}, bf16[1,4,32,1024]{3,2,1,0:T(8,128)(2,1)S(1)}, u32[]{:S(2)}, u32[]{:S(2)}) collective-permute-start(bf16[1,4,32,1024]{3,2,1,0:T(8,128)(2,1)S(1)} %constant_dynamic-slice_fusion.2), channel_id=1, source_target_pairs={{0,2},{2,0},{1,3},{3,1},{4,6},{6,4},{5,7},{7,5},{8,10},{10,8},{9,1... | collective-permute-start | bytes 786440 | tf_op jit(solution)/shard_map/ppermute | solution.py:269
  79.5 17.8 %collective-permute-done = bf16[1,4,32,1024]{3,2,1,0:T(8,128)(2,1)S(1)} collective-permute-done((bf16[1,4,32,1024]{3,2,1,0:T(8,128)(2,1)S(1)}, bf16[1,4,32,1024]{3,2,1,0:T(8,128)(2,1)S(1)}, u32[]{:S(2)}, u32[]{:S(2)}) %collective-permute-start) | collective-permute-done | bytes 262176 | tf_op jit(solution)/shard_map/ppermute | solution.py:269
  97.3 0.0 copy-start.4
  97.3 0.0 collective-permute-done.2.refs_4_
  97.3 0.0 collective-permute-done.3.refs_5_
  97.3 0.7 copy-done.4
  98.0 10.7 %spatial.1 = bf16[2,4,32,1024]{3,2,1,0:T(8,128)(2,1)} custom-call(s32[2]{0:T(128)} %pad_add_fusion.refs_0_.place, bf16[3,4,32,4096]{3,2,1,0:T(8,128)(2,1)} %refs_1_.2, bf16[4,32,1024]{2,1,0:T(8,128)(2,1)} %bitcast.35, bf16[2,4,32,1024]{3,2,1,0:T(8,128)(2,1)} %collective-permute-done.1.refs_3_, bf16[2,4,32,1024]{3,2,1,0:T(8,128)(2,1)} %collective-permute-done.2.refs_4_, ...), custom_call_target="tpu_custom_call" | custom-call | tf_op jit(solution)/shard_map/spatial/pallas_call | solution.py:52
  108.7 0.3 collective-permute-start.4
  109.0 13.8 %collective-permute-done.4.far = bf16[2,128,1024]{2,1,0:T(8,128)(2,1)S(1)} collective-permute-done((bf16[2,128,1024]{2,1,0:T(8,128)(2,1)}, bf16[2,128,1024]{2,1,0:T(8,128)(2,1)S(1)}, u32[]{:S(2)}, u32[]{:S(2)}) %collective-permute-start.4) | collective-permute-done | bytes 524320 | tf_op jit(solution)/shard_map/ppermute | solution.py:280
  122.8 0.0 copy-start.2
  122.8 0.0 collective-permute-done.5.wo_mate
  122.8 0.8 copy-done.2
  123.6 9.1 %project_spatial.1.partial = f32[2,128,2,1024]{3,2,1,0:T(2,128)} custom-call(s32[2]{0:T(128)} %pad_add_fusion.refs_0_.place, bf16[2,128,1024]{2,1,0:T(8,128)(2,1)} %bitcast.34, bf16[2,128,1024]{2,1,0:T(8,128)(2,1)} %copy-done.2, bf16[4096,1024]{1,0:T(8,128)(2,1)} %wo.5, bf16[4096,1024]{1,0:T(8,128)(2,1)} %collective-permute-done.5.wo_mate), custom_call_target="tpu_custom_call" | custom-call | tf_op jit(solution)/shard_map/project_spatial/pallas_call | solution.py:175
  132.7 0.0 all-to-all-done.2
  132.7 7.7 %project_far.1 = bf16[128,2,1024]{2,1,0:T(2,128)(2,1)} custom-call(s32[2]{0:T(128)} %pad_add_fusion.refs_0_.place, f32[2,128,2,1024]{3,2,1,0:T(2,128)} %project_spatial.1.partial, bf16[8,2,128,256]{3,2,1,0:T(8,128)(2,1)} %bitcast.12.returned, bf16[4096,1024]{1,0:T(8,128)(2,1)} %wo.5, bf16[4096,1024]{1,0:T(8,128)(2,1)} %collective-permute-done.5.wo_mate), custom_call_target="tpu_custom_call" | custom-call | tf_op jit(solution)/shard_map/project_far/pallas_call | solution.py:218
  140.4 0.3 collective-permute-start.8
  140.7 7.7 %project_own.1 = bf16[128,2,1024]{2,1,0:T(2,128)(2,1)} custom-call(s32[2]{0:T(128)} %pad_add_fusion.refs_0_.place, f32[2,128,2,1024]{3,2,1,0:T(2,128)} %project_spatial.1.partial, bf16[8,2,128,256]{3,2,1,0:T(8,128)(2,1)} %bitcast.12.returned, bf16[4096,1024]{1,0:T(8,128)(2,1)} %wo.5, bf16[4096,1024]{1,0:T(8,128)(2,1)} %collective-permute-done.5.wo_mate), custom_call_target="tpu_custom_call" | custom-call | tf_op jit(solution)/shard_map/project_own/pallas_call | solution.py:218
  148.4 2.1 %fusion.1 = (bf16[128,1,1024]{2,1,0:T(2,128)(2,1)S(1)}, bf16[128,1,1024]{2,1,0:T(2,128)(2,1)S(1)}) fusion(bf16[128,2,1024]{2,1,0:T(2,128)(2,1)} %project_own.1), kind=kLoop, calls=%fused_computation.11 | loop fusion | bytes 1048576 | tf_op jit(solution)/shard_map/slice | solution.py:296
  150.5 0.1 broadcast_in_dim.4
  150.6 0.1 bitcast_dynamic-update-slice_fusion.3
  150.7 0.1 bitcast_dynamic-update-slice_fusion.2
  150.8 2.7 %collective-permute-done.8 = bf16[128,2,1024]{2,1,0:T(2,128)(2,1)S(1)} collective-permute-done((bf16[128,2,1024]{2,1,0:T(2,128)(2,1)}, bf16[128,2,1024]{2,1,0:T(2,128)(2,1)S(1)}, u32[]{:S(2)}, u32[]{:S(2)}) %collective-permute-start.8) | collective-permute-done | bytes 524320 | tf_op jit(solution)/shard_map/ppermute | solution.py:291
  153.6 0.7 fusion
  154.3 0.1 bitcast_dynamic-update-slice_fusion.1
  154.4 0.1 bitcast_dynamic-update-slice_fusion
  154.5 0.0 copy-start.1
  154.5 1.0 copy-done.1
  (2 shorter events, 0.1 us)
Async XLA Ops:
  0.0 23.8 %copy-start = (bf16[3,4,32,4096]{3,2,1,0:T(8,128)(2,1)S(1)}, bf16[3,4,32,4096]{3,2,1,0:T(8,128)(2,1)}, u32[]{:S(2)}) copy-start(bf16[3,4,32,4096]{3,2,1,0:T(8,128)(2,1)} %refs_1_.2) | copy-start | bytes 9437188
  0.0 122.8 %collective-permute-start.5 = (bf16[4096,1024]{1,0:T(8,128)(2,1)}, bf16[4096,1024]{1,0:T(8,128)(2,1)}, u32[]{:S(2)}, u32[]{:S(2)}) collective-permute-start(bf16[4096,1024]{1,0:T(8,128)(2,1)} %wo.5), channel_id=1, source_target_pairs={{0,1},{1,0},{2,3},{3,2},{4,5},{5,4},{6,7},{7,6},{8,9},{9,8},{10,11... | collective-permute-start | bytes 25165832 | tf_op jit(solution)/shard_map/ppermute | solution.py:276
  21.9 40.0 %collective-permute-start.6 = (bf16[8,2,2,4,32,128]{5,4,3,2,1,0:T(8,128)(2,1)}, bf16[8,2,2,4,32,128]{5,4,3,2,1,0:T(8,128)(2,1)}, u32[]{:S(2)}, u32[]{:S(2)}) collective-permute-start(bf16[8,2,2,4,32,128]{5,4,3,2,1,0:T(8,128)(2,1)} %all_to_all.15.refs_3_), channel_id=1, source_target_pairs={{0,32},{32,64},{64,96},{96,128},{128,160},{160,192},{192,224},{224... | collective-permute-start | bytes 3145736 | tf_op jit(solution)/shard_map/ppermute | solution.py:261
  24.9 16.7 %collective-permute-start.1 = (bf16[2,4,32,1024]{3,2,1,0:T(8,128)(2,1)}, bf16[2,4,32,1024]{3,2,1,0:T(8,128)(2,1)}, u32[]{:S(2)}, u32[]{:S(2)}) collective-permute-start(bf16[2,4,32,1024]{3,2,1,0:T(8,128)(2,1)} %get-tuple-element.6), channel_id=1, source_target_pairs={{0,2},{2,0},{1,3},{3,1},{4,6},{6,4},{5,7},{7,5},{8,10},{10,8},{9,1... | collective-permute-start | bytes 1572872 | tf_op jit(solution)/shard_map/ppermute | solution.py:266
  28.0 17.7 %all-to-all-start = ((bf16[8,1,2,4,32,128]{5,4,3,2,1,0:T(8,128)(2,1)}), bf16[8,1,2,4,32,128]{5,4,3,2,1,0:T(8,128)(2,1)}, u32[]{:S(2)}, u32[]{:S(2)}) async-start(bf16[8,1,2,4,32,128]{5,4,3,2,1,0:T(8,128)(2,1)} %bitcast.31), calls=%async_computation | async-start | bytes 1048576 | tf_op jit(solution)/shard_map/all_to_all | solution.py:260
  36.3 25.5 %collective-permute-start.7 = (bf16[2,2,2,4,32,128]{5,4,3,2,1,0:T(8,128)(2,1)}, bf16[2,2,2,4,32,128]{5,4,3,2,1,0:T(8,128)(2,1)S(1)}, u32[]{:S(2)}, u32[]{:S(2)}) collective-permute-start(bf16[2,2,2,4,32,128]{5,4,3,2,1,0:T(8,128)(2,1)} %slice.28), channel_id=1, source_target_pairs={{0,64},{32,96},{64,128},{96,160},{128,192},{160,224},{192,0},{224,... | collective-permute-start | bytes 786440 | tf_op jit(solution)/shard_map/ppermute | solution.py:262
  40.8 56.5 %collective-permute-start.2 = (bf16[2,4,32,1024]{3,2,1,0:T(8,128)(2,1)}, bf16[2,4,32,1024]{3,2,1,0:T(8,128)(2,1)}, u32[]{:S(2)}, u32[]{:S(2)}) collective-permute-start(bf16[2,4,32,1024]{3,2,1,0:T(8,128)(2,1)} %get-tuple-element.5), channel_id=1, source_target_pairs={{0,1},{1,0},{2,3},{3,2},{4,5},{5,4},{6,7},{7,6},{8,9},{9,8},{10,11... | collective-permute-start | bytes 1572872 | tf_op jit(solution)/shard_map/ppermute | solution.py:272
  41.5 55.8 %collective-permute-start.3 = (bf16[2,4,32,1024]{3,2,1,0:T(8,128)(2,1)}, bf16[2,4,32,1024]{3,2,1,0:T(8,128)(2,1)}, u32[]{:S(2)}, u32[]{:S(2)}) collective-permute-start(bf16[2,4,32,1024]{3,2,1,0:T(8,128)(2,1)} %collective-permute-done.1.refs_3_), channel_id=1, source_target_pairs={{0,1},{1,0},{2,3},{3,2},{4,5},{5,4},{6,7},{7,6},{8,9},{9,8},{10,11... | collective-permute-start | bytes 1572872 | tf_op jit(solution)/shard_map/ppermute | solution.py:275
  61.9 0.7 copy-start.3
  71.3 61.4 %all-to-all-start.2 = ((bf16[16,128,256]{2,1,0:T(8,128)(2,1)}), bf16[16,128,256]{2,1,0:T(8,128)(2,1)}, u32[]{:S(2)}, u32[]{:S(2)}) async-start(bf16[16,128,256]{2,1,0:T(8,128)(2,1)} %bitcast.28), calls=%async_computation.2 | async-start | bytes 2097152 | tf_op jit(solution)/shard_map/all_to_all | solution.py:286
  77.4 19.9 %collective-permute-start = (bf16[1,4,32,1024]{3,2,1,0:T(8,128)(2,1)S(1)}, bf16[1,4,32,1024]{3,2,1,0:T(8,128)(2,1)S(1)}, u32[]{:S(2)}, u32[]{:S(2)}) collective-permute-start(bf16[1,4,32,1024]{3,2,1,0:T(8,128)(2,1)S(1)} %constant_dynamic-slice_fusion.2), channel_id=1, source_target_pairs={{0,2},{2,0},{1,3},{3,1},{4,6},{6,4},{5,7},{7,5},{8,10},{10,8},{9,1... | collective-permute-start | bytes 786440 | tf_op jit(solution)/shard_map/ppermute | solution.py:269
  97.3 0.7 copy-start.4
  108.7 14.1 %collective-permute-start.4 = (bf16[2,128,1024]{2,1,0:T(8,128)(2,1)}, bf16[2,128,1024]{2,1,0:T(8,128)(2,1)S(1)}, u32[]{:S(2)}, u32[]{:S(2)}) collective-permute-start(bf16[2,128,1024]{2,1,0:T(8,128)(2,1)} %bitcast.33), channel_id=1, source_target_pairs={{0,2},{2,0},{1,3},{3,1},{4,6},{6,4},{5,7},{7,5},{8,10},{10,8},{9,1... | collective-permute-start | bytes 1572872 | tf_op jit(solution)/shard_map/ppermute | solution.py:280
  122.8 0.8 copy-start.2
  140.4 13.2 %collective-permute-start.8 = (bf16[128,2,1024]{2,1,0:T(2,128)(2,1)}, bf16[128,2,1024]{2,1,0:T(2,128)(2,1)S(1)}, u32[]{:S(2)}, u32[]{:S(2)}) collective-permute-start(bf16[128,2,1024]{2,1,0:T(2,128)(2,1)} %project_far.1), channel_id=1, source_target_pairs={{0,2},{2,0},{1,3},{3,1},{4,6},{6,4},{5,7},{7,5},{8,10},{10,8},{9,1... | collective-permute-start | bytes 1572872 | tf_op jit(solution)/shard_map/ppermute | solution.py:291
  154.5 1.0 copy-start.1

commit v2 on v0

v2 whole, which is shorter than its diff:
```python
import jax
import jax.numpy as jnp
import numpy as np
from jax import lax
from jax.experimental import pallas as pl
from jax.experimental.pallas import tpu as pltpu
from jax.sharding import Mesh, PartitionSpec as P

HS = 128
Z, Y, XL, XH, C = 8, 4, 2, 2, 2
PLANE = Y * XL
EXP2_SCALE = HS ** (-0.5) * float(np.log2(np.e))
F32 = jnp.float32
BF16 = jnp.bfloat16
GROUP = 8
ROUNDS = 2

SWAP = [(0, 1), (1, 0)]

SMEM = pl.BlockSpec(memory_space=pltpu.SMEM)
WHOLE = pl.BlockSpec(memory_space=pltpu.VMEM)
ANYWHERE = pl.BlockSpec(memory_space=pl.ANY)
IN_HBM = pl.BlockSpec(memory_space=pltpu.HBM)
WIDE = 60
QUICK = pl.CostEstimate(flops=1024, bytes_accessed=1024, transcendentals=0)


def kernel_params(mebibytes):
    return pltpu.CompilerParams(vmem_limit_bytes=mebibytes * 1024 * 1024)


def softmax_parts(scores):
    top = jnp.max(scores, axis=-1, keepdims=True)
    return jnp.exp2((scores - top) * EXP2_SCALE).astype(BF16)


def weighted(raised, values):
    both = jnp.concatenate([values, jnp.ones_like(values)], axis=1)
    result = jnp.dot(raised, both, preferred_element_type=F32)
    return result[:, :HS] / result[:, HS:]


def spatial_attend(own, far, mate_own, mate_far, after):
    _, frames, tok, width = own.shape

    def body(own, far, mate_own, mate_far, after, out):
        blocks = [(f, slice(head * HS, (head + 1) * HS)) for f in range(frames) for head in range(width // HS)]

        def keyvals_of(which, f, cols):
            return jnp.concatenate([ref[which, f, :, cols] for ref in (own, far, mate_own, mate_far)], axis=0)

        for first in range(0, len(blocks), 8):
            batch = blocks[first : first + 8]
            scores = []
            for f, cols in batch:
                queries = jnp.concatenate([own[0, f, :, cols], far[0, f, :, cols]], axis=0)
                scores.append(
                    lax.dot_general(
                        queries, keyvals_of(1, f, cols), (((1,), (1,)), ((), ())), preferred_element_type=F32
                    )
                )
            raised = [softmax_parts(block) for block in scores]
            results = [weighted(block, keyvals_of(2, f, cols)).astype(BF16) for block, (f, cols) in zip(raised, batch)]
            for result, (f, cols) in zip(results, batch):
                out[0, f, :, cols] = result[:tok]
                out[1, f, :, cols] = result[tok:]

    return pl.pallas_call(
        body,
        in_specs=[WHOLE] * 4 + [ANYWHERE],
        out_specs=WHOLE,
        out_shape=jax.ShapeDtypeStruct((2, frames, tok, width), BF16),
        compiler_params=kernel_params(16),
        cost_estimate=QUICK,
        name="spatial",
    )(own, far, mate_own, mate_far, after)


def temporal_kernel(clips, turn, place, lengths, queries, own, before, before2, after, out, bias):
    sources, _, groups, rows, _ = queries.shape
    frames_dev = rows // GROUP
    query_rows = sources * rows
    past_frames = (sources + before2.shape[1]) * frames_dev
    key_count = query_rows + past_frames * GROUP

    row = lax.broadcasted_iota(jnp.int32, (query_rows, 1), 0)
    first = place[0] * (sources * frames_dev)
    frame = first + row // GROUP
    start = jnp.zeros_like(frame)
    begin = jnp.int32(0)
    for clip in range(clips):
        start = jnp.where(frame >= begin, begin, start)
        begin = begin + lengths[clip]
    token = (row % GROUP) * 4096
    low = token + start - first + past_frames
    high = token + frame - first + past_frames
    col = lax.broadcasted_iota(jnp.int32, (1, key_count), 1)
    code = (col % GROUP) * 4096 + col // GROUP
    bias[...] = jnp.where((code >= low) & (code <= high), 0.0, -1e30)

    pieces = []
    for group in range(groups):
        def rows_of(ref, which):
            return ref[:, which, group].reshape(-1, HS)

        key_rows = jnp.concatenate([rows_of(before2.at[turn], 0), rows_of(before, 0), rows_of(own, 0)], axis=0)
        values = jnp.concatenate([rows_of(before2.at[turn], 1), rows_of(before, 1), rows_of(own, 1)], axis=0)
        scores = lax.dot_general(
            queries[:, turn, group].reshape(-1, HS), key_rows, (((1,), (1,)), ((), ())), preferred_element_type=F32
        )
        result = weighted(softmax_parts(scores + bias[...]), values)
        pieces.append(result.reshape(sources * frames_dev, 1, GROUP, HS))
    joined = jnp.concatenate(pieces, axis=1).reshape(sources, frames_dev * groups * GROUP, HS).astype(BF16)
    for copy in range(XH):
        out[:, copy] = joined


def temporal_attend(turn, place, lengths, queries, own, before, before2, after):
    sources, _, groups, rows, _ = queries.shape
    clips = lengths.shape[0]

    def body(*refs):
        temporal_kernel(clips, turn, *refs)

    key_count = (2 * sources + before2.shape[1]) * rows
    return pl.pallas_call(
        body,
        in_specs=[SMEM, SMEM, WHOLE, WHOLE, WHOLE, WHOLE, ANYWHERE],
        out_specs=WHOLE,
        out_shape=jax.ShapeDtypeStruct((sources, XH, groups * rows, HS), BF16),
        scratch_shapes=[pltpu.VMEM((sources * rows, key_count), F32)],
        compiler_params=kernel_params(16),
        cost_estimate=QUICK,
        name="temporal",
    )(place, lengths, queries, own, before, before2, after)


def returned_rows(returned, x_half):
    return jnp.concatenate([returned[source, x_half] for source in range(PLANE)], axis=1)


def project_first(place, near, far, returned, wo, wo_mate):
    rows, width = near.shape[1:]
    features, cols = wo.shape
    half = features // 2
    parts = features // width - 1

    def body(place, near, far, returned, wo, wo_mate, out, weights, arrivals):
        x_place = place[1]
        sides = (wo, wo_mate)

        def fetch(part, side):
            if part == 0:
                start = pl.multiple_of(x_place * width, width)
            elif part == 1:
                start = pl.multiple_of((1 - x_place) * width, width)
            else:
                start = half + (part - 2) * width
            return pltpu.make_async_copy(
                sides[side].at[pl.ds(start, width)], weights.at[side, part], arrivals.at[side, part]
            )

        for part in range(parts):
            for side in range(2):
                fetch(part, side).start()
        lhs = [
            jnp.concatenate([near[0], near[1]], axis=0),
            jnp.concatenate([far[1], far[0]], axis=0),
            jnp.concatenate([returned_rows(returned, x_place), returned_rows(returned, 1 - x_place)], axis=0),
        ]
        for part in range(parts):
            for side in range(2):
                fetch(part, side).wait()
                product = jnp.dot(lhs[part], weights[side, part], preferred_element_type=F32)
                for which in range(2):
                    mine = product[which * rows : (which + 1) * rows]
                    out[which, side] = mine if part == 0 else out[which, side] + mine

    return pl.pallas_call(
        body,
        in_specs=[SMEM] + [WHOLE] * 3 + [IN_HBM] * 2,
        out_specs=WHOLE,
        out_shape=jax.ShapeDtypeStruct((2, 2, rows, cols), F32),
        scratch_shapes=[pltpu.VMEM((2, parts, width, cols), BF16), pltpu.SemaphoreType.DMA((2, parts))],
        compiler_params=kernel_params(WIDE),
        cost_estimate=QUICK,
        name="project_first",
    )(place, near, far, returned, wo, wo_mate)


def fetch_last(wo, wo_mate, weights, arrivals, pieces=4):
    _, width, cols = weights.shape
    first = wo.shape[0] - width
    step = width // pieces
    copies = []
    for side, source in enumerate((wo, wo_mate)):
        for piece in range(pieces):
            part = pl.ds(piece * step, step)
            copies.append(
                pltpu.make_async_copy(
                    source.at[pl.ds(first + piece * step, step)], weights.at[side, part], arrivals.at[side, piece]
                )
            )
    return copies


def finish(left, partial, weights, copies, pieces=4):
    width = weights.shape[1]
    step = width // pieces
    for side in range(2):
        total = partial[side]
        for piece in range(pieces):
            copies[side * pieces + piece].wait()
            part = slice(piece * step, (piece + 1) * step)
            total = total + jnp.dot(left[:, part], weights[side, part], preferred_element_type=F32)
        yield side, total


def project_next(place, partial, returned, wo, wo_mate):
    _, _, rows, cols = partial.shape
    width = PLANE * HS

    def body(place, partial, returned, wo, wo_mate, out, weights, arrivals):
        copies = fetch_last(wo, wo_mate, weights, arrivals)
        for copy in copies:
            copy.start()
        left = returned_rows(returned, 1 - place[1])
        for side, total in finish(left, partial[1], weights, copies):
            out[:, side * cols : (side + 1) * cols] = total.astype(BF16)

    return pl.pallas_call(
        body,
        in_specs=[SMEM] + [WHOLE] * 2 + [IN_HBM] * 2,
        out_specs=WHOLE,
        out_shape=jax.ShapeDtypeStruct((rows, 2 * cols), BF16),
        scratch_shapes=[pltpu.VMEM((2, width, cols), BF16), pltpu.SemaphoreType.DMA((2, 4))],
        compiler_params=kernel_params(WIDE),
        cost_estimate=QUICK,
        name="project_next",
    )(place, partial, returned, wo, wo_mate)


def project_own(place, partial, returned, wo, wo_mate):
    _, _, rows, cols = partial.shape
    width = PLANE * HS

    def body(place, partial, returned, wo, wo_mate, out, weights, arrivals):
        copies = fetch_last(wo, wo_mate, weights, arrivals)
        for copy in copies:
            copy.start()
        left = returned_rows(returned, place[1])
        for side, total in finish(left, partial[0], weights, copies):
            block = place[1] * C + place[2] + side * (1 - 2 * place[2])
            out[:, pl.ds(pl.multiple_of(block * cols, cols), cols)] = total.astype(BF16)

    return pl.pallas_call(
        body,
        in_specs=[SMEM] + [WHOLE] * 2 + [IN_HBM] * 2,
        out_specs=WHOLE,
        out_shape=jax.ShapeDtypeStruct((rows, XH * C * cols), BF16),
        scratch_shapes=[pltpu.VMEM((2, width, cols), BF16), pltpu.SemaphoreType.DMA((2, 4))],
        compiler_params=kernel_params(WIDE),
        cost_estimate=QUICK,
        name="project_own",
    )(place, partial, returned, wo, wo_mate)


def put_arrived(place, mixed, arrived):
    rows, width = arrived.shape
    cols = width // 2

    def body(place, mixed, arrived, out):
        out[...] = arrived[...]

    def target(side, place):
        return 0, (1 - place[1]) * C + place[2] + side * (1 - 2 * place[2])

    return pl.pallas_call(
        body,
        grid_spec=pltpu.PrefetchScalarGridSpec(
            num_scalar_prefetch=1,
            grid=(2,),
            in_specs=[ANYWHERE, pl.BlockSpec((rows, cols), lambda side, place: (0, side))],
            out_specs=pl.BlockSpec((rows, cols), target),
        ),
        out_shape=jax.ShapeDtypeStruct(mixed.shape, mixed.dtype),
        input_output_aliases={1: 0},
        compiler_params=kernel_params(16),
        cost_estimate=QUICK,
        name="put_arrived",
    )(place, mixed, arrived)


def on_device(qkv, clip_lengths, wo):
    _, frames, tok, model_width = qkv.shape
    half = model_width // 2
    quarter = half // 2
    x_place = lax.axis_index("xh")
    place = jnp.stack([lax.axis_index("z"), x_place, lax.axis_index("c")]).astype(jnp.int32)

    groups = tok // GROUP
    rows = frames * GROUP

    def by_plane(block):
        count = block.shape[0]
        heads = block.shape[3] // HS // PLANE
        split = block.reshape(count, frames, groups, GROUP, heads, PLANE, HS)
        return split.transpose(5, 0, 4, 2, 1, 3, 6).reshape(PLANE, count * heads, groups, rows, HS)

    keyvals, before = [], []
    for turn in range(ROUNDS):
        first = half + turn * PLANE * HS
        got = lax.all_to_all(by_plane(qkv[1:, :, :, first : first + PLANE * HS]), ("y", "xl"), 0, 0, tiled=True)
        keyvals.append(got)
        before.append(lax.ppermute(got, "z", [(i, (i + 1) % Z) for i in range(Z)]))
    last_two = jnp.stack([got[PLANE - 2 :] for got in keyvals])
    before2 = lax.ppermute(last_two, "z", [(i, (i + 2) % Z) for i in range(Z)])
    queries = lax.all_to_all(by_plane(qkv[:1, :, :, half:]), ("y", "xl"), 0, 0, tiled=True)

    own_cols = x_place * quarter
    far_cols = (1 - x_place) * quarter
    wo_mate = lax.ppermute(wo, "c", SWAP)
    own = lax.dynamic_slice(qkv, (0, 0, 0, own_cols), (3, frames, tok, quarter))
    far = lax.ppermute(lax.dynamic_slice(qkv, (0, 0, 0, far_cols), (3, frames, tok, quarter)), "xh", SWAP)
    mate_own = lax.ppermute(own, "c", SWAP)
    mate_far = lax.ppermute(far, "c", SWAP)
    near = spatial_attend(own, far, mate_own, mate_far, wo_mate)
    near = near.reshape(2, frames * tok, quarter)
    far = lax.ppermute(near, "xh", SWAP)

    returned = []
    after = (near, far)
    for turn in range(ROUNDS):
        mine = temporal_attend(turn, place, clip_lengths, queries, keyvals[turn], before[turn], before2, after[turn])
        sent = mine.reshape((PLANE * XH,) + mine.shape[2:])
        returned.append(lax.all_to_all(sent, ("y", "xl", "xh"), 0, 0, tiled=True).reshape(mine.shape))

    partial = project_first(place, near, far, returned[0], wo, wo_mate)
    for_next = project_next(place, partial, returned[1], wo, wo_mate)
    arrived = lax.ppermute(for_next, "xh", SWAP)
    mixed = project_own(place, partial, returned[1], wo, wo_mate)
    return put_arrived(place, mixed, arrived).reshape(frames, tok, model_width)


def solution(mesh):
    fine = Mesh(mesh.devices.reshape(Z, Y, XL, XH, C), ("z", "y", "xl", "xh", "c"))
    return jax.shard_map(
        on_device,
        mesh=fine,
        in_specs=(P(None, ("z", "y", "xl"), ("xh", "c"), None), P(), P(None, ("xh", "c"))),
        out_specs=P(("z", "y", "xl"), ("xh", "c"), None),
        check_vma=False,
    )
```

time: 516 us -> 120 us (0.23)
  starting transfers between devices: 225 us -> 40.4 us
  waiting for transfers between devices: 163 us -> 40 us
  local copies, waits for them, and re-layouts: 60.3 us -> 7.53 us
  Pallas kernels: 0 us -> 30.5 us
  matrix products: 30.2 us -> 0 us
  blocking collectives: 18.5 us -> 0 us
  between operations: 13.6 us -> 0.14 us
    ppermute x10 -> x9, starting transfers between devices: 225 us -> 13.6 us  [the longest x2 3.83 us: on_device(): before.append(lax.ppermute(got, 'z', [(i, (i + 1) % Z) for i in range(Z)]))]
    all_gather x2 -> x0, waiting for transfers between devices: 147 us -> none  [the longest x1 147 us: on_device(): lax.all_gather(attention, 'space', axis=0, tiled=True)]
    unnamed x26 -> x12, local copies, waits for them, and re-layouts: 36.6 us -> 0.82 us
    pallas_call x0 -> x7, Pallas kernels: none -> 30.5 us  [the longest x1 8.3 us: project_first(): pl.pallas_call(body, in_specs=[SMEM] + [WHOLE] * 3 + [IN_HBM] * 2, out_sp...]
    all_to_all x0 -> x5, starting transfers between devices: none -> 26.9 us  [the longest x2 11.5 us: on_device(): lax.all_to_all(sent, ('y', 'xl', 'xh'), 0, 0, tiled=True)]
    all_to_all x0 -> x5, waiting for transfers between devices: none -> 26.4 us  [the longest x2 22.2 us: on_device(): lax.all_to_all(by_plane(qkv[1:, :, :, first:first + PLANE * HS]), ('y', '...]
    dot_general x4 -> x0, matrix products: 22.5 us -> none  [the longest x1 9.14 us: on_device(): jnp.dot(lax.all_gather(attention, 'space', axis=0, tiled=True), wo, prefe...]
    slice x4 -> x1, local copies, waits for them, and re-layouts: 19.7 us -> 1.08 us  [on_device(): qkv[:1, :, :, half:]]
  transfers between devices with their start and end apart: 12 -> 14, of which waited for: 3 -> 5; matrix products, arithmetic and copies ran while one was open for 11% -> 6% of each run, Pallas kernels for 0% -> 20%
where the time goes in v2:
time: 120 us; the launch traced here: 119 us
  starting transfers between devices  40.4 us (34%)
  waiting for transfers between devices  40 us (33%)
  Pallas kernels  30.5 us (25%)
  local copies, waits for them, and re-layouts  7.53 us (6%)
    all_to_all x2, waiting for transfers between devices, on_device(): lax.all_to_all(by_plane(qkv[1:, :, :, first:first + PLANE * HS]), ('y', '...  22.2 us
    all_to_all x2, starting transfers between devices, on_device(): lax.all_to_all(sent, ('y', 'xl', 'xh'), 0, 0, tiled=True)  11.5 us
    all_to_all x2, starting transfers between devices, on_device(): lax.all_to_all(by_plane(qkv[1:, :, :, first:first + PLANE * HS]), ('y', '...  10.8 us
    ppermute x1, waiting for transfers between devices, on_device(): before2 = lax.ppermute(last_two, 'z', [(i, (i + 2) % Z) for i in range(Z)])  9.85 us
    pallas_call x1, Pallas kernels, project_first(): pl.pallas_call(body, in_specs=[SMEM] + [WHOLE] * 3 + [IN_HBM] * 2, out_sp...  8.3 us
    pallas_call x2, Pallas kernels, temporal_attend(): pl.pallas_call(body, in_specs=[SMEM, SMEM, WHOLE, WHOLE, WHOLE, WHOLE, AN...  7.42 us
    pallas_call x1, Pallas kernels, project_own(): pl.pallas_call(body, in_specs=[SMEM] + [WHOLE] * 2 + [IN_HBM] * 2, out_sp...  5.1 us
    pallas_call x1, Pallas kernels, project_next(): pl.pallas_call(body, in_specs=[SMEM] + [WHOLE] * 2 + [IN_HBM] * 2, out_sp...  4.93 us
  transfers between devices with their start and end apart: 14, of which 5 were waited for; matrix products, arithmetic and copies ran while one was open for 6% of the time, Pallas kernels for 20%

profile of v2, /device:TPU:2, one launch (start us, length us, event | category | flops | bytes accessed | tf_op | source)
XLA Modules:
  0.0 118.7 jit_solution(5524056324253729157)
XLA Ops:
  0.0 0.0 collective-permute-start.3
  0.0 1.5 %constant_dynamic-slice_fusion = (bf16[3,4,32,1024]{3,2,1,0:T(8,128)(2,1)S(1)}, bf16[3,4,32,1024]{3,2,1,0:T(8,128)(2,1)S(1)}) fusion(bf16[3,4,32,4096]{3,2,1,0:T(8,128)(2,1)} %param.3, s32[]{:T(128)S(6)} %select_n.7, s32[]{:T(128)S(6)} %select_n.6), kind=kLoop, calls=%fused_computation.9 | loop fusion | bytes 3145736 | tf_op jit(solution)/shard_map/dynamic_slice | solution.py:324
  1.5 2.2 %collective-permute-start = (bf16[3,4,32,1024]{3,2,1,0:T(8,128)(2,1)S(1)}, bf16[3,4,32,1024]{3,2,1,0:T(8,128)(2,1)}, u32[]{:S(2)}, u32[]{:S(2)}) collective-permute-start(bf16[3,4,32,1024]{3,2,1,0:T(8,128)(2,1)S(1)} %get-tuple-element.7), channel_id=1, source_target_pairs={{0,2},{2,0},{1,3},{3,1},{4,6},{6,4},{5,7},{7,5},{8,10},{10,8},{9,1... | collective-permute-start | bytes 2359304 | tf_op jit(solution)/shard_map/ppermute | solution.py:324
  3.8 1.3 %slice_bitcast_fusion = (bf16[2,4,4,8,1,8,128]{6,3,5,2,1,0,4:T(8,128)(2,1)S(1)}, bf16[2,4,4,8,1,8,128]{6,3,5,2,1,0,4:T(8,128)(2,1)S(1)}) fusion(bf16[3,4,32,4096]{3,2,1,0:T(8,128)(2,1)} %param.3), kind=kLoop, calls=%fused_computation.3 | loop fusion | bytes 2097152 | tf_op jit(solution)/shard_map/reshape | solution.py:307
  5.1 0.9 copy.12
  6.0 5.9 %all-to-all-start.1 = ((bf16[8,2,4,32,128]{4,3,2,1,0:T(8,128)(2,1)}), bf16[8,2,4,32,128]{4,3,2,1,0:T(8,128)(2,1)S(1)}, u32[]{:S(2)}, u32[]{:S(2)}) async-start(bf16[8,2,4,32,128]{4,3,2,1,0:T(8,128)(2,1)} %bitcast.31), calls=%async_computation.1 | async-start | bytes 1048576 | tf_op jit(solution)/shard_map/all_to_all | solution.py:313
  11.9 0.9 copy.11
  12.8 17.5 %all-to-all-done.1.refs_3_ = bf16[8,2,4,32,128]{4,3,2,1,0:T(8,128)(2,1)S(1)} async-done(((bf16[8,2,4,32,128]{4,3,2,1,0:T(8,128)(2,1)}), bf16[8,2,4,32,128]{4,3,2,1,0:T(8,128)(2,1)S(1)}, u32[]{:S(2)}, u32[]{:S(2)}) %all-to-all-start.1) | async-done | bytes 524320 | tf_op jit(solution)/shard_map/all_to_all | solution.py:313
  30.3 4.8 %all-to-all-start.2 = ((bf16[8,2,4,32,128]{4,3,2,1,0:T(8,128)(2,1)}), bf16[8,2,4,32,128]{4,3,2,1,0:T(8,128)(2,1)S(1)}, u32[]{:S(2)}, u32[]{:S(2)}) async-start(bf16[8,2,4,32,128]{4,3,2,1,0:T(8,128)(2,1)} %bitcast.30), calls=%async_computation.2 | async-start | bytes 1048576 | tf_op jit(solution)/shard_map/all_to_all | solution.py:313
  35.2 0.0 collective-permute-start.1
  35.2 0.0 collective-permute-done.far
  35.2 0.5 collective-permute-start.2
  35.7 1.1 slice.15
  36.8 0.9 copy.13
  37.7 1.9 %collective-permute-start.5 = (bf16[8,2,4,32,128]{4,3,2,1,0:T(8,128)(2,1)S(1)}, bf16[8,2,4,32,128]{4,3,2,1,0:T(8,128)(2,1)}, u32[]{:S(2)}, u32[]{:S(2)}) collective-permute-start(bf16[8,2,4,32,128]{4,3,2,1,0:T(8,128)(2,1)S(1)} %all-to-all-done.1.refs_3_), channel_id=1, source_target_pairs={{0,32},{32,64},{64,96},{96,128},{128,160},{160,192},{192,224},{224... | collective-permute-start | bytes 1572872 | tf_op jit(solution)/shard_map/ppermute | solution.py:315
  39.6 4.7 %all-to-all-done.2.refs_3_ = bf16[8,2,4,32,128]{4,3,2,1,0:T(8,128)(2,1)S(1)} async-done(((bf16[8,2,4,32,128]{4,3,2,1,0:T(8,128)(2,1)}), bf16[8,2,4,32,128]{4,3,2,1,0:T(8,128)(2,1)S(1)}, u32[]{:S(2)}, u32[]{:S(2)}) %all-to-all-start.2) | async-done | bytes 524320 | tf_op jit(solution)/shard_map/all_to_all | solution.py:313
  44.3 4.6 %all-to-all-start = ((bf16[8,2,4,32,128]{4,3,2,1,0:T(8,128)(2,1)}), bf16[8,2,4,32,128]{4,3,2,1,0:T(8,128)(2,1)S(1)}, u32[]{:S(2)}, u32[]{:S(2)}) async-start(bf16[8,2,4,32,128]{4,3,2,1,0:T(8,128)(2,1)} %bitcast.32), calls=%async_computation | async-start | bytes 1048576 | tf_op jit(solution)/shard_map/all_to_all | solution.py:318
  48.9 3.3 %collective-permute-start.6 = (bf16[2,2,2,4,32,128]{5,4,3,2,1,0:T(8,128)(2,1)S(1)}, bf16[2,2,2,4,32,128]{5,4,3,2,1,0:T(8,128)(2,1)S(1)}, u32[]{:S(2)}, u32[]{:S(2)}) collective-permute-start(bf16[2,2,2,4,32,128]{5,4,3,2,1,0:T(8,128)(2,1)S(1)} %pad_maximum_fusion), channel_id=1, source_target_pairs={{0,64},{32,96},{64,128},{96,160},{128,192},{160,224},{192,0},{224,... | collective-permute-start | bytes 786440 | tf_op jit(solution)/shard_map/ppermute | solution.py:317
  52.3 0.0 copy-start.4
  52.3 0.0 collective-permute-done.1.mate_own
  52.3 1.9 %collective-permute-start.7 = (bf16[8,2,4,32,128]{4,3,2,1,0:T(8,128)(2,1)S(1)}, bf16[8,2,4,32,128]{4,3,2,1,0:T(8,128)(2,1)}, u32[]{:S(2)}, u32[]{:S(2)}) collective-permute-start(bf16[8,2,4,32,128]{4,3,2,1,0:T(8,128)(2,1)S(1)} %all-to-all-done.2.refs_3_), channel_id=1, source_target_pairs={{0,32},{32,64},{64,96},{96,128},{128,160},{160,192},{192,224},{224... | collective-permute-start | bytes 1572872 | tf_op jit(solution)/shard_map/ppermute | solution.py:315
  54.2 0.0 collective-permute-done.2.mate_far
  54.2 0.0 collective-permute-done.3.after.wo_mate
  54.2 3.4 %spatial.1 = bf16[2,4,32,1024]{3,2,1,0:T(8,128)(2,1)S(1)} custom-call(bf16[3,4,32,1024]{3,2,1,0:T(8,128)(2,1)S(1)} %get-tuple-element.8.own, bf16[3,4,32,1024]{3,2,1,0:T(8,128)(2,1)} %collective-permute-done.far, bf16[3,4,32,1024]{3,2,1,0:T(8,128)(2,1)} %collective-permute-done.1.mate_own, bf16[3,4,32,1024]{3,2,1,0:T(8,128)(2,1)} %collective-permute-done.2.mate_far, ...), custom_call_target="tpu_custom_call" | custom-call | flops 1024 | bytes 1024 | tf_op jit(solution)/shard_map/spatial/pallas_call | solution.py:68
  57.5 0.0 copy-start
  57.6 1.5 %collective-permute-start.4 = (bf16[2,128,1024]{2,1,0:T(8,128)(2,1)S(1)}, bf16[2,128,1024]{2,1,0:T(8,128)(2,1)S(1)}, u32[]{:S(2)}, u32[]{:S(2)}) collective-permute-start(bf16[2,128,1024]{2,1,0:T(8,128)(2,1)S(1)} %bitcast.33), channel_id=1, source_target_pairs={{0,2},{2,0},{1,3},{3,1},{4,6},{6,4},{5,7},{7,5},{8,10},{10,8},{9,1... | collective-permute-start | bytes 1572872 | tf_op jit(solution)/shard_map/ppermute | solution.py:329
  59.1 0.1 pad_add_fusion.refs_0_.place
  59.1 0.0 copy-start.2
  59.1 0.0 all-to-all-done.refs_2_
  59.1 9.8 %collective-permute-done.6.refs_5_ = bf16[2,2,2,4,32,128]{5,4,3,2,1,0:T(8,128)(2,1)S(1)} collective-permute-done((bf16[2,2,2,4,32,128]{5,4,3,2,1,0:T(8,128)(2,1)S(1)}, bf16[2,2,2,4,32,128]{5,4,3,2,1,0:T(8,128)(2,1)S(1)}, u32[]{:S(2)}, u32[]{:S(2)}) %collective-permute-start.6) | collective-permute-done | bytes 262176 | tf_op jit(solution)/shard_map/ppermute | solution.py:317
  69.0 0.0 collective-permute-done.5.refs_4_
  69.0 0.0 copy-done.4
  69.0 3.6 %temporal.2 = bf16[8,2,128,128]{3,2,1,0:T(8,128)(2,1)} custom-call(s32[3]{0:T(128)S(1)} %pad_add_fusion.refs_0_.place, s32[16]{0:T(128)S(1)} %copy-done.4, bf16[8,2,4,32,128]{4,3,2,1,0:T(8,128)(2,1)S(1)} %all-to-all-done.refs_2_, bf16[8,2,4,32,128]{4,3,2,1,0:T(8,128)(2,1)S(1)} %all-to-all-done.1.refs_3_, ...), custom_call_target="tpu_custom_call" | custom-call | flops 1024 | bytes 1024 | tf_op jit(solution)/shard_map/temporal/pallas_call | solution.py:126
  72.6 6.3 %all-to-all-start.3 = ((bf16[16,128,128]{2,1,0:T(8,128)(2,1)}), bf16[16,128,128]{2,1,0:T(8,128)(2,1)}, u32[]{:S(2)}, u32[]{:S(2)}) async-start(bf16[16,128,128]{2,1,0:T(8,128)(2,1)} %bitcast.15), calls=%async_computation.3 | async-start | bytes 1048576 | tf_op jit(solution)/shard_map/all_to_all | solution.py:336
  78.9 0.0 collective-permute-done.7.refs_4_
  78.9 0.0 collective-permute-done.4.far.refs_6_
  78.9 0.0 copy-start.1
  78.9 3.8 %temporal.3 = bf16[8,2,128,128]{3,2,1,0:T(8,128)(2,1)} custom-call(s32[3]{0:T(128)S(1)} %pad_add_fusion.refs_0_.place, s32[16]{0:T(128)S(1)} %copy-done.4, bf16[8,2,4,32,128]{4,3,2,1,0:T(8,128)(2,1)S(1)} %all-to-all-done.refs_2_, bf16[8,2,4,32,128]{4,3,2,1,0:T(8,128)(2,1)S(1)} %all-to-all-done.2.refs_3_, ...), custom_call_target="tpu_custom_call" | custom-call | flops 1024 | bytes 1024 | tf_op jit(solution)/shard_map/temporal/pallas_call | solution.py:126
  82.7 0.0 copy-done
  82.7 0.0 copy-done.2
  82.7 4.2 %all-to-all-done.3 = bf16[16,128,128]{2,1,0:T(8,128)(2,1)} async-done(((bf16[16,128,128]{2,1,0:T(8,128)(2,1)}), bf16[16,128,128]{2,1,0:T(8,128)(2,1)}, u32[]{:S(2)}, u32[]{:S(2)}) %all-to-all-start.3) | async-done | bytes 524320 | tf_op jit(solution)/shard_map/all_to_all | solution.py:336
  87.0 5.2 %all-to-all-start.4 = ((bf16[16,128,128]{2,1,0:T(8,128)(2,1)}), bf16[16,128,128]{2,1,0:T(8,128)(2,1)S(1)}, u32[]{:S(2)}, u32[]{:S(2)}) async-start(bf16[16,128,128]{2,1,0:T(8,128)(2,1)} %bitcast.17), calls=%async_computation.4 | async-start | bytes 1048576 | tf_op jit(solution)/shard_map/all_to_all | solution.py:336
  92.2 0.0 copy-done.1
  92.2 8.3 %project_first.1.partial = f32[2,2,128,1024]{3,2,1,0:T(8,128)} custom-call(s32[3]{0:T(128)} %copy-done.2, bf16[2,128,1024]{2,1,0:T(8,128)(2,1)} %bitcast.35, bf16[2,128,1024]{2,1,0:T(8,128)(2,1)} %copy-done.1, bf16[8,2,128,128]{3,2,1,0:T(8,128)(2,1)} %bitcast.16.returned, bf16[4096,1024]{1,0:T(8,128)(2,1)} %wo.5, ...), custom_call_target="tpu_custom_call" | custom-call | flops 1024 | bytes 1024 | tf_op jit(solution)/shard_map/project_first/pallas_call | solution.py:179
  100.5 0.0 all-to-all-done.4
  100.5 0.0 copy-start.5
  100.5 0.8 copy-done.5
  101.3 4.9 %project_next.1 = bf16[128,2048]{1,0:T(8,128)(2,1)} custom-call(s32[3]{0:T(128)} %copy-done.2, f32[2,2,128,1024]{3,2,1,0:T(8,128)} %project_first.1.partial, bf16[8,2,128,128]{3,2,1,0:T(8,128)(2,1)} %bitcast.36, bf16[4096,1024]{1,0:T(8,128)(2,1)} %wo.5, bf16[4096,1024]{1,0:T(8,128)(2,1)} %collective-permute-done.3.after.wo_mate), custom_call_target="tpu_custom_call" | custom-call | flops 1024 | bytes 1024 | tf_op jit(solution)/shard_map/project_next/pallas_call | solution.py:231
  106.3 0.0 copy-start.3
  106.3 2.2 %collective-permute-start.8 = (bf16[128,2048]{1,0:T(8,128)(2,1)}, bf16[128,2048]{1,0:T(8,128)(2,1)S(1)}, u32[]{:S(2)}, u32[]{:S(2)}) collective-permute-start(bf16[128,2048]{1,0:T(8,128)(2,1)} %project_next.1), channel_id=1, source_target_pairs={{0,2},{2,0},{1,3},{3,1},{4,6},{6,4},{5,7},{7,5},{8,10},{10,8},{9,1... | collective-permute-start | bytes 1572872 | tf_op jit(solution)/shard_map/ppermute | solution.py:340
  108.4 5.1 %project_own.1.mixed = bf16[128,4096]{1,0:T(8,128)(2,1)} custom-call(s32[3]{0:T(128)} %copy-done.2, f32[2,2,128,1024]{3,2,1,0:T(8,128)} %project_first.1.partial, bf16[8,2,128,128]{3,2,1,0:T(8,128)(2,1)} %bitcast.37, bf16[4096,1024]{1,0:T(8,128)(2,1)} %wo.5, bf16[4096,1024]{1,0:T(8,128)(2,1)} %collective-permute-done.3.after.wo_mate), custom_call_target="tpu_custom_call" | custom-call | flops 1024 | bytes 1024 | tf_op jit(solution)/shard_map/project_own/pallas_call | solution.py:256
  113.5 3.7 %collective-permute-done.8.arrived = bf16[128,2048]{1,0:T(8,128)(2,1)S(1)} collective-permute-done((bf16[128,2048]{1,0:T(8,128)(2,1)}, bf16[128,2048]{1,0:T(8,128)(2,1)S(1)}, u32[]{:S(2)}, u32[]{:S(2)}) %collective-permute-start.8) | collective-permute-done | bytes 524320 | tf_op jit(solution)/shard_map/ppermute | solution.py:340
  117.3 0.0 copy-done.3
  117.3 1.4 %put_arrived.1 = bf16[128,4096]{1,0:T(8,128)(2,1)} custom-call(s32[3]{0:T(128)S(1)} %copy-done.3, bf16[128,4096]{1,0:T(8,128)(2,1)} %project_own.1.mixed, bf16[128,2048]{1,0:T(8,128)(2,1)S(1)} %collective-permute-done.8.arrived), custom_call_target="tpu_custom_call", output_to_operand_aliasing={{}: (1, {})} | custom-call | flops 1024 | bytes 1024 | tf_op jit(solution)/shard_map/put_arrived/pallas_call | solution.py:278
  (3 shorter events, 0.0 us)
Async XLA Ops:
  0.0 54.2 %collective-permute-start.3 = (bf16[4096,1024]{1,0:T(8,128)(2,1)}, bf16[4096,1024]{1,0:T(8,128)(2,1)}, u32[]{:S(2)}, u32[]{:S(2)}) collective-permute-start(bf16[4096,1024]{1,0:T(8,128)(2,1)} %wo.5), channel_id=1, source_target_pairs={{0,1},{1,0},{2,3},{3,2},{4,5},{5,4},{6,7},{7,6},{8,9},{9,8},{10,11... | collective-permute-start | bytes 25165832 | tf_op jit(solution)/shard_map/ppermute | solution.py:322
  1.5 33.6 %collective-permute-start = (bf16[3,4,32,1024]{3,2,1,0:T(8,128)(2,1)S(1)}, bf16[3,4,32,1024]{3,2,1,0:T(8,128)(2,1)}, u32[]{:S(2)}, u32[]{:S(2)}) collective-permute-start(bf16[3,4,32,1024]{3,2,1,0:T(8,128)(2,1)S(1)} %get-tuple-element.7), channel_id=1, source_target_pairs={{0,2},{2,0},{1,3},{3,1},{4,6},{6,4},{5,7},{7,5},{8,10},{10,8},{9,1... | collective-permute-start | bytes 2359304 | tf_op jit(solution)/shard_map/ppermute | solution.py:324
  6.0 24.4 %all-to-all-start.1 = ((bf16[8,2,4,32,128]{4,3,2,1,0:T(8,128)(2,1)}), bf16[8,2,4,32,128]{4,3,2,1,0:T(8,128)(2,1)S(1)}, u32[]{:S(2)}, u32[]{:S(2)}) async-start(bf16[8,2,4,32,128]{4,3,2,1,0:T(8,128)(2,1)} %bitcast.31), calls=%async_computation.1 | async-start | bytes 1048576 | tf_op jit(solution)/shard_map/all_to_all | solution.py:313
  30.3 13.9 %all-to-all-start.2 = ((bf16[8,2,4,32,128]{4,3,2,1,0:T(8,128)(2,1)}), bf16[8,2,4,32,128]{4,3,2,1,0:T(8,128)(2,1)S(1)}, u32[]{:S(2)}, u32[]{:S(2)}) async-start(bf16[8,2,4,32,128]{4,3,2,1,0:T(8,128)(2,1)} %bitcast.30), calls=%async_computation.2 | async-start | bytes 1048576 | tf_op jit(solution)/shard_map/all_to_all | solution.py:313
  35.2 17.1 %collective-permute-start.1 = (bf16[3,4,32,1024]{3,2,1,0:T(8,128)(2,1)S(1)}, bf16[3,4,32,1024]{3,2,1,0:T(8,128)(2,1)}, u32[]{:S(2)}, u32[]{:S(2)}) collective-permute-start(bf16[3,4,32,1024]{3,2,1,0:T(8,128)(2,1)S(1)} %get-tuple-element.8.own), channel_id=1, source_target_pairs={{0,1},{1,0},{2,3},{3,2},{4,5},{5,4},{6,7},{7,6},{8,9},{9,8},{10,11... | collective-permute-start | bytes 2359304 | tf_op jit(solution)/shard_map/ppermute | solution.py:325
  35.2 19.0 %collective-permute-start.2 = (bf16[3,4,32,1024]{3,2,1,0:T(8,128)(2,1)}, bf16[3,4,32,1024]{3,2,1,0:T(8,128)(2,1)}, u32[]{:S(2)}, u32[]{:S(2)}) collective-permute-start(bf16[3,4,32,1024]{3,2,1,0:T(8,128)(2,1)} %collective-permute-done.far), channel_id=1, source_target_pairs={{0,1},{1,0},{2,3},{3,2},{4,5},{5,4},{6,7},{7,6},{8,9},{9,8},{10,11... | collective-permute-start | bytes 2359304 | tf_op jit(solution)/shard_map/ppermute | solution.py:326
  37.7 31.3 %collective-permute-start.5 = (bf16[8,2,4,32,128]{4,3,2,1,0:T(8,128)(2,1)S(1)}, bf16[8,2,4,32,128]{4,3,2,1,0:T(8,128)(2,1)}, u32[]{:S(2)}, u32[]{:S(2)}) collective-permute-start(bf16[8,2,4,32,128]{4,3,2,1,0:T(8,128)(2,1)S(1)} %all-to-all-done.1.refs_3_), channel_id=1, source_target_pairs={{0,32},{32,64},{64,96},{96,128},{128,160},{160,192},{192,224},{224... | collective-permute-start | bytes 1572872 | tf_op jit(solution)/shard_map/ppermute | solution.py:315
  44.3 14.8 %all-to-all-start = ((bf16[8,2,4,32,128]{4,3,2,1,0:T(8,128)(2,1)}), bf16[8,2,4,32,128]{4,3,2,1,0:T(8,128)(2,1)S(1)}, u32[]{:S(2)}, u32[]{:S(2)}) async-start(bf16[8,2,4,32,128]{4,3,2,1,0:T(8,128)(2,1)} %bitcast.32), calls=%async_computation | async-start | bytes 1048576 | tf_op jit(solution)/shard_map/all_to_all | solution.py:318
  48.9 20.1 %collective-permute-start.6 = (bf16[2,2,2,4,32,128]{5,4,3,2,1,0:T(8,128)(2,1)S(1)}, bf16[2,2,2,4,32,128]{5,4,3,2,1,0:T(8,128)(2,1)S(1)}, u32[]{:S(2)}, u32[]{:S(2)}) collective-permute-start(bf16[2,2,2,4,32,128]{5,4,3,2,1,0:T(8,128)(2,1)S(1)} %pad_maximum_fusion), channel_id=1, source_target_pairs={{0,64},{32,96},{64,128},{96,160},{128,192},{160,224},{192,0},{224,... | collective-permute-start | bytes 786440 | tf_op jit(solution)/shard_map/ppermute | solution.py:317
  52.3 16.7 %copy-start.4 = (s32[16]{0:T(128)S(1)}, s32[16]{0:T(128)}, u32[]{:S(2)}) copy-start(s32[16]{0:T(128)} %refs_1_.3) | copy-start | bytes 196
  52.3 26.6 %collective-permute-start.7 = (bf16[8,2,4,32,128]{4,3,2,1,0:T(8,128)(2,1)S(1)}, bf16[8,2,4,32,128]{4,3,2,1,0:T(8,128)(2,1)}, u32[]{:S(2)}, u32[]{:S(2)}) collective-permute-start(bf16[8,2,4,32,128]{4,3,2,1,0:T(8,128)(2,1)S(1)} %all-to-all-done.2.refs_3_), channel_id=1, source_target_pairs={{0,32},{32,64},{64,96},{96,128},{128,160},{160,192},{192,224},{224... | collective-permute-start | bytes 1572872 | tf_op jit(solution)/shard_map/ppermute | solution.py:315
  57.5 25.2 %copy-start = (bf16[2,4,32,1024]{3,2,1,0:T(8,128)(2,1)}, bf16[2,4,32,1024]{3,2,1,0:T(8,128)(2,1)S(1)}, u32[]{:S(2)}) copy-start(bf16[2,4,32,1024]{3,2,1,0:T(8,128)(2,1)S(1)} %spatial.1) | copy-start | bytes 1572868
  57.6 21.3 %collective-permute-start.4 = (bf16[2,128,1024]{2,1,0:T(8,128)(2,1)S(1)}, bf16[2,128,1024]{2,1,0:T(8,128)(2,1)S(1)}, u32[]{:S(2)}, u32[]{:S(2)}) collective-permute-start(bf16[2,128,1024]{2,1,0:T(8,128)(2,1)S(1)} %bitcast.33), channel_id=1, source_target_pairs={{0,2},{2,0},{1,3},{3,1},{4,6},{6,4},{5,7},{7,5},{8,10},{10,8},{9,1... | collective-permute-start | bytes 1572872 | tf_op jit(solution)/shard_map/ppermute | solution.py:329
  59.1 23.6 %copy-start.2 = (s32[3]{0:T(128)}, s32[3]{0:T(128)S(1)}, u32[]{:S(2)}) copy-start(s32[3]{0:T(128)S(1)} %pad_add_fusion.refs_0_.place) | copy-start | bytes 40
  72.6 14.4 %all-to-all-start.3 = ((bf16[16,128,128]{2,1,0:T(8,128)(2,1)}), bf16[16,128,128]{2,1,0:T(8,128)(2,1)}, u32[]{:S(2)}, u32[]{:S(2)}) async-start(bf16[16,128,128]{2,1,0:T(8,128)(2,1)} %bitcast.15), calls=%async_computation.3 | async-start | bytes 1048576 | tf_op jit(solution)/shard_map/all_to_all | solution.py:336
  78.9 13.3 %copy-start.1 = (bf16[2,128,1024]{2,1,0:T(8,128)(2,1)}, bf16[2,128,1024]{2,1,0:T(8,128)(2,1)S(1)}, u32[]{:S(2)}) copy-start(bf16[2,128,1024]{2,1,0:T(8,128)(2,1)S(1)} %collective-permute-done.4.far.refs_6_) | copy-start | bytes 1572868
  87.0 13.5 %all-to-all-start.4 = ((bf16[16,128,128]{2,1,0:T(8,128)(2,1)}), bf16[16,128,128]{2,1,0:T(8,128)(2,1)S(1)}, u32[]{:S(2)}, u32[]{:S(2)}) async-start(bf16[16,128,128]{2,1,0:T(8,128)(2,1)} %bitcast.17), calls=%async_computation.4 | async-start | bytes 1048576 | tf_op jit(solution)/shard_map/all_to_all | solution.py:336
  100.5 0.8 copy-start.5
  106.3 11.0 %copy-start.3 = (s32[3]{0:T(128)S(1)}, s32[3]{0:T(128)}, u32[]{:S(2)}) copy-start(s32[3]{0:T(128)} %copy-done.2) | copy-start | bytes 40
  106.3 11.0 %collective-permute-start.8 = (bf16[128,2048]{1,0:T(8,128)(2,1)}, bf16[128,2048]{1,0:T(8,128)(2,1)S(1)}, u32[]{:S(2)}, u32[]{:S(2)}) collective-permute-start(bf16[128,2048]{1,0:T(8,128)(2,1)} %project_next.1), channel_id=1, source_target_pairs={{0,2},{2,0},{1,3},{3,1},{4,6},{6,4},{5,7},{7,5},{8,10},{10,8},{9,1... | collective-permute-start | bytes 1572872 | tf_op jit(solution)/shard_map/ppermute | solution.py:340

commit v3 on v2

v3 whole, which is shorter than its diff:
```python
import jax
import jax.numpy as jnp
import numpy as np
from jax import lax
from jax.experimental import pallas as pl
from jax.experimental.pallas import tpu as pltpu
from jax.sharding import Mesh, PartitionSpec as P

HS = 128
Z, Y, XL, XH, C = 8, 4, 2, 2, 2
PLANE = Y * XL
EXP2_SCALE = HS ** (-0.5) * float(np.log2(np.e))
F32 = jnp.float32
BF16 = jnp.bfloat16
GROUP = 8
ROUNDS = 2

SWAP = [(0, 1), (1, 0)]

SMEM = pl.BlockSpec(memory_space=pltpu.SMEM)
WHOLE = pl.BlockSpec(memory_space=pltpu.VMEM)
ANYWHERE = pl.BlockSpec(memory_space=pl.ANY)
IN_HBM = pl.BlockSpec(memory_space=pltpu.HBM)
LAST_VMEM = 44
QUICK = pl.CostEstimate(flops=1024, bytes_accessed=1024, transcendentals=0)


def kernel_params(mebibytes):
    return pltpu.CompilerParams(vmem_limit_bytes=mebibytes * 1024 * 1024)


def behind(array, *after):
    def body(*refs):
        pass

    return pl.pallas_call(
        body,
        in_specs=[ANYWHERE] * (1 + len(after)),
        out_specs=ANYWHERE,
        out_shape=jax.ShapeDtypeStruct(array.shape, array.dtype),
        input_output_aliases={0: 0},
        compiler_params=kernel_params(1),
        cost_estimate=QUICK,
        name="behind",
    )(array, *after)


def softmax_parts(scores):
    top = jnp.max(scores, axis=-1, keepdims=True)
    return jnp.exp2((scores - top) * EXP2_SCALE).astype(BF16)


def weighted(raised, values):
    both = jnp.concatenate([values, jnp.ones_like(values)], axis=1)
    result = jnp.dot(raised, both, preferred_element_type=F32)
    return result[:, :HS] / result[:, HS:]


def spatial_attend(own, far, mate_own, mate_far, after):
    _, frames, tok, width = own.shape

    def body(own, far, mate_own, mate_far, after, out):
        blocks = [(f, slice(head * HS, (head + 1) * HS)) for f in range(frames) for head in range(width // HS)]

        def keyvals_of(which, f, cols):
            return jnp.concatenate([ref[which, f, :, cols] for ref in (own, far, mate_own, mate_far)], axis=0)

        for first in range(0, len(blocks), 8):
            batch = blocks[first : first + 8]
            scores = []
            for f, cols in batch:
                queries = jnp.concatenate([own[0, f, :, cols], far[0, f, :, cols]], axis=0)
                scores.append(
                    lax.dot_general(
                        queries, keyvals_of(1, f, cols), (((1,), (1,)), ((), ())), preferred_element_type=F32
                    )
                )
            raised = [softmax_parts(block) for block in scores]
            results = [weighted(block, keyvals_of(2, f, cols)).astype(BF16) for block, (f, cols) in zip(raised, batch)]
            for result, (f, cols) in zip(results, batch):
                out[0, f, :, cols] = result[:tok]
                out[1, f, :, cols] = result[tok:]

    return pl.pallas_call(
        body,
        in_specs=[WHOLE] * 4 + [ANYWHERE],
        out_specs=WHOLE,
        out_shape=jax.ShapeDtypeStruct((2, frames, tok, width), BF16),
        compiler_params=kernel_params(16),
        cost_estimate=QUICK,
        name="spatial",
    )(own, far, mate_own, mate_far, after)


def temporal_scores(clips, place, lengths, queries, keyvals, first_query, first_key, bias, store):
    _, _, groups, rows, _ = queries.shape
    frames_dev = rows // GROUP
    query_rows, key_count = bias.shape
    first = place[0] * (PLANE * frames_dev)

    row = lax.broadcasted_iota(jnp.int32, (query_rows, 1), 0)
    frame = first + first_query * frames_dev + row // GROUP
    start = jnp.zeros_like(frame)
    begin = jnp.int32(0)
    for clip in range(clips):
        start = jnp.where(frame >= begin, begin, start)
        begin = begin + lengths[clip]
    oldest = first + first_key * frames_dev
    token = (row % GROUP) * 4096
    low = token + start - oldest
    high = token + frame - oldest
    col = lax.broadcasted_iota(jnp.int32, (1, key_count), 1)
    code = (col % GROUP) * 4096 + col // GROUP
    bias[...] = jnp.where((code >= low) & (code <= high), 0.0, -1e30)

    blocks = slice(first_query, first_query + query_rows // rows)
    for turn in range(ROUNDS):
        pieces = []
        for group in range(groups):
            def rows_of(which):
                return jnp.concatenate([part[:, which, group].reshape(-1, HS) for part in keyvals[turn]], axis=0)

            asked = queries[blocks, turn, group].reshape(-1, HS)
            scores = lax.dot_general(asked, rows_of(0), (((1,), (1,)), ((), ())), preferred_element_type=F32)
            result = weighted(softmax_parts(scores + bias[...]), rows_of(1))
            pieces.append(result.reshape(-1, 1, GROUP, HS))
        joined = jnp.concatenate(pieces, axis=1).reshape(-1, frames_dev * groups * GROUP, HS).astype(BF16)
        store(turn, joined)


EARLY = 2


def temporal_late(place, lengths, queries, own, before):
    sources, _, groups, rows, _ = queries.shape
    clips = lengths.shape[0]

    def body(place, lengths, queries, *refs):
        own, before = refs[:ROUNDS], refs[ROUNDS : 2 * ROUNDS]
        out, bias = refs[2 * ROUNDS :]

        def store(turn, joined):
            for copy in range(XH):
                out[EARLY:, copy, :, turn * HS : (turn + 1) * HS] = joined

        keyvals = [(before[turn], own[turn]) for turn in range(ROUNDS)]
        temporal_scores(clips, place, lengths, queries, keyvals, EARLY, -sources, bias, store)

    return pl.pallas_call(
        body,
        in_specs=[SMEM, SMEM] + [WHOLE] * (1 + 2 * ROUNDS),
        out_specs=WHOLE,
        out_shape=jax.ShapeDtypeStruct((sources, XH, groups * rows, ROUNDS * HS), BF16),
        scratch_shapes=[pltpu.VMEM(((sources - EARLY) * rows, 2 * sources * rows), F32)],
        compiler_params=kernel_params(12),
        cost_estimate=QUICK,
        name="temporal_late",
    )(place, lengths, queries, *own, *before)


def temporal_early(place, lengths, queries, own, before, before2, late, after):
    sources, _, groups, rows, _ = queries.shape
    clips = lengths.shape[0]

    def body(place, lengths, queries, *refs):
        own, before, before2 = (refs[part * ROUNDS : (part + 1) * ROUNDS] for part in range(3))
        out, bias = refs[-2:]

        def store(turn, joined):
            for copy in range(XH):
                out[:, copy, :, turn * HS : (turn + 1) * HS] = joined

        keyvals = [(before2[turn], before[turn], own[turn].at[:EARLY]) for turn in range(ROUNDS)]
        temporal_scores(clips, place, lengths, queries, keyvals, 0, -sources - EARLY, bias, store)

    block = (EARLY,) + late.shape[1:]
    return pl.pallas_call(
        body,
        grid=(1,),
        in_specs=[SMEM, SMEM] + [WHOLE] * (1 + 3 * ROUNDS) + [ANYWHERE] * 2,
        out_specs=pl.BlockSpec(block, lambda step: (0, 0, 0, 0)),
        out_shape=jax.ShapeDtypeStruct(late.shape, BF16),
        scratch_shapes=[pltpu.VMEM((EARLY * rows, (sources + 2 * EARLY) * rows), F32)],
        input_output_aliases={3 + 3 * ROUNDS: 0},
        compiler_params=kernel_params(12),
        cost_estimate=QUICK,
        name="temporal_early",
    )(place, lengths, queries, *own, *before, *before2, late, after)


def returned_rows(returned, x_half):
    return jnp.concatenate([returned[source, x_half] for source in range(PLANE)], axis=1)


def fetch_rows(sources, starts, targets, arrivals):
    return [
        pltpu.make_async_copy(source.at[pl.ds(start, targets.shape[2])], targets.at[side, part], arrivals.at[side, part])
        for part, start in enumerate(starts)
        for side, source in enumerate(sources)
    ]


def project_first(place, near, far, wo, wo_mate):
    rows, width = near.shape[1:]
    cols = wo.shape[1]

    def body(place, near, far, wo, wo_mate, out, weights, arrivals):
        x_place = place[1]
        starts = [pl.multiple_of(x_place * width, width), pl.multiple_of((1 - x_place) * width, width)]
        copies = fetch_rows((wo, wo_mate), starts, weights, arrivals)
        for copy in copies:
            copy.start()
        lhs = [
            jnp.concatenate([near[0], near[1]], axis=0),
            jnp.concatenate([far[1], far[0]], axis=0),
        ]
        for part in range(2):
            for side in range(2):
                copies[part * 2 + side].wait()
                product = jnp.dot(lhs[part], weights[side, part], preferred_element_type=F32)
                for which in range(2):
                    mine = product[which * rows : (which + 1) * rows]
                    out[which, side] = mine if part == 0 else out[which, side] + mine

    return pl.pallas_call(
        body,
        in_specs=[SMEM] + [WHOLE] * 2 + [IN_HBM] * 2,
        out_specs=WHOLE,
        out_shape=jax.ShapeDtypeStruct((2, 2, rows, cols), F32),
        scratch_shapes=[pltpu.VMEM((2, 2, width, cols), BF16), pltpu.SemaphoreType.DMA((2, 2))],
        compiler_params=kernel_params(LAST_VMEM),
        cost_estimate=QUICK,
        name="project_first",
    )(place, near, far, wo, wo_mate)


def project_last(name, which, place, partial, returned, wo, wo_mate, out_cols, store):
    _, _, rows, cols = partial.shape
    half = wo.shape[0] // 2
    parts = 4
    step = half // parts

    def body(place, partial, returned, wo, wo_mate, out, weights, arrivals):
        copies = fetch_rows((wo, wo_mate), [half + part * step for part in range(parts)], weights, arrivals)
        for copy in copies:
            copy.start()
        left = returned_rows(returned, 1 - place[1] if which else place[1])
        total = [partial[which, 0], partial[which, 1]]
        for part in range(parts):
            for side in range(2):
                copies[part * 2 + side].wait()
                block = left[:, part * step : (part + 1) * step]
                total[side] = total[side] + jnp.dot(block, weights[side, part], preferred_element_type=F32)
        for side in range(2):
            store(place, out, side, total[side].astype(BF16))

    return pl.pallas_call(
        body,
        in_specs=[SMEM] + [WHOLE] * 2 + [IN_HBM] * 2,
        out_specs=WHOLE,
        out_shape=jax.ShapeDtypeStruct((rows, out_cols), BF16),
        scratch_shapes=[pltpu.VMEM((2, parts, step, cols), BF16), pltpu.SemaphoreType.DMA((2, parts))],
        compiler_params=kernel_params(LAST_VMEM),
        cost_estimate=QUICK,
        name=name,
    )(place, partial, returned, wo, wo_mate)


def project_next(place, partial, returned, wo, wo_mate):
    cols = wo.shape[1]

    def store(place, out, side, block):
        out[:, side * cols : (side + 1) * cols] = block

    return project_last("project_next", 1, place, partial, returned, wo, wo_mate, 2 * cols, store)


def project_own(place, partial, returned, wo, wo_mate):
    cols = wo.shape[1]

    def store(place, out, side, block):
        target = place[1] * C + place[2] + side * (1 - 2 * place[2])
        out[:, pl.ds(pl.multiple_of(target * cols, cols), cols)] = block

    return project_last("project_own", 0, place, partial, returned, wo, wo_mate, XH * C * cols, store)


def put_arrived(place, mixed, arrived):
    rows, width = arrived.shape
    cols = width // 2

    def body(place, mixed, arrived, out):
        out[...] = arrived[...]

    def target(side, place):
        return 0, (1 - place[1]) * C + place[2] + side * (1 - 2 * place[2])

    return pl.pallas_call(
        body,
        grid_spec=pltpu.PrefetchScalarGridSpec(
            num_scalar_prefetch=1,
            grid=(2,),
            in_specs=[ANYWHERE, pl.BlockSpec((rows, cols), lambda side, place: (0, side))],
            out_specs=pl.BlockSpec((rows, cols), target),
        ),
        out_shape=jax.ShapeDtypeStruct(mixed.shape, mixed.dtype),
        input_output_aliases={1: 0},
        compiler_params=kernel_params(16),
        cost_estimate=QUICK,
        name="put_arrived",
    )(place, mixed, arrived)


def on_device(qkv, clip_lengths, wo):
    _, frames, tok, model_width = qkv.shape
    half = model_width // 2
    quarter = half // 2
    x_place = lax.axis_index("xh")
    place = jnp.stack([lax.axis_index("z"), x_place, lax.axis_index("c")]).astype(jnp.int32)

    groups = tok // GROUP
    rows = frames * GROUP

    def by_plane(block, turn=None):
        split = block.reshape(block.shape[0], frames, groups, GROUP, PLANE, ROUNDS, HS)
        if turn is not None:
            split = split[:, :, :, :, :, turn : turn + 1]
        return split.transpose(4, 0, 5, 2, 1, 3, 6).reshape(PLANE, -1, groups, rows, HS)

    onward = [(i, (i + 1) % Z) for i in range(Z)]
    keyvals, before, before2 = [], [], []
    for turn in range(ROUNDS):
        got = lax.all_to_all(by_plane(qkv[1:, :, :, half:], turn), ("y", "xl"), 0, 0, tiled=True)
        keyvals.append(got)
        before.append(lax.ppermute(got, "z", onward))
        before2.append(lax.ppermute(before[-1][PLANE - EARLY :], "z", onward))
    own_cols = x_place * quarter
    far_cols = (1 - x_place) * quarter
    wo_mate = lax.ppermute(wo, "c", SWAP)
    own = lax.dynamic_slice(qkv, (0, 0, 0, own_cols), (3, frames, tok, quarter))
    far = lax.ppermute(lax.dynamic_slice(qkv, (0, 0, 0, far_cols), (3, frames, tok, quarter)), "xh", SWAP)
    mate_own = lax.ppermute(own, "c", SWAP)
    mate_far = lax.ppermute(far, "c", SWAP)
    near = spatial_attend(own, far, mate_own, mate_far, wo_mate)
    near = near.reshape(2, frames * tok, quarter)
    far = lax.ppermute(near, "xh", SWAP)

    queries = by_plane(qkv[:1, :, :, half:])
    queries = lax.all_to_all(queries, ("y", "xl"), 0, 0, tiled=True)
    mine = temporal_late(place, clip_lengths, queries, keyvals, before)
    mine = temporal_early(place, clip_lengths, queries, keyvals, before, before2, mine, far)
    sent = mine.reshape((PLANE * XH,) + mine.shape[2:])
    returned = lax.all_to_all(sent, ("y", "xl", "xh"), 0, 0, tiled=True).reshape(mine.shape)

    partial = project_first(place, near, far, wo, wo_mate)
    for_next = project_next(place, partial, returned, wo, wo_mate)
    arrived = lax.ppermute(for_next, "xh", SWAP)
    mixed = project_own(place, partial, returned, wo, wo_mate)
    return put_arrived(place, mixed, arrived).reshape(frames, tok, model_width)


def solution(mesh):
    fine = Mesh(mesh.devices.reshape(Z, Y, XL, XH, C), ("z", "y", "xl", "xh", "c"))
    return jax.shard_map(
        on_device,
        mesh=fine,
        in_specs=(P(None, ("z", "y", "xl"), ("xh", "c"), None), P(), P(None, ("xh", "c"))),
        out_specs=P(("z", "y", "xl"), ("xh", "c"), None),
        check_vma=False,
    )
```

time: 120 us -> 114 us (0.950)
  starting transfers between devices: 40.4 us -> 33.9 us
  Pallas kernels: 30.5 us -> 26.1 us
  waiting for transfers between devices: 40 us -> 43.3 us
    ppermute x1, waiting for transfers between devices: 0.01 us -> 11.4 us  [on_device(): lax.ppermute(lax.dynamic_slice(qkv, (0, 0, 0, far_cols), (3, frames, tok,...]
    all_to_all x3, waiting for transfers between devices: 22.2 us -> 16.1 us  [the longest x2 13 us: on_device(): lax.all_to_all(by_plane(qkv[1:, :, :, half:], turn), ('y', 'xl'), 0, 0, t...]
    all_to_all x2 -> x1, starting transfers between devices: 11.5 us -> 6.29 us  [on_device(): lax.all_to_all(sent, ('y', 'xl', 'xh'), 0, 0, tiled=True)]
    ppermute x3 -> x4, waiting for transfers between devices: 9.85 us -> 5.22 us  [the longest x2 4.78 us: on_device(): before.append(lax.ppermute(got, 'z', onward))]
    pallas_call x5, Pallas kernels: 25.8 us -> 21.4 us  [the longest x2 9.68 us: project_last(): pl.pallas_call(body, in_specs=[SMEM] + [WHOLE] * 2 + [IN_HBM] * 2, out_sp...]
    reshape x4 -> x1, local copies, waits for them, and re-layouts: 4.09 us -> 0.93 us  [by_plane(): block.reshape(block.shape[0], frames, groups, GROUP, PLANE, ROUNDS, HS)]
    slice x1 -> x5, local copies, waits for them, and re-layouts: 1.08 us -> 3.34 us  [the longest x1 1.29 us: on_device(): qkv[1:, :, :, half:]]
    unnamed x12 -> x8, local copies, waits for them, and re-layouts: 0.82 us -> 2.91 us
  transfers between devices with their start and end apart: 14 -> 14, of which waited for: 5 -> 8; matrix products, arithmetic and copies ran while one was open for 6% -> 7% of each run, Pallas kernels for 20% -> 15%
where the time goes in v3:
time: 114 us; the launch traced here: 112 us
  waiting for transfers between devices  43.3 us (38%)
  starting transfers between devices  33.9 us (30%)
  Pallas kernels  26.1 us (23%)
  local copies, waits for them, and re-layouts  8.72 us (8%)
    all_to_all x2, waiting for transfers between devices, on_device(): lax.all_to_all(by_plane(qkv[1:, :, :, half:], turn), ('y', 'xl'), 0, 0, t...  13 us
    ppermute x1, waiting for transfers between devices, on_device(): lax.ppermute(lax.dynamic_slice(qkv, (0, 0, 0, far_cols), (3, frames, tok,...  11.4 us
    all_to_all x2, starting transfers between devices, on_device(): lax.all_to_all(by_plane(qkv[1:, :, :, half:], turn), ('y', 'xl'), 0, 0, t...  10.8 us
    pallas_call x2, Pallas kernels, project_last(): pl.pallas_call(body, in_specs=[SMEM] + [WHOLE] * 2 + [IN_HBM] * 2, out_sp...  9.68 us
    all_to_all x1, starting transfers between devices, on_device(): lax.all_to_all(sent, ('y', 'xl', 'xh'), 0, 0, tiled=True)  6.29 us
    ppermute x1, waiting for transfers between devices, on_device(): arrived = lax.ppermute(for_next, 'xh', SWAP)  5.44 us
    pallas_call x1, Pallas kernels, project_first(): pl.pallas_call(body, in_specs=[SMEM] + [WHOLE] * 2 + [IN_HBM] * 2, out_sp...  5.37 us
    all_to_all x1, waiting for transfers between devices, on_device(): lax.all_to_all(sent, ('y', 'xl', 'xh'), 0, 0, tiled=True)  5.26 us
  transfers between devices with their start and end apart: 14, of which 8 were waited for; matrix products, arithmetic and copies ran while one was open for 7% of the time, Pallas kernels for 15%

profile of v3, /device:TPU:2, one launch (start us, length us, event | category | flops | bytes accessed | tf_op | source)
XLA Modules:
  0.0 112.3 jit_solution(817752742497483873)
XLA Ops:
  0.0 0.0 collective-permute-start.3
  0.0 1.5 %constant_dynamic-slice_fusion = (bf16[3,4,32,1024]{3,2,1,0:T(8,128)(2,1)S(1)}, bf16[3,4,32,1024]{3,2,1,0:T(8,128)(2,1)S(1)}) fusion(bf16[3,4,32,4096]{3,2,1,0:T(8,128)(2,1)} %param.3, s32[]{:T(128)S(6)} %select_n.7, s32[]{:T(128)S(6)} %select_n.6), kind=kLoop, calls=%fused_computation.4 | loop fusion | bytes 3145736 | tf_op jit(solution)/shard_map/dynamic_slice | solution.py:341
  1.5 2.2 %collective-permute-start = (bf16[3,4,32,1024]{3,2,1,0:T(8,128)(2,1)S(1)}, bf16[3,4,32,1024]{3,2,1,0:T(8,128)(2,1)}, u32[]{:S(2)}, u32[]{:S(2)}) collective-permute-start(bf16[3,4,32,1024]{3,2,1,0:T(8,128)(2,1)S(1)} %get-tuple-element.5), channel_id=1, source_target_pairs={{0,2},{2,0},{1,3},{3,1},{4,6},{6,4},{5,7},{7,5},{8,10},{10,8},{9,1... | collective-permute-start | bytes 2359304 | tf_op jit(solution)/shard_map/ppermute | solution.py:341
  3.8 1.3 %slice.20 = bf16[2,4,32,2048]{3,2,1,0:T(8,128)(2,1)S(1)} slice(bf16[3,4,32,4096]{3,2,1,0:T(8,128)(2,1)} %param.3), slice={[1:3], [0:4], [0:32], [2048:4096]} | slice | bytes 2097152 | tf_op jit(solution)/shard_map/slice | solution.py:333
  5.1 0.3 fusion
  5.3 0.9 copy.15
  6.3 5.9 %all-to-all-start.1 = ((bf16[8,2,4,32,128]{4,3,2,1,0:T(8,128)(2,1)}), bf16[8,2,4,32,128]{4,3,2,1,0:T(8,128)(2,1)S(1)}, u32[]{:S(2)}, u32[]{:S(2)}) async-start(bf16[8,2,4,32,128]{4,3,2,1,0:T(8,128)(2,1)} %bitcast.22), calls=%async_computation.1 | async-start | bytes 1048576 | tf_op jit(solution)/shard_map/all_to_all | solution.py:333
  12.2 0.0 collective-permute-start.1
  12.2 11.4 %collective-permute-done.far = bf16[3,4,32,1024]{3,2,1,0:T(8,128)(2,1)} collective-permute-done((bf16[3,4,32,1024]{3,2,1,0:T(8,128)(2,1)S(1)}, bf16[3,4,32,1024]{3,2,1,0:T(8,128)(2,1)}, u32[]{:S(2)}, u32[]{:S(2)}) %collective-permute-start) | collective-permute-done | bytes 786464 | tf_op jit(solution)/shard_map/ppermute | solution.py:341
  23.6 0.0 collective-permute-start.2
  23.6 0.9 copy.14
  24.5 5.8 %all-to-all-done.1.refs_0_ = bf16[8,2,4,32,128]{4,3,2,1,0:T(8,128)(2,1)S(1)} async-done(((bf16[8,2,4,32,128]{4,3,2,1,0:T(8,128)(2,1)}), bf16[8,2,4,32,128]{4,3,2,1,0:T(8,128)(2,1)S(1)}, u32[]{:S(2)}, u32[]{:S(2)}) %all-to-all-start.1) | async-done | bytes 524320 | tf_op jit(solution)/shard_map/all_to_all | solution.py:333
  30.3 4.8 %all-to-all-start.2 = ((bf16[8,2,4,32,128]{4,3,2,1,0:T(8,128)(2,1)}), bf16[8,2,4,32,128]{4,3,2,1,0:T(8,128)(2,1)S(1)}, u32[]{:S(2)}, u32[]{:S(2)}) async-start(bf16[8,2,4,32,128]{4,3,2,1,0:T(8,128)(2,1)} %bitcast.21), calls=%async_computation.2 | async-start | bytes 1048576 | tf_op jit(solution)/shard_map/all_to_all | solution.py:333
  35.2 1.9 %collective-permute-start.5 = (bf16[8,2,4,32,128]{4,3,2,1,0:T(8,128)(2,1)S(1)}, bf16[8,2,4,32,128]{4,3,2,1,0:T(8,128)(2,1)S(1)}, u32[]{:S(2)}, u32[]{:S(2)}) collective-permute-start(bf16[8,2,4,32,128]{4,3,2,1,0:T(8,128)(2,1)S(1)} %all-to-all-done.1.refs_0_), channel_id=1, source_target_pairs={{0,32},{32,64},{64,96},{96,128},{128,160},{160,192},{192,224},{224... | collective-permute-start | bytes 1572872 | tf_op jit(solution)/shard_map/ppermute | solution.py:335
  37.1 7.2 %all-to-all-done.2.refs_1_ = bf16[8,2,4,32,128]{4,3,2,1,0:T(8,128)(2,1)S(1)} async-done(((bf16[8,2,4,32,128]{4,3,2,1,0:T(8,128)(2,1)}), bf16[8,2,4,32,128]{4,3,2,1,0:T(8,128)(2,1)S(1)}, u32[]{:S(2)}, u32[]{:S(2)}) %all-to-all-start.2) | async-done | bytes 524320 | tf_op jit(solution)/shard_map/all_to_all | solution.py:333
  44.3 1.9 %collective-permute-start.6 = (bf16[8,2,4,32,128]{4,3,2,1,0:T(8,128)(2,1)S(1)}, bf16[8,2,4,32,128]{4,3,2,1,0:T(8,128)(2,1)S(1)}, u32[]{:S(2)}, u32[]{:S(2)}) collective-permute-start(bf16[8,2,4,32,128]{4,3,2,1,0:T(8,128)(2,1)S(1)} %all-to-all-done.2.refs_1_), channel_id=1, source_target_pairs={{0,32},{32,64},{64,96},{96,128},{128,160},{160,192},{192,224},{224... | collective-permute-start | bytes 1572872 | tf_op jit(solution)/shard_map/ppermute | solution.py:335
  46.2 0.0 collective-permute-done.1.mate_own
  46.2 0.0 collective-permute-done.2.mate_far
  46.2 0.0 collective-permute-done.3.after.wo_mate
  46.2 3.4 %spatial.1 = bf16[2,4,32,1024]{3,2,1,0:T(8,128)(2,1)S(1)} custom-call(bf16[3,4,32,1024]{3,2,1,0:T(8,128)(2,1)S(1)} %get-tuple-element.6.own, bf16[3,4,32,1024]{3,2,1,0:T(8,128)(2,1)} %collective-permute-done.far, bf16[3,4,32,1024]{3,2,1,0:T(8,128)(2,1)} %collective-permute-done.1.mate_own, bf16[3,4,32,1024]{3,2,1,0:T(8,128)(2,1)} %collective-permute-done.2.mate_far, ...), custom_call_target="tpu_custom_call" | custom-call | flops 1024 | bytes 1024 | tf_op jit(solution)/shard_map/spatial/pallas_call | solution.py:84
  49.6 0.0 copy-start
  49.6 0.0 copy-start.2
  49.6 1.5 %collective-permute-start.4 = (bf16[2,128,1024]{2,1,0:T(8,128)(2,1)S(1)}, bf16[2,128,1024]{2,1,0:T(8,128)(2,1)}, u32[]{:S(2)}, u32[]{:S(2)}) collective-permute-start(bf16[2,128,1024]{2,1,0:T(8,128)(2,1)S(1)} %bitcast.26), channel_id=1, source_target_pairs={{0,2},{2,0},{1,3},{3,1},{4,6},{6,4},{5,7},{7,5},{8,10},{10,8},{9,1... | collective-permute-start | bytes 1572872 | tf_op jit(solution)/shard_map/ppermute | solution.py:346
  51.1 1.1 slice.19
  52.2 0.9 copy.16
  53.1 5.2 %all-to-all-start = ((bf16[8,2,4,32,128]{4,3,2,1,0:T(8,128)(2,1)}), bf16[8,2,4,32,128]{4,3,2,1,0:T(8,128)(2,1)S(1)}, u32[]{:S(2)}, u32[]{:S(2)}) async-start(bf16[8,2,4,32,128]{4,3,2,1,0:T(8,128)(2,1)} %bitcast.29), calls=%async_computation | async-start | bytes 1048576 | tf_op jit(solution)/shard_map/all_to_all | solution.py:349
  58.3 0.0 collective-permute-done.5.refs_2_
  58.3 2.0 %collective-permute-start.7 = (bf16[2,2,4,32,128]{4,3,2,1,0:T(8,128)(2,1)S(1)}, bf16[2,2,4,32,128]{4,3,2,1,0:T(8,128)(2,1)S(1)}, u32[]{:S(2)}, u32[]{:S(2)}) collective-permute-start(bf16[2,2,4,32,128]{4,3,2,1,0:T(8,128)(2,1)S(1)} %slice.27), channel_id=1, source_target_pairs={{0,32},{32,64},{64,96},{96,128},{128,160},{160,192},{192,224},{224... | collective-permute-start | bytes 393224 | tf_op jit(solution)/shard_map/ppermute | solution.py:336
  60.3 4.8 %collective-permute-done.6.refs_3_ = bf16[8,2,4,32,128]{4,3,2,1,0:T(8,128)(2,1)S(1)} collective-permute-done((bf16[8,2,4,32,128]{4,3,2,1,0:T(8,128)(2,1)S(1)}, bf16[8,2,4,32,128]{4,3,2,1,0:T(8,128)(2,1)S(1)}, u32[]{:S(2)}, u32[]{:S(2)}) %collective-permute-start.6) | collective-permute-done | bytes 524320 | tf_op jit(solution)/shard_map/ppermute | solution.py:335
  65.1 0.7 slice.28
  65.7 0.0 collective-permute-start.8
  65.7 0.1 pad_add_fusion.place
  65.8 3.0 %all-to-all-done.queries = bf16[8,2,4,32,128]{4,3,2,1,0:T(8,128)(2,1)S(1)} async-done(((bf16[8,2,4,32,128]{4,3,2,1,0:T(8,128)(2,1)}), bf16[8,2,4,32,128]{4,3,2,1,0:T(8,128)(2,1)S(1)}, u32[]{:S(2)}, u32[]{:S(2)}) %all-to-all-start) | async-done | bytes 524320 | tf_op jit(solution)/shard_map/all_to_all | solution.py:349
  68.8 0.0 copy-done.2
  68.8 2.8 %temporal_late.1.refs_6_ = bf16[8,2,128,256]{3,2,1,0:T(8,128)(2,1)} custom-call(s32[3]{0:T(128)S(1)} %pad_add_fusion.place, s32[16]{0:T(128)S(1)} %copy-done.2, bf16[8,2,4,32,128]{4,3,2,1,0:T(8,128)(2,1)S(1)} %all-to-all-done.queries, bf16[8,2,4,32,128]{4,3,2,1,0:T(8,128)(2,1)S(1)} %all-to-all-done.1.refs_0_, ...), custom_call_target="tpu_custom_call" | custom-call | flops 1024 | bytes 1024 | tf_op jit(solution)/shard_map/temporal_late/pallas_call | solution.py:149
  71.7 0.0 copy-done
  71.7 0.0 collective-permute-done.7.refs_4_
  71.7 0.4 collective-permute-done.8.refs_5_
  72.1 0.0 collective-permute-done.4.far.refs_7_
  72.1 3.5 %temporal_early.1 = bf16[8,2,128,256]{3,2,1,0:T(8,128)(2,1)} custom-call(s32[3]{0:T(128)S(1)} %pad_add_fusion.place, s32[16]{0:T(128)S(1)} %copy-done.2, bf16[8,2,4,32,128]{4,3,2,1,0:T(8,128)(2,1)S(1)} %all-to-all-done.queries, bf16[8,2,4,32,128]{4,3,2,1,0:T(8,128)(2,1)S(1)} %all-to-all-done.1.refs_0_, ...), custom_call_target="tpu_custom_call", output_to_operand_aliasing={{}: (9, {})} | custom-call | flops 1024 | bytes 1024 | tf_op jit(solution)/shard_map/temporal_early/pallas_call | solution.py:177
  75.6 6.3 %all-to-all-start.3 = ((bf16[16,128,256]{2,1,0:T(8,128)(2,1)}), bf16[16,128,256]{2,1,0:T(8,128)(2,1)S(1)}, u32[]{:S(2)}, u32[]{:S(2)}) async-start(bf16[16,128,256]{2,1,0:T(8,128)(2,1)} %bitcast.12), calls=%async_computation.3 | async-start | bytes 2097152 | tf_op jit(solution)/shard_map/all_to_all | solution.py:353
  81.9 0.0 copy-start.1
  81.9 1.0 copy-done.1
  83.0 5.4 %project_first.1.partial = f32[2,2,128,1024]{3,2,1,0:T(8,128)S(1)} custom-call(s32[3]{0:T(128)S(1)} %pad_add_fusion.place, bf16[2,128,1024]{2,1,0:T(8,128)(2,1)S(1)} %bitcast.27, bf16[2,128,1024]{2,1,0:T(8,128)(2,1)} %collective-permute-done.4.far.refs_7_, bf16[4096,1024]{1,0:T(8,128)(2,1)} %wo.5, bf16[4096,1024]{1,0:T(8,128)(2,1)} %collective-permute-done.3.after.wo_mate), custom_call_target="tpu_custom_call" | custom-call | flops 1024 | bytes 1024 | tf_op jit(solution)/shard_map/project_first/pallas_call | solution.py:225
  88.3 5.3 %all-to-all-done.3 = bf16[16,128,256]{2,1,0:T(8,128)(2,1)S(1)} async-done(((bf16[16,128,256]{2,1,0:T(8,128)(2,1)}), bf16[16,128,256]{2,1,0:T(8,128)(2,1)S(1)}, u32[]{:S(2)}, u32[]{:S(2)}) %all-to-all-start.3) | async-done | bytes 1048608 | tf_op jit(solution)/shard_map/all_to_all | solution.py:353
  93.6 4.4 %project_next.1 = bf16[128,2048]{1,0:T(8,128)(2,1)S(1)} custom-call(s32[3]{0:T(128)S(1)} %pad_add_fusion.place, f32[2,2,128,1024]{3,2,1,0:T(8,128)S(1)} %project_first.1.partial, bf16[8,2,128,256]{3,2,1,0:T(8,128)(2,1)S(1)} %bitcast.24, bf16[4096,1024]{1,0:T(8,128)(2,1)} %wo.5, bf16[4096,1024]{1,0:T(8,128)(2,1)} %collective-permute-done.3.after.wo_mate), custom_call_target="tpu_custom_call" | custom-call | flops 1024 | bytes 1024 | tf_op jit(solution)/shard_map/project_next/pallas_call | solution.py:257
  98.0 2.1 %collective-permute-start.9 = (bf16[128,2048]{1,0:T(8,128)(2,1)S(1)}, bf16[128,2048]{1,0:T(8,128)(2,1)S(1)}, u32[]{:S(2)}, u32[]{:S(2)}) collective-permute-start(bf16[128,2048]{1,0:T(8,128)(2,1)S(1)} %project_next.1), channel_id=1, source_target_pairs={{0,2},{2,0},{1,3},{3,1},{4,6},{6,4},{5,7},{7,5},{8,10},{10,8},{9,1... | collective-permute-start | bytes 1572872 | tf_op jit(solution)/shard_map/ppermute | solution.py:357
  100.1 5.3 %project_own.1.mixed = bf16[128,4096]{1,0:T(8,128)(2,1)} custom-call(s32[3]{0:T(128)S(1)} %pad_add_fusion.place, f32[2,2,128,1024]{3,2,1,0:T(8,128)S(1)} %project_first.1.partial, bf16[8,2,128,256]{3,2,1,0:T(8,128)(2,1)S(1)} %bitcast.25, bf16[4096,1024]{1,0:T(8,128)(2,1)} %wo.5, bf16[4096,1024]{1,0:T(8,128)(2,1)} %collective-permute-done.3.after.wo_mate), custom_call_target="tpu_custom_call" | custom-call | flops 1024 | bytes 1024 | tf_op jit(solution)/shard_map/project_own/pallas_call | solution.py:257
  105.4 5.4 %collective-permute-done.9.arrived = bf16[128,2048]{1,0:T(8,128)(2,1)S(1)} collective-permute-done((bf16[128,2048]{1,0:T(8,128)(2,1)S(1)}, bf16[128,2048]{1,0:T(8,128)(2,1)S(1)}, u32[]{:S(2)}, u32[]{:S(2)}) %collective-permute-start.9) | collective-permute-done | bytes 524320 | tf_op jit(solution)/shard_map/ppermute | solution.py:357
  110.9 1.4 %put_arrived.1 = bf16[128,4096]{1,0:T(8,128)(2,1)} custom-call(s32[3]{0:T(128)S(1)} %pad_add_fusion.place, bf16[128,4096]{1,0:T(8,128)(2,1)} %project_own.1.mixed, bf16[128,2048]{1,0:T(8,128)(2,1)S(1)} %collective-permute-done.9.arrived), custom_call_target="tpu_custom_call", output_to_operand_aliasing={{}: (1, {})} | custom-call | flops 1024 | bytes 1024 | tf_op jit(solution)/shard_map/put_arrived/pallas_call | solution.py:298
  (1 shorter events, 0.0 us)
Async XLA Ops:
  0.0 46.2 %collective-permute-start.3 = (bf16[4096,1024]{1,0:T(8,128)(2,1)}, bf16[4096,1024]{1,0:T(8,128)(2,1)}, u32[]{:S(2)}, u32[]{:S(2)}) collective-permute-start(bf16[4096,1024]{1,0:T(8,128)(2,1)} %wo.5), channel_id=1, source_target_pairs={{0,1},{1,0},{2,3},{3,2},{4,5},{5,4},{6,7},{7,6},{8,9},{9,8},{10,11... | collective-permute-start | bytes 25165832 | tf_op jit(solution)/shard_map/ppermute | solution.py:339
  1.5 22.0 %collective-permute-start = (bf16[3,4,32,1024]{3,2,1,0:T(8,128)(2,1)S(1)}, bf16[3,4,32,1024]{3,2,1,0:T(8,128)(2,1)}, u32[]{:S(2)}, u32[]{:S(2)}) collective-permute-start(bf16[3,4,32,1024]{3,2,1,0:T(8,128)(2,1)S(1)} %get-tuple-element.5), channel_id=1, source_target_pairs={{0,2},{2,0},{1,3},{3,1},{4,6},{6,4},{5,7},{7,5},{8,10},{10,8},{9,1... | collective-permute-start | bytes 2359304 | tf_op jit(solution)/shard_map/ppermute | solution.py:341
  6.3 24.1 %all-to-all-start.1 = ((bf16[8,2,4,32,128]{4,3,2,1,0:T(8,128)(2,1)}), bf16[8,2,4,32,128]{4,3,2,1,0:T(8,128)(2,1)S(1)}, u32[]{:S(2)}, u32[]{:S(2)}) async-start(bf16[8,2,4,32,128]{4,3,2,1,0:T(8,128)(2,1)} %bitcast.22), calls=%async_computation.1 | async-start | bytes 1048576 | tf_op jit(solution)/shard_map/all_to_all | solution.py:333
  12.2 34.0 %collective-permute-start.1 = (bf16[3,4,32,1024]{3,2,1,0:T(8,128)(2,1)S(1)}, bf16[3,4,32,1024]{3,2,1,0:T(8,128)(2,1)}, u32[]{:S(2)}, u32[]{:S(2)}) collective-permute-start(bf16[3,4,32,1024]{3,2,1,0:T(8,128)(2,1)S(1)} %get-tuple-element.6.own), channel_id=1, source_target_pairs={{0,1},{1,0},{2,3},{3,2},{4,5},{5,4},{6,7},{7,6},{8,9},{9,8},{10,11... | collective-permute-start | bytes 2359304 | tf_op jit(solution)/shard_map/ppermute | solution.py:342
  23.6 22.6 %collective-permute-start.2 = (bf16[3,4,32,1024]{3,2,1,0:T(8,128)(2,1)}, bf16[3,4,32,1024]{3,2,1,0:T(8,128)(2,1)}, u32[]{:S(2)}, u32[]{:S(2)}) collective-permute-start(bf16[3,4,32,1024]{3,2,1,0:T(8,128)(2,1)} %collective-permute-done.far), channel_id=1, source_target_pairs={{0,1},{1,0},{2,3},{3,2},{4,5},{5,4},{6,7},{7,6},{8,9},{9,8},{10,11... | collective-permute-start | bytes 2359304 | tf_op jit(solution)/shard_map/ppermute | solution.py:343
  30.3 13.9 %all-to-all-start.2 = ((bf16[8,2,4,32,128]{4,3,2,1,0:T(8,128)(2,1)}), bf16[8,2,4,32,128]{4,3,2,1,0:T(8,128)(2,1)S(1)}, u32[]{:S(2)}, u32[]{:S(2)}) async-start(bf16[8,2,4,32,128]{4,3,2,1,0:T(8,128)(2,1)} %bitcast.21), calls=%async_computation.2 | async-start | bytes 1048576 | tf_op jit(solution)/shard_map/all_to_all | solution.py:333
  35.2 23.1 %collective-permute-start.5 = (bf16[8,2,4,32,128]{4,3,2,1,0:T(8,128)(2,1)S(1)}, bf16[8,2,4,32,128]{4,3,2,1,0:T(8,128)(2,1)S(1)}, u32[]{:S(2)}, u32[]{:S(2)}) collective-permute-start(bf16[8,2,4,32,128]{4,3,2,1,0:T(8,128)(2,1)S(1)} %all-to-all-done.1.refs_0_), channel_id=1, source_target_pairs={{0,32},{32,64},{64,96},{96,128},{128,160},{160,192},{192,224},{224... | collective-permute-start | bytes 1572872 | tf_op jit(solution)/shard_map/ppermute | solution.py:335
  44.3 20.8 %collective-permute-start.6 = (bf16[8,2,4,32,128]{4,3,2,1,0:T(8,128)(2,1)S(1)}, bf16[8,2,4,32,128]{4,3,2,1,0:T(8,128)(2,1)S(1)}, u32[]{:S(2)}, u32[]{:S(2)}) collective-permute-start(bf16[8,2,4,32,128]{4,3,2,1,0:T(8,128)(2,1)S(1)} %all-to-all-done.2.refs_1_), channel_id=1, source_target_pairs={{0,32},{32,64},{64,96},{96,128},{128,160},{160,192},{192,224},{224... | collective-permute-start | bytes 1572872 | tf_op jit(solution)/shard_map/ppermute | solution.py:335
  49.6 22.1 %copy-start = (bf16[2,4,32,1024]{3,2,1,0:T(8,128)(2,1)}, bf16[2,4,32,1024]{3,2,1,0:T(8,128)(2,1)S(1)}, u32[]{:S(2)}) copy-start(bf16[2,4,32,1024]{3,2,1,0:T(8,128)(2,1)S(1)} %spatial.1) | copy-start | bytes 1572868
  49.6 19.3 %copy-start.2 = (s32[16]{0:T(128)S(1)}, s32[16]{0:T(128)}, u32[]{:S(2)}) copy-start(s32[16]{0:T(128)} %lengths.3) | copy-start | bytes 196
  49.6 22.5 %collective-permute-start.4 = (bf16[2,128,1024]{2,1,0:T(8,128)(2,1)S(1)}, bf16[2,128,1024]{2,1,0:T(8,128)(2,1)}, u32[]{:S(2)}, u32[]{:S(2)}) collective-permute-start(bf16[2,128,1024]{2,1,0:T(8,128)(2,1)S(1)} %bitcast.26), channel_id=1, source_target_pairs={{0,2},{2,0},{1,3},{3,1},{4,6},{6,4},{5,7},{7,5},{8,10},{10,8},{9,1... | collective-permute-start | bytes 1572872 | tf_op jit(solution)/shard_map/ppermute | solution.py:346
  53.1 15.7 %all-to-all-start = ((bf16[8,2,4,32,128]{4,3,2,1,0:T(8,128)(2,1)}), bf16[8,2,4,32,128]{4,3,2,1,0:T(8,128)(2,1)S(1)}, u32[]{:S(2)}, u32[]{:S(2)}) async-start(bf16[8,2,4,32,128]{4,3,2,1,0:T(8,128)(2,1)} %bitcast.29), calls=%async_computation | async-start | bytes 1048576 | tf_op jit(solution)/shard_map/all_to_all | solution.py:349
  58.3 13.4 %collective-permute-start.7 = (bf16[2,2,4,32,128]{4,3,2,1,0:T(8,128)(2,1)S(1)}, bf16[2,2,4,32,128]{4,3,2,1,0:T(8,128)(2,1)S(1)}, u32[]{:S(2)}, u32[]{:S(2)}) collective-permute-start(bf16[2,2,4,32,128]{4,3,2,1,0:T(8,128)(2,1)S(1)} %slice.27), channel_id=1, source_target_pairs={{0,32},{32,64},{64,96},{96,128},{128,160},{160,192},{192,224},{224... | collective-permute-start | bytes 393224 | tf_op jit(solution)/shard_map/ppermute | solution.py:336
  65.7 6.4 %collective-permute-start.8 = (bf16[2,2,4,32,128]{4,3,2,1,0:T(8,128)(2,1)}, bf16[2,2,4,32,128]{4,3,2,1,0:T(8,128)(2,1)S(1)}, u32[]{:S(2)}, u32[]{:S(2)}) collective-permute-start(bf16[2,2,4,32,128]{4,3,2,1,0:T(8,128)(2,1)} %slice.28), channel_id=1, source_target_pairs={{0,32},{32,64},{64,96},{96,128},{128,160},{160,192},{192,224},{224... | collective-permute-start | bytes 393224 | tf_op jit(solution)/shard_map/ppermute | solution.py:336
  75.6 18.0 %all-to-all-start.3 = ((bf16[16,128,256]{2,1,0:T(8,128)(2,1)}), bf16[16,128,256]{2,1,0:T(8,128)(2,1)S(1)}, u32[]{:S(2)}, u32[]{:S(2)}) async-start(bf16[16,128,256]{2,1,0:T(8,128)(2,1)} %bitcast.12), calls=%async_computation.3 | async-start | bytes 2097152 | tf_op jit(solution)/shard_map/all_to_all | solution.py:353
  81.9 1.0 copy-start.1
  98.0 12.9 %collective-permute-start.9 = (bf16[128,2048]{1,0:T(8,128)(2,1)S(1)}, bf16[128,2048]{1,0:T(8,128)(2,1)S(1)}, u32[]{:S(2)}, u32[]{:S(2)}) collective-permute-start(bf16[128,2048]{1,0:T(8,128)(2,1)S(1)} %project_next.1), channel_id=1, source_target_pairs={{0,2},{2,0},{1,3},{3,1},{4,6},{6,4},{5,7},{7,5},{8,10},{10,8},{9,1... | collective-permute-start | bytes 1572872 | tf_op jit(solution)/shard_map/ppermute | solution.py:357

commit v4 on v3

--- a/solution.py
+++ b/solution.py
@@ -21,6 +21,7 @@
 WHOLE = pl.BlockSpec(memory_space=pltpu.VMEM)
 ANYWHERE = pl.BlockSpec(memory_space=pl.ANY)
 IN_HBM = pl.BlockSpec(memory_space=pltpu.HBM)
+PACK_VMEM = 60
 LAST_VMEM = 44
 QUICK = pl.CostEstimate(flops=1024, bytes_accessed=1024, transcendentals=0)
 
@@ -54,6 +55,36 @@
     both = jnp.concatenate([values, jnp.ones_like(values)], axis=1)
     result = jnp.dot(raised, both, preferred_element_type=F32)
     return result[:, :HS] / result[:, HS:]
+
+
+def pack_rest(qkv):
+    _, frames, tok, model_width = qkv.shape
+    half = model_width // 2
+    groups = tok // GROUP
+    step = 2
+
+    def body(qkv, queries, keyvals):
+        for device in range(PLANE):
+            for slot in range(ROUNDS + 2):
+                which, turn = (0, slot) if slot < ROUNDS else (slot - ROUNDS + 1, ROUNDS - 1)
+                target, place = (queries, slot) if slot < ROUNDS else (keyvals, slot - ROUNDS)
+                first = (device * ROUNDS + turn) * HS
+                block = qkv[which, :, :, first : first + HS].astype(F32).reshape(step, groups, GROUP, HS)
+                for group in range(groups):
+                    target[device, place, group] = block[:, group].reshape(step * GROUP, HS).astype(BF16)
+
+    rows = jax.ShapeDtypeStruct((PLANE, 2, groups, frames * GROUP, HS), BF16)
+    rows_spec = pl.BlockSpec((PLANE, 2, groups, step * GROUP, HS), lambda f: (0, 0, 0, f, 0))
+    return pl.pallas_call(
+        body,
+        grid=(frames // step,),
+        in_specs=[pl.BlockSpec((3, step, tok, half), lambda f: (0, f, 0, 1))],
+        out_specs=[rows_spec] * 2,
+        out_shape=[rows] * 2,
+        compiler_params=kernel_params(PACK_VMEM),
+        cost_estimate=QUICK,
+        name="pack_rest",
+    )(qkv)
 
 
 def spatial_attend(own, far, mate_own, mate_far, after):
@@ -92,7 +123,7 @@
     )(own, far, mate_own, mate_far, after)
 
 
-def temporal_scores(clips, place, lengths, queries, keyvals, first_query, first_key, bias, store):
+def temporal_scores(clips, place, lengths, queries, keyvals, first_query, first_key, bias, batch, store):
     _, _, groups, rows, _ = queries.shape
     frames_dev = rows // GROUP
     query_rows, key_count = bias.shape
@@ -114,18 +145,27 @@
     bias[...] = jnp.where((code >= low) & (code <= high), 0.0, -1e30)
 
     blocks = slice(first_query, first_query + query_rows // rows)
-    for turn in range(ROUNDS):
-        pieces = []
-        for group in range(groups):
-            def rows_of(which):
-                return jnp.concatenate([part[:, which, group].reshape(-1, HS) for part in keyvals[turn]], axis=0)
-
-            asked = queries[blocks, turn, group].reshape(-1, HS)
-            scores = lax.dot_general(asked, rows_of(0), (((1,), (1,)), ((), ())), preferred_element_type=F32)
-            result = weighted(softmax_parts(scores + bias[...]), rows_of(1))
-            pieces.append(result.reshape(-1, 1, GROUP, HS))
-        joined = jnp.concatenate(pieces, axis=1).reshape(-1, frames_dev * groups * GROUP, HS).astype(BF16)
-        store(turn, joined)
+    def rows_of(which, turn, group):
+        return jnp.concatenate([part[:, which, group].reshape(-1, HS) for part in keyvals[turn]], axis=0)
+
+    units = [(turn, group) for turn in range(ROUNDS) for group in range(groups)]
+    for first_unit in range(0, len(units), batch):
+        some = units[first_unit : first_unit + batch]
+        scores = [
+            lax.dot_general(
+                queries[blocks, turn, group].reshape(-1, HS),
+                rows_of(0, turn, group),
+                (((1,), (1,)), ((), ())),
+                preferred_element_type=F32,
+            )
+            for turn, group in some
+        ]
+        raised = [softmax_parts(block + bias[...]) for block in scores]
+        results = [weighted(block, rows_of(1, turn, group)) for block, (turn, group) in zip(raised, some)]
+        for at in range(0, len(some), groups):
+            pieces = [result.reshape(-1, 1, GROUP, HS) for result in results[at : at + groups]]
+            joined = jnp.concatenate(pieces, axis=1).reshape(-1, frames_dev * groups * GROUP, HS).astype(BF16)
+            store(some[at][0], joined)
 
 
 EARLY = 2
@@ -144,7 +184,7 @@
                 out[EARLY:, copy, :, turn * HS : (turn + 1) * HS] = joined
 
         keyvals = [(before[turn], own[turn]) for turn in range(ROUNDS)]
-        temporal_scores(clips, place, lengths, queries, keyvals, EARLY, -sources, bias, store)
+        temporal_scores(clips, place, lengths, queries, keyvals, EARLY, -sources, bias, groups, store)
 
     return pl.pallas_call(
         body,
@@ -171,7 +211,7 @@
                 out[:, copy, :, turn * HS : (turn + 1) * HS] = joined
 
         keyvals = [(before2[turn], before[turn], own[turn].at[:EARLY]) for turn in range(ROUNDS)]
-        temporal_scores(clips, place, lengths, queries, keyvals, 0, -sources - EARLY, bias, store)
+        temporal_scores(clips, place, lengths, queries, keyvals, 0, -sources - EARLY, bias, ROUNDS * groups, store)
 
     block = (EARLY,) + late.shape[1:]
     return pl.pallas_call(
@@ -321,19 +361,15 @@
     groups = tok // GROUP
     rows = frames * GROUP
 
-    def by_plane(block, turn=None):
-        split = block.reshape(block.shape[0], frames, groups, GROUP, PLANE, ROUNDS, HS)
-        if turn is not None:
-            split = split[:, :, :, :, :, turn : turn + 1]
-        return split.transpose(4, 0, 5, 2, 1, 3, 6).reshape(PLANE, -1, groups, rows, HS)
+    def by_plane(block, turn):
+        split = block.reshape(block.shape[0], frames, groups, GROUP, PLANE, ROUNDS, HS)[:, :, :, :, :, turn]
+        return split.transpose(4, 0, 2, 1, 3, 5).reshape(PLANE, -1, groups, rows, HS)
 
     onward = [(i, (i + 1) % Z) for i in range(Z)]
-    keyvals, before, before2 = [], [], []
-    for turn in range(ROUNDS):
-        got = lax.all_to_all(by_plane(qkv[1:, :, :, half:], turn), ("y", "xl"), 0, 0, tiled=True)
-        keyvals.append(got)
-        before.append(lax.ppermute(got, "z", onward))
-        before2.append(lax.ppermute(before[-1][PLANE - EARLY :], "z", onward))
+    queries, last_packed = pack_rest(qkv)
+    packed = (by_plane(qkv[1:, :, :, half:], 0), last_packed)
+    arrived = [lax.all_to_all(block, ("y", "xl"), 0, 0, tiled=True) for block in packed]
+
     own_cols = x_place * quarter
     far_cols = (1 - x_place) * quarter
     wo_mate = lax.ppermute(wo, "c", SWAP)
@@ -345,7 +381,14 @@
     near = near.reshape(2, frames * tok, quarter)
     far = lax.ppermute(near, "xh", SWAP)
 
-    queries = by_plane(qkv[:1, :, :, half:])
+    keyvals, before, before2 = [], [], []
+    for turn, got in enumerate(arrived):
+        if turn:
+            got = behind(got, near)
+        keyvals.append(got)
+        before.append(lax.ppermute(got, "z", onward))
+        before2.append(lax.ppermute(before[-1][PLANE - EARLY :], "z", onward))
+
     queries = lax.all_to_all(queries, ("y", "xl"), 0, 0, tiled=True)
     mine = temporal_late(place, clip_lengths, queries, keyvals, before)
     mine = temporal_early(place, clip_lengths, queries, keyvals, before, before2, mine, far)

time: 114 us -> 111 us (0.974)
  local copies, waits for them, and re-layouts: 8.72 us -> 5.47 us
  waiting for transfers between devices: 43.3 us -> 44.8 us
    ppermute x2, waiting for transfers between devices: 4.78 us -> 11.3 us  [on_device(): before.append(lax.ppermute(got, 'z', onward))]
    all_to_all x2, waiting for transfers between devices: 13 us -> 8.26 us  [on_device(): lax.all_to_all(block, ('y', 'xl'), 0, 0, tiled=True)]
    all_to_all x1, waiting for transfers between devices: 3.03 us -> 0.01 us  [on_device(): queries = lax.all_to_all(queries, ('y', 'xl'), 0, 0, tiled=True)]
    ppermute x2, waiting for transfers between devices: 0.44 us -> 3.41 us  [on_device(): before2.append(lax.ppermute(before[-1][PLANE - EARLY:], 'z', onward))]
    pallas_call x0 -> x2, Pallas kernels: none -> 2.31 us  [the longest x1 2.31 us: pack_rest(): pl.pallas_call(body, grid=(frames // step,), in_specs=[pl.BlockSpec((3, s...]
    unnamed x8 -> x6, local copies, waits for them, and re-layouts: 2.91 us -> 1.05 us
    pallas_call x1, Pallas kernels: 3.48 us -> 2.02 us  [temporal_early(): pl.pallas_call(body, grid=(1,), in_specs=[SMEM, SMEM] + [WHOLE] * (1 + 3...]
    slice x3 -> x1, local copies, waits for them, and re-layouts: 2.66 us -> 1.29 us  [on_device(): packed = (by_plane(qkv[1:, :, :, half:], 0), last_packed)]
  transfers between devices with their start and end apart: 14 -> 14, of which waited for: 8 -> 8; matrix products, arithmetic and copies ran while one was open for 7% -> 4% of each run, Pallas kernels for 15% -> 17%
where the time goes in v4:
time: 111 us; the launch traced here: 110 us
  waiting for transfers between devices  44.8 us (40%)
  starting transfers between devices  32.8 us (30%)
  Pallas kernels  27 us (24%)
  local copies, waits for them, and re-layouts  5.47 us (5%)
    ppermute x1, waiting for transfers between devices, on_device(): lax.ppermute(lax.dynamic_slice(qkv, (0, 0, 0, far_cols), (3, frames, tok,...  11.7 us
    ppermute x2, waiting for transfers between devices, on_device(): before.append(lax.ppermute(got, 'z', onward))  11.3 us
    all_to_all x2, starting transfers between devices, on_device(): lax.all_to_all(block, ('y', 'xl'), 0, 0, tiled=True)  10.8 us
    pallas_call x2, Pallas kernels, project_last(): pl.pallas_call(body, in_specs=[SMEM] + [WHOLE] * 2 + [IN_HBM] * 2, out_sp...  9.68 us
    all_to_all x2, waiting for transfers between devices, on_device(): lax.all_to_all(block, ('y', 'xl'), 0, 0, tiled=True)  8.26 us
    all_to_all x1, starting transfers between devices, on_device(): lax.all_to_all(sent, ('y', 'xl', 'xh'), 0, 0, tiled=True)  6.29 us
    ppermute x1, waiting for transfers between devices, on_device(): arrived = lax.ppermute(for_next, 'xh', SWAP)  5.44 us
    pallas_call x1, Pallas kernels, project_first(): pl.pallas_call(body, in_specs=[SMEM] + [WHOLE] * 2 + [IN_HBM] * 2, out_sp...  5.37 us
  transfers between devices with their start and end apart: 14, of which 8 were waited for; matrix products, arithmetic and copies ran while one was open for 4% of the time, Pallas kernels for 17%

profile of v4, /device:TPU:2, one launch (start us, length us, event | category | flops | bytes accessed | tf_op | source)
XLA Modules:
  0.0 110.3 jit_solution(13874750341267581373)
XLA Ops:
  0.0 0.0 collective-permute-start.3
  0.0 1.5 %constant_dynamic-slice_fusion = (bf16[3,4,32,1024]{3,2,1,0:T(8,128)(2,1)S(1)}, bf16[3,4,32,1024]{3,2,1,0:T(8,128)(2,1)S(1)}) fusion(bf16[3,4,32,4096]{3,2,1,0:T(8,128)(2,1)} %qkv.1, s32[]{:T(128)S(6)} %select_n.7, s32[]{:T(128)S(6)} %select_n.6), kind=kLoop, calls=%fused_computation.2 | loop fusion | bytes 3145736 | tf_op jit(solution)/shard_map/dynamic_slice | solution.py:377
  1.5 2.2 %collective-permute-start = (bf16[3,4,32,1024]{3,2,1,0:T(8,128)(2,1)S(1)}, bf16[3,4,32,1024]{3,2,1,0:T(8,128)(2,1)}, u32[]{:S(2)}, u32[]{:S(2)}) collective-permute-start(bf16[3,4,32,1024]{3,2,1,0:T(8,128)(2,1)S(1)} %get-tuple-element.9), channel_id=1, source_target_pairs={{0,2},{2,0},{1,3},{3,1},{4,6},{6,4},{5,7},{7,5},{8,10},{10,8},{9,1... | collective-permute-start | bytes 2359304 | tf_op jit(solution)/shard_map/ppermute | solution.py:377
  3.8 1.3 %slice.12 = bf16[2,4,32,2048]{3,2,1,0:T(8,128)(2,1)S(1)} slice(bf16[3,4,32,4096]{3,2,1,0:T(8,128)(2,1)} %qkv.1), slice={[1:3], [0:4], [0:32], [2048:4096]} | slice | bytes 2097152 | tf_op jit(solution)/shard_map/slice | solution.py:370
  5.1 0.9 copy_bitcast_fusion
  6.0 5.9 %all-to-all-start.1 = ((bf16[8,2,4,32,128]{4,3,2,1,0:T(8,128)(2,1)}), bf16[8,2,4,32,128]{4,3,2,1,0:T(8,128)(2,1)S(1)}, u32[]{:S(2)}, u32[]{:S(2)}) async-start(bf16[8,2,4,32,128]{4,3,2,1,0:T(8,128)(2,1)} %copy_bitcast_fusion), calls=%async_computation.1 | async-start | bytes 1048576 | tf_op jit(solution)/shard_map/all_to_all | solution.py:371
  11.9 0.0 collective-permute-start.1
  11.9 11.7 %collective-permute-done.far = bf16[3,4,32,1024]{3,2,1,0:T(8,128)(2,1)} collective-permute-done((bf16[3,4,32,1024]{3,2,1,0:T(8,128)(2,1)S(1)}, bf16[3,4,32,1024]{3,2,1,0:T(8,128)(2,1)}, u32[]{:S(2)}, u32[]{:S(2)}) %collective-permute-start) | collective-permute-done | bytes 786464 | tf_op jit(solution)/shard_map/ppermute | solution.py:377
  23.6 0.0 collective-permute-start.2
  23.6 2.3 %pack_rest.1 = (bf16[8,2,4,32,128]{4,3,2,1,0:T(8,128)(2,1)}, bf16[8,2,4,32,128]{4,3,2,1,0:T(8,128)(2,1)}) custom-call(bf16[3,4,32,4096]{3,2,1,0:T(8,128)(2,1)} %qkv.1), custom_call_target="tpu_custom_call" | custom-call | flops 1024 | bytes 1024 | tf_op jit(solution)/shard_map/pack_rest/pallas_call | solution.py:78
  25.9 4.5 %all-to-all-done.1.refs_0_ = bf16[8,2,4,32,128]{4,3,2,1,0:T(8,128)(2,1)S(1)} async-done(((bf16[8,2,4,32,128]{4,3,2,1,0:T(8,128)(2,1)}), bf16[8,2,4,32,128]{4,3,2,1,0:T(8,128)(2,1)S(1)}, u32[]{:S(2)}, u32[]{:S(2)}) %all-to-all-start.1) | async-done | bytes 524320 | tf_op jit(solution)/shard_map/all_to_all | solution.py:371
  30.3 4.8 %all-to-all-start.2 = ((bf16[8,2,4,32,128]{4,3,2,1,0:T(8,128)(2,1)}), bf16[8,2,4,32,128]{4,3,2,1,0:T(8,128)(2,1)S(1)}, u32[]{:S(2)}, u32[]{:S(2)}) async-start(bf16[8,2,4,32,128]{4,3,2,1,0:T(8,128)(2,1)} %get-tuple-element.8), calls=%async_computation.2 | async-start | bytes 1048576 | tf_op jit(solution)/shard_map/all_to_all | solution.py:371
  35.2 1.9 %collective-permute-start.5 = (bf16[8,2,4,32,128]{4,3,2,1,0:T(8,128)(2,1)S(1)}, bf16[8,2,4,32,128]{4,3,2,1,0:T(8,128)(2,1)S(1)}, u32[]{:S(2)}, u32[]{:S(2)}) collective-permute-start(bf16[8,2,4,32,128]{4,3,2,1,0:T(8,128)(2,1)S(1)} %all-to-all-done.1.refs_0_), channel_id=1, source_target_pairs={{0,32},{32,64},{64,96},{96,128},{128,160},{160,192},{192,224},{224... | collective-permute-start | bytes 1572872 | tf_op jit(solution)/shard_map/ppermute | solution.py:389
  37.1 0.0 collective-permute-done.1.mate_own
  37.1 0.0 collective-permute-done.2.mate_far
  37.1 0.0 collective-permute-done.3.after.wo_mate
  37.1 3.3 %spatial.1 = bf16[2,4,32,1024]{3,2,1,0:T(8,128)(2,1)S(1)} custom-call(bf16[3,4,32,1024]{3,2,1,0:T(8,128)(2,1)S(1)} %get-tuple-element.10.own, bf16[3,4,32,1024]{3,2,1,0:T(8,128)(2,1)} %collective-permute-done.far, bf16[3,4,32,1024]{3,2,1,0:T(8,128)(2,1)} %collective-permute-done.1.mate_own, bf16[3,4,32,1024]{3,2,1,0:T(8,128)(2,1)} %collective-permute-done.2.mate_far, ...), custom_call_target="tpu_custom_call" | custom-call | flops 1024 | bytes 1024 | tf_op jit(solution)/shard_map/spatial/pallas_call | solution.py:115
  40.5 0.0 copy-start
  40.5 0.0 copy-start.2
  40.5 3.8 %all-to-all-done.2.refs_0_ = bf16[8,2,4,32,128]{4,3,2,1,0:T(8,128)(2,1)S(1)} async-done(((bf16[8,2,4,32,128]{4,3,2,1,0:T(8,128)(2,1)}), bf16[8,2,4,32,128]{4,3,2,1,0:T(8,128)(2,1)S(1)}, u32[]{:S(2)}, u32[]{:S(2)}) %all-to-all-start.2) | async-done | bytes 524320 | tf_op jit(solution)/shard_map/all_to_all | solution.py:371
  44.3 1.9 %collective-permute-start.6 = (bf16[8,2,4,32,128]{4,3,2,1,0:T(8,128)(2,1)S(1)}, bf16[8,2,4,32,128]{4,3,2,1,0:T(8,128)(2,1)S(1)}, u32[]{:S(2)}, u32[]{:S(2)}) collective-permute-start(bf16[8,2,4,32,128]{4,3,2,1,0:T(8,128)(2,1)S(1)} %behind.1.refs_1_), channel_id=1, source_target_pairs={{0,32},{32,64},{64,96},{96,128},{128,160},{160,192},{192,224},{224... | collective-permute-start | bytes 1572872 | tf_op jit(solution)/shard_map/ppermute | solution.py:389
  46.2 1.4 %collective-permute-start.4 = (bf16[2,128,1024]{2,1,0:T(8,128)(2,1)S(1)}, bf16[2,128,1024]{2,1,0:T(8,128)(2,1)}, u32[]{:S(2)}, u32[]{:S(2)}) collective-permute-start(bf16[2,128,1024]{2,1,0:T(8,128)(2,1)S(1)} %bitcast.17), channel_id=1, source_target_pairs={{0,2},{2,0},{1,3},{3,1},{4,6},{6,4},{5,7},{7,5},{8,10},{10,8},{9,1... | collective-permute-start | bytes 1572872 | tf_op jit(solution)/shard_map/ppermute | solution.py:382
  47.6 5.2 %all-to-all-start = ((bf16[8,2,4,32,128]{4,3,2,1,0:T(8,128)(2,1)}), bf16[8,2,4,32,128]{4,3,2,1,0:T(8,128)(2,1)S(1)}, u32[]{:S(2)}, u32[]{:S(2)}) async-start(bf16[8,2,4,32,128]{4,3,2,1,0:T(8,128)(2,1)} %get-tuple-element.7), calls=%async_computation | async-start | bytes 1048576 | tf_op jit(solution)/shard_map/all_to_all | solution.py:392
  52.8 1.0 collective-permute-done.5.refs_2_
  53.8 1.0 collective-permute-start.7
  54.8 10.3 %collective-permute-done.6.refs_3_ = bf16[8,2,4,32,128]{4,3,2,1,0:T(8,128)(2,1)S(1)} collective-permute-done((bf16[8,2,4,32,128]{4,3,2,1,0:T(8,128)(2,1)S(1)}, bf16[8,2,4,32,128]{4,3,2,1,0:T(8,128)(2,1)S(1)}, u32[]{:S(2)}, u32[]{:S(2)}) %collective-permute-start.6) | collective-permute-done | bytes 524320 | tf_op jit(solution)/shard_map/ppermute | solution.py:389
  65.1 0.7 slice.18
  65.7 0.0 collective-permute-start.8
  65.7 0.1 pad_add_fusion.place
  65.8 0.0 all-to-all-done.queries
  65.8 0.0 copy-done.2
  65.8 2.9 %temporal_late.1.refs_6_ = bf16[8,2,128,256]{3,2,1,0:T(8,128)(2,1)} custom-call(s32[3]{0:T(128)S(1)} %pad_add_fusion.place, s32[16]{0:T(128)S(1)} %copy-done.2, bf16[8,2,4,32,128]{4,3,2,1,0:T(8,128)(2,1)S(1)} %all-to-all-done.queries, bf16[8,2,4,32,128]{4,3,2,1,0:T(8,128)(2,1)S(1)} %all-to-all-done.1.refs_0_, bf16[8,2,4,32,128]{4,3,2,1,0:T(8,128)(2,1)S(1)} %behind.1.refs_1_, ...), custom_call_target="tpu_custom_call" | custom-call | flops 1024 | bytes 1024 | tf_op jit(solution)/shard_map/temporal_late/pallas_call | solution.py:189
  68.7 0.0 copy-done
  68.7 0.0 collective-permute-done.7.refs_4_
  68.7 0.0 collective-permute-done.4.far.refs_7_
  68.7 3.4 %collective-permute-done.8.refs_5_ = bf16[2,2,4,32,128]{4,3,2,1,0:T(8,128)(2,1)S(1)} collective-permute-done((bf16[2,2,4,32,128]{4,3,2,1,0:T(8,128)(2,1)}, bf16[2,2,4,32,128]{4,3,2,1,0:T(8,128)(2,1)S(1)}, u32[]{:S(2)}, u32[]{:S(2)}) %collective-permute-start.8) | collective-permute-done | bytes 131104 | tf_op jit(solution)/shard_map/ppermute | solution.py:390
  72.1 2.0 %temporal_early.1 = bf16[8,2,128,256]{3,2,1,0:T(8,128)(2,1)} custom-call(s32[3]{0:T(128)S(1)} %pad_add_fusion.place, s32[16]{0:T(128)S(1)} %copy-done.2, bf16[8,2,4,32,128]{4,3,2,1,0:T(8,128)(2,1)S(1)} %all-to-all-done.queries, bf16[8,2,4,32,128]{4,3,2,1,0:T(8,128)(2,1)S(1)} %all-to-all-done.1.refs_0_, ...), custom_call_target="tpu_custom_call", output_to_operand_aliasing={{}: (9, {})} | custom-call | flops 1024 | bytes 1024 | tf_op jit(solution)/shard_map/temporal_early/pallas_call | solution.py:217
  74.1 6.3 %all-to-all-start.3 = ((bf16[16,128,256]{2,1,0:T(8,128)(2,1)}), bf16[16,128,256]{2,1,0:T(8,128)(2,1)S(1)}, u32[]{:S(2)}, u32[]{:S(2)}) async-start(bf16[16,128,256]{2,1,0:T(8,128)(2,1)} %bitcast.8), calls=%async_computation.3 | async-start | bytes 2097152 | tf_op jit(solution)/shard_map/all_to_all | solution.py:396
  80.4 0.0 copy-start.1
  80.4 1.0 copy-done.1
  81.5 5.4 %project_first.1.partial = f32[2,2,128,1024]{3,2,1,0:T(8,128)S(1)} custom-call(s32[3]{0:T(128)S(1)} %pad_add_fusion.place, bf16[2,128,1024]{2,1,0:T(8,128)(2,1)S(1)} %bitcast.18, bf16[2,128,1024]{2,1,0:T(8,128)(2,1)} %collective-permute-done.4.far.refs_7_, bf16[4096,1024]{1,0:T(8,128)(2,1)} %wo.5, bf16[4096,1024]{1,0:T(8,128)(2,1)} %collective-permute-done.3.after.wo_mate), custom_call_target="tpu_custom_call" | custom-call | flops 1024 | bytes 1024 | tf_op jit(solution)/shard_map/project_first/pallas_call | solution.py:265
  86.9 4.7 %all-to-all-done.3 = bf16[16,128,256]{2,1,0:T(8,128)(2,1)S(1)} async-done(((bf16[16,128,256]{2,1,0:T(8,128)(2,1)}), bf16[16,128,256]{2,1,0:T(8,128)(2,1)S(1)}, u32[]{:S(2)}, u32[]{:S(2)}) %all-to-all-start.3) | async-done | bytes 1048608 | tf_op jit(solution)/shard_map/all_to_all | solution.py:396
  91.6 4.4 %project_next.1 = bf16[128,2048]{1,0:T(8,128)(2,1)S(1)} custom-call(s32[3]{0:T(128)S(1)} %pad_add_fusion.place, f32[2,2,128,1024]{3,2,1,0:T(8,128)S(1)} %project_first.1.partial, bf16[8,2,128,256]{3,2,1,0:T(8,128)(2,1)S(1)} %bitcast.14, bf16[4096,1024]{1,0:T(8,128)(2,1)} %wo.5, bf16[4096,1024]{1,0:T(8,128)(2,1)} %collective-permute-done.3.after.wo_mate), custom_call_target="tpu_custom_call" | custom-call | flops 1024 | bytes 1024 | tf_op jit(solution)/shard_map/project_next/pallas_call | solution.py:297
  95.9 2.1 %collective-permute-start.9 = (bf16[128,2048]{1,0:T(8,128)(2,1)S(1)}, bf16[128,2048]{1,0:T(8,128)(2,1)S(1)}, u32[]{:S(2)}, u32[]{:S(2)}) collective-permute-start(bf16[128,2048]{1,0:T(8,128)(2,1)S(1)} %project_next.1), channel_id=1, source_target_pairs={{0,2},{2,0},{1,3},{3,1},{4,6},{6,4},{5,7},{7,5},{8,10},{10,8},{9,1... | collective-permute-start | bytes 1572872 | tf_op jit(solution)/shard_map/ppermute | solution.py:400
  98.1 5.3 %project_own.1.mixed = bf16[128,4096]{1,0:T(8,128)(2,1)} custom-call(s32[3]{0:T(128)S(1)} %pad_add_fusion.place, f32[2,2,128,1024]{3,2,1,0:T(8,128)S(1)} %project_first.1.partial, bf16[8,2,128,256]{3,2,1,0:T(8,128)(2,1)S(1)} %bitcast.15, bf16[4096,1024]{1,0:T(8,128)(2,1)} %wo.5, bf16[4096,1024]{1,0:T(8,128)(2,1)} %collective-permute-done.3.after.wo_mate), custom_call_target="tpu_custom_call" | custom-call | flops 1024 | bytes 1024 | tf_op jit(solution)/shard_map/project_own/pallas_call | solution.py:297
  103.4 5.4 %collective-permute-done.9.arrived = bf16[128,2048]{1,0:T(8,128)(2,1)S(1)} collective-permute-done((bf16[128,2048]{1,0:T(8,128)(2,1)S(1)}, bf16[128,2048]{1,0:T(8,128)(2,1)S(1)}, u32[]{:S(2)}, u32[]{:S(2)}) %collective-permute-start.9) | collective-permute-done | bytes 524320 | tf_op jit(solution)/shard_map/ppermute | solution.py:400
  108.8 1.4 %put_arrived.1 = bf16[128,4096]{1,0:T(8,128)(2,1)} custom-call(s32[3]{0:T(128)S(1)} %pad_add_fusion.place, bf16[128,4096]{1,0:T(8,128)(2,1)} %project_own.1.mixed, bf16[128,2048]{1,0:T(8,128)(2,1)S(1)} %collective-permute-done.9.arrived), custom_call_target="tpu_custom_call", output_to_operand_aliasing={{}: (1, {})} | custom-call | flops 1024 | bytes 1024 | tf_op jit(solution)/shard_map/put_arrived/pallas_call | solution.py:338
  (2 shorter events, 0.0 us)
Async XLA Ops:
  0.0 37.1 %collective-permute-start.3 = (bf16[4096,1024]{1,0:T(8,128)(2,1)}, bf16[4096,1024]{1,0:T(8,128)(2,1)}, u32[]{:S(2)}, u32[]{:S(2)}) collective-permute-start(bf16[4096,1024]{1,0:T(8,128)(2,1)} %wo.5), channel_id=1, source_target_pairs={{0,1},{1,0},{2,3},{3,2},{4,5},{5,4},{6,7},{7,6},{8,9},{9,8},{10,11... | collective-permute-start | bytes 25165832 | tf_op jit(solution)/shard_map/ppermute | solution.py:375
  1.5 22.0 %collective-permute-start = (bf16[3,4,32,1024]{3,2,1,0:T(8,128)(2,1)S(1)}, bf16[3,4,32,1024]{3,2,1,0:T(8,128)(2,1)}, u32[]{:S(2)}, u32[]{:S(2)}) collective-permute-start(bf16[3,4,32,1024]{3,2,1,0:T(8,128)(2,1)S(1)} %get-tuple-element.9), channel_id=1, source_target_pairs={{0,2},{2,0},{1,3},{3,1},{4,6},{6,4},{5,7},{7,5},{8,10},{10,8},{9,1... | collective-permute-start | bytes 2359304 | tf_op jit(solution)/shard_map/ppermute | solution.py:377
  6.0 24.4 %all-to-all-start.1 = ((bf16[8,2,4,32,128]{4,3,2,1,0:T(8,128)(2,1)}), bf16[8,2,4,32,128]{4,3,2,1,0:T(8,128)(2,1)S(1)}, u32[]{:S(2)}, u32[]{:S(2)}) async-start(bf16[8,2,4,32,128]{4,3,2,1,0:T(8,128)(2,1)} %copy_bitcast_fusion), calls=%async_computation.1 | async-start | bytes 1048576 | tf_op jit(solution)/shard_map/all_to_all | solution.py:371
  11.9 25.2 %collective-permute-start.1 = (bf16[3,4,32,1024]{3,2,1,0:T(8,128)(2,1)S(1)}, bf16[3,4,32,1024]{3,2,1,0:T(8,128)(2,1)}, u32[]{:S(2)}, u32[]{:S(2)}) collective-permute-start(bf16[3,4,32,1024]{3,2,1,0:T(8,128)(2,1)S(1)} %get-tuple-element.10.own), channel_id=1, source_target_pairs={{0,1},{1,0},{2,3},{3,2},{4,5},{5,4},{6,7},{7,6},{8,9},{9,8},{10,11... | collective-permute-start | bytes 2359304 | tf_op jit(solution)/shard_map/ppermute | solution.py:378
  23.6 13.5 %collective-permute-start.2 = (bf16[3,4,32,1024]{3,2,1,0:T(8,128)(2,1)}, bf16[3,4,32,1024]{3,2,1,0:T(8,128)(2,1)}, u32[]{:S(2)}, u32[]{:S(2)}) collective-permute-start(bf16[3,4,32,1024]{3,2,1,0:T(8,128)(2,1)} %collective-permute-done.far), channel_id=1, source_target_pairs={{0,1},{1,0},{2,3},{3,2},{4,5},{5,4},{6,7},{7,6},{8,9},{9,8},{10,11... | collective-permute-start | bytes 2359304 | tf_op jit(solution)/shard_map/ppermute | solution.py:379
  30.3 13.9 %all-to-all-start.2 = ((bf16[8,2,4,32,128]{4,3,2,1,0:T(8,128)(2,1)}), bf16[8,2,4,32,128]{4,3,2,1,0:T(8,128)(2,1)S(1)}, u32[]{:S(2)}, u32[]{:S(2)}) async-start(bf16[8,2,4,32,128]{4,3,2,1,0:T(8,128)(2,1)} %get-tuple-element.8), calls=%async_computation.2 | async-start | bytes 1048576 | tf_op jit(solution)/shard_map/all_to_all | solution.py:371
  35.2 18.7 %collective-permute-start.5 = (bf16[8,2,4,32,128]{4,3,2,1,0:T(8,128)(2,1)S(1)}, bf16[8,2,4,32,128]{4,3,2,1,0:T(8,128)(2,1)S(1)}, u32[]{:S(2)}, u32[]{:S(2)}) collective-permute-start(bf16[8,2,4,32,128]{4,3,2,1,0:T(8,128)(2,1)S(1)} %all-to-all-done.1.refs_0_), channel_id=1, source_target_pairs={{0,32},{32,64},{64,96},{96,128},{128,160},{160,192},{192,224},{224... | collective-permute-start | bytes 1572872 | tf_op jit(solution)/shard_map/ppermute | solution.py:389
  40.5 28.3 %copy-start = (bf16[2,4,32,1024]{3,2,1,0:T(8,128)(2,1)}, bf16[2,4,32,1024]{3,2,1,0:T(8,128)(2,1)S(1)}, u32[]{:S(2)}) copy-start(bf16[2,4,32,1024]{3,2,1,0:T(8,128)(2,1)S(1)} %spatial.1) | copy-start | bytes 1572868
  40.5 25.4 %copy-start.2 = (s32[16]{0:T(128)S(1)}, s32[16]{0:T(128)}, u32[]{:S(2)}) copy-start(s32[16]{0:T(128)} %lengths.3) | copy-start | bytes 196
  44.3 20.8 %collective-permute-start.6 = (bf16[8,2,4,32,128]{4,3,2,1,0:T(8,128)(2,1)S(1)}, bf16[8,2,4,32,128]{4,3,2,1,0:T(8,128)(2,1)S(1)}, u32[]{:S(2)}, u32[]{:S(2)}) collective-permute-start(bf16[8,2,4,32,128]{4,3,2,1,0:T(8,128)(2,1)S(1)} %behind.1.refs_1_), channel_id=1, source_target_pairs={{0,32},{32,64},{64,96},{96,128},{128,160},{160,192},{192,224},{224... | collective-permute-start | bytes 1572872 | tf_op jit(solution)/shard_map/ppermute | solution.py:389
  46.2 22.5 %collective-permute-start.4 = (bf16[2,128,1024]{2,1,0:T(8,128)(2,1)S(1)}, bf16[2,128,1024]{2,1,0:T(8,128)(2,1)}, u32[]{:S(2)}, u32[]{:S(2)}) collective-permute-start(bf16[2,128,1024]{2,1,0:T(8,128)(2,1)S(1)} %bitcast.17), channel_id=1, source_target_pairs={{0,2},{2,0},{1,3},{3,1},{4,6},{6,4},{5,7},{7,5},{8,10},{10,8},{9,1... | collective-permute-start | bytes 1572872 | tf_op jit(solution)/shard_map/ppermute | solution.py:382
  47.6 18.2 %all-to-all-start = ((bf16[8,2,4,32,128]{4,3,2,1,0:T(8,128)(2,1)}), bf16[8,2,4,32,128]{4,3,2,1,0:T(8,128)(2,1)S(1)}, u32[]{:S(2)}, u32[]{:S(2)}) async-start(bf16[8,2,4,32,128]{4,3,2,1,0:T(8,128)(2,1)} %get-tuple-element.7), calls=%async_computation | async-start | bytes 1048576 | tf_op jit(solution)/shard_map/all_to_all | solution.py:392
  53.8 14.9 %collective-permute-start.7 = (bf16[2,2,4,32,128]{4,3,2,1,0:T(8,128)(2,1)S(1)}, bf16[2,2,4,32,128]{4,3,2,1,0:T(8,128)(2,1)S(1)}, u32[]{:S(2)}, u32[]{:S(2)}) collective-permute-start(bf16[2,2,4,32,128]{4,3,2,1,0:T(8,128)(2,1)S(1)} %slice.17), channel_id=1, source_target_pairs={{0,32},{32,64},{64,96},{96,128},{128,160},{160,192},{192,224},{224... | collective-permute-start | bytes 393224 | tf_op jit(solution)/shard_map/ppermute | solution.py:390
  65.7 6.4 %collective-permute-start.8 = (bf16[2,2,4,32,128]{4,3,2,1,0:T(8,128)(2,1)}, bf16[2,2,4,32,128]{4,3,2,1,0:T(8,128)(2,1)S(1)}, u32[]{:S(2)}, u32[]{:S(2)}) collective-permute-start(bf16[2,2,4,32,128]{4,3,2,1,0:T(8,128)(2,1)} %slice.18), channel_id=1, source_target_pairs={{0,32},{32,64},{64,96},{96,128},{128,160},{160,192},{192,224},{224... | collective-permute-start | bytes 393224 | tf_op jit(solution)/shard_map/ppermute | solution.py:390
  74.1 17.4 %all-to-all-start.3 = ((bf16[16,128,256]{2,1,0:T(8,128)(2,1)}), bf16[16,128,256]{2,1,0:T(8,128)(2,1)S(1)}, u32[]{:S(2)}, u32[]{:S(2)}) async-start(bf16[16,128,256]{2,1,0:T(8,128)(2,1)} %bitcast.8), calls=%async_computation.3 | async-start | bytes 2097152 | tf_op jit(solution)/shard_map/all_to_all | solution.py:396
  80.4 1.0 copy-start.1
  95.9 12.9 %collective-permute-start.9 = (bf16[128,2048]{1,0:T(8,128)(2,1)S(1)}, bf16[128,2048]{1,0:T(8,128)(2,1)S(1)}, u32[]{:S(2)}, u32[]{:S(2)}) collective-permute-start(bf16[128,2048]{1,0:T(8,128)(2,1)S(1)} %project_next.1), channel_id=1, source_target_pairs={{0,2},{2,0},{1,3},{3,1},{4,6},{6,4},{5,7},{7,5},{8,10},{10,8},{9,1... | collective-permute-start | bytes 1572872 | tf_op jit(solution)/shard_map/ppermute | solution.py:400

commit v5 on v4

--- a/solution.py
+++ b/solution.py
@@ -326,26 +326,28 @@
 
 
 def put_arrived(place, mixed, arrived):
-    rows, width = arrived.shape
-    cols = width // 2
-
-    def body(place, mixed, arrived, out):
-        out[...] = arrived[...]
-
-    def target(side, place):
-        return 0, (1 - place[1]) * C + place[2] + side * (1 - 2 * place[2])
-
-    return pl.pallas_call(
-        body,
-        grid_spec=pltpu.PrefetchScalarGridSpec(
-            num_scalar_prefetch=1,
-            grid=(2,),
-            in_specs=[ANYWHERE, pl.BlockSpec((rows, cols), lambda side, place: (0, side))],
-            out_specs=pl.BlockSpec((rows, cols), target),
-        ),
+    cols = arrived.shape[1] // 2
+
+    def body(place, mixed, arrived, out, arrivals):
+        copies = []
+        for side in range(2):
+            block = (1 - place[1]) * C + place[2] + side * (1 - 2 * place[2])
+            target = out.at[:, pl.ds(pl.multiple_of(block * cols, cols), cols)]
+            source = arrived.at[:, side * cols : (side + 1) * cols]
+            copies.append(pltpu.make_async_copy(source, target, arrivals.at[side]))
+        for copy in copies:
+            copy.start()
+        for copy in copies:
+            copy.wait()
+
+    return pl.pallas_call(
+        body,
+        in_specs=[SMEM, IN_HBM, ANYWHERE],
+        out_specs=IN_HBM,
         out_shape=jax.ShapeDtypeStruct(mixed.shape, mixed.dtype),
+        scratch_shapes=[pltpu.SemaphoreType.DMA((2,))],
         input_output_aliases={1: 0},
-        compiler_params=kernel_params(16),
+        compiler_params=kernel_params(4),
         cost_estimate=QUICK,
         name="put_arrived",
     )(place, mixed, arrived)

time: 111 us -> 111 us (level)
  no operation moved by 1% of the time
where the time goes in v5:
time: 111 us; the launch traced here: 110 us
  waiting for transfers between devices  44.8 us (40%)
  starting transfers between devices  32.8 us (30%)
  Pallas kernels  27 us (24%)
  local copies, waits for them, and re-layouts  5.47 us (5%)
    ppermute x1, waiting for transfers between devices, on_device(): lax.ppermute(lax.dynamic_slice(qkv, (0, 0, 0, far_cols), (3, frames, tok,...  11.7 us
    ppermute x2, waiting for transfers between devices, on_device(): before.append(lax.ppermute(got, 'z', onward))  11.3 us
    all_to_all x2, starting transfers between devices, on_device(): lax.all_to_all(block, ('y', 'xl'), 0, 0, tiled=True)  10.8 us
    pallas_call x2, Pallas kernels, project_last(): pl.pallas_call(body, in_specs=[SMEM] + [WHOLE] * 2 + [IN_HBM] * 2, out_sp...  9.68 us
    all_to_all x2, waiting for transfers between devices, on_device(): lax.all_to_all(block, ('y', 'xl'), 0, 0, tiled=True)  8.26 us
    all_to_all x1, starting transfers between devices, on_device(): lax.all_to_all(sent, ('y', 'xl', 'xh'), 0, 0, tiled=True)  6.29 us
    ppermute x1, waiting for transfers between devices, on_device(): arrived = lax.ppermute(for_next, 'xh', SWAP)  5.44 us
    pallas_call x1, Pallas kernels, project_first(): pl.pallas_call(body, in_specs=[SMEM] + [WHOLE] * 2 + [IN_HBM] * 2, out_sp...  5.37 us
  transfers between devices with their start and end apart: 14, of which 8 were waited for; matrix products, arithmetic and copies ran while one was open for 4% of the time, Pallas kernels for 17%

profile of v5, /device:TPU:2, one launch (start us, length us, event | category | flops | bytes accessed | tf_op | source)
XLA Modules:
  0.0 110.4 jit_solution(6626215397479160281)
XLA Ops:
  0.0 0.0 collective-permute-start.3
  0.0 1.5 %constant_dynamic-slice_fusion = (bf16[3,4,32,1024]{3,2,1,0:T(8,128)(2,1)S(1)}, bf16[3,4,32,1024]{3,2,1,0:T(8,128)(2,1)S(1)}) fusion(bf16[3,4,32,4096]{3,2,1,0:T(8,128)(2,1)} %qkv.1, s32[]{:T(128)S(6)} %select_n.7, s32[]{:T(128)S(6)} %select_n.6), kind=kLoop, calls=%fused_computation.2 | loop fusion | bytes 3145736 | tf_op jit(solution)/shard_map/dynamic_slice | solution.py:379
  1.5 2.2 %collective-permute-start = (bf16[3,4,32,1024]{3,2,1,0:T(8,128)(2,1)S(1)}, bf16[3,4,32,1024]{3,2,1,0:T(8,128)(2,1)}, u32[]{:S(2)}, u32[]{:S(2)}) collective-permute-start(bf16[3,4,32,1024]{3,2,1,0:T(8,128)(2,1)S(1)} %get-tuple-element.9), channel_id=1, source_target_pairs={{0,2},{2,0},{1,3},{3,1},{4,6},{6,4},{5,7},{7,5},{8,10},{10,8},{9,1... | collective-permute-start | bytes 2359304 | tf_op jit(solution)/shard_map/ppermute | solution.py:379
  3.8 1.3 %slice.12 = bf16[2,4,32,2048]{3,2,1,0:T(8,128)(2,1)S(1)} slice(bf16[3,4,32,4096]{3,2,1,0:T(8,128)(2,1)} %qkv.1), slice={[1:3], [0:4], [0:32], [2048:4096]} | slice | bytes 2097152 | tf_op jit(solution)/shard_map/slice | solution.py:372
  5.1 0.9 copy_bitcast_fusion
  6.0 5.9 %all-to-all-start.1 = ((bf16[8,2,4,32,128]{4,3,2,1,0:T(8,128)(2,1)}), bf16[8,2,4,32,128]{4,3,2,1,0:T(8,128)(2,1)S(1)}, u32[]{:S(2)}, u32[]{:S(2)}) async-start(bf16[8,2,4,32,128]{4,3,2,1,0:T(8,128)(2,1)} %copy_bitcast_fusion), calls=%async_computation.1 | async-start | bytes 1048576 | tf_op jit(solution)/shard_map/all_to_all | solution.py:373
  11.9 0.0 collective-permute-start.1
  11.9 11.7 %collective-permute-done.far = bf16[3,4,32,1024]{3,2,1,0:T(8,128)(2,1)} collective-permute-done((bf16[3,4,32,1024]{3,2,1,0:T(8,128)(2,1)S(1)}, bf16[3,4,32,1024]{3,2,1,0:T(8,128)(2,1)}, u32[]{:S(2)}, u32[]{:S(2)}) %collective-permute-start) | collective-permute-done | bytes 786464 | tf_op jit(solution)/shard_map/ppermute | solution.py:379
  23.6 0.0 collective-permute-start.2
  23.6 2.3 %pack_rest.1 = (bf16[8,2,4,32,128]{4,3,2,1,0:T(8,128)(2,1)}, bf16[8,2,4,32,128]{4,3,2,1,0:T(8,128)(2,1)}) custom-call(bf16[3,4,32,4096]{3,2,1,0:T(8,128)(2,1)} %qkv.1), custom_call_target="tpu_custom_call" | custom-call | flops 1024 | bytes 1024 | tf_op jit(solution)/shard_map/pack_rest/pallas_call | solution.py:78
  25.9 4.5 %all-to-all-done.1.refs_0_ = bf16[8,2,4,32,128]{4,3,2,1,0:T(8,128)(2,1)S(1)} async-done(((bf16[8,2,4,32,128]{4,3,2,1,0:T(8,128)(2,1)}), bf16[8,2,4,32,128]{4,3,2,1,0:T(8,128)(2,1)S(1)}, u32[]{:S(2)}, u32[]{:S(2)}) %all-to-all-start.1) | async-done | bytes 524320 | tf_op jit(solution)/shard_map/all_to_all | solution.py:373
  30.3 4.8 %all-to-all-start.2 = ((bf16[8,2,4,32,128]{4,3,2,1,0:T(8,128)(2,1)}), bf16[8,2,4,32,128]{4,3,2,1,0:T(8,128)(2,1)S(1)}, u32[]{:S(2)}, u32[]{:S(2)}) async-start(bf16[8,2,4,32,128]{4,3,2,1,0:T(8,128)(2,1)} %get-tuple-element.8), calls=%async_computation.2 | async-start | bytes 1048576 | tf_op jit(solution)/shard_map/all_to_all | solution.py:373
  35.2 1.9 %collective-permute-start.5 = (bf16[8,2,4,32,128]{4,3,2,1,0:T(8,128)(2,1)S(1)}, bf16[8,2,4,32,128]{4,3,2,1,0:T(8,128)(2,1)S(1)}, u32[]{:S(2)}, u32[]{:S(2)}) collective-permute-start(bf16[8,2,4,32,128]{4,3,2,1,0:T(8,128)(2,1)S(1)} %all-to-all-done.1.refs_0_), channel_id=1, source_target_pairs={{0,32},{32,64},{64,96},{96,128},{128,160},{160,192},{192,224},{224... | collective-permute-start | bytes 1572872 | tf_op jit(solution)/shard_map/ppermute | solution.py:391
  37.1 0.0 collective-permute-done.1.mate_own
  37.1 0.0 collective-permute-done.2.mate_far
  37.1 0.0 collective-permute-done.3.after.wo_mate
  37.1 3.3 %spatial.1 = bf16[2,4,32,1024]{3,2,1,0:T(8,128)(2,1)S(1)} custom-call(bf16[3,4,32,1024]{3,2,1,0:T(8,128)(2,1)S(1)} %get-tuple-element.10.own, bf16[3,4,32,1024]{3,2,1,0:T(8,128)(2,1)} %collective-permute-done.far, bf16[3,4,32,1024]{3,2,1,0:T(8,128)(2,1)} %collective-permute-done.1.mate_own, bf16[3,4,32,1024]{3,2,1,0:T(8,128)(2,1)} %collective-permute-done.2.mate_far, ...), custom_call_target="tpu_custom_call" | custom-call | flops 1024 | bytes 1024 | tf_op jit(solution)/shard_map/spatial/pallas_call | solution.py:115
  40.5 0.0 copy-start
  40.5 0.0 copy-start.2
  40.5 3.8 %all-to-all-done.2.refs_0_ = bf16[8,2,4,32,128]{4,3,2,1,0:T(8,128)(2,1)S(1)} async-done(((bf16[8,2,4,32,128]{4,3,2,1,0:T(8,128)(2,1)}), bf16[8,2,4,32,128]{4,3,2,1,0:T(8,128)(2,1)S(1)}, u32[]{:S(2)}, u32[]{:S(2)}) %all-to-all-start.2) | async-done | bytes 524320 | tf_op jit(solution)/shard_map/all_to_all | solution.py:373
  44.3 1.9 %collective-permute-start.6 = (bf16[8,2,4,32,128]{4,3,2,1,0:T(8,128)(2,1)S(1)}, bf16[8,2,4,32,128]{4,3,2,1,0:T(8,128)(2,1)S(1)}, u32[]{:S(2)}, u32[]{:S(2)}) collective-permute-start(bf16[8,2,4,32,128]{4,3,2,1,0:T(8,128)(2,1)S(1)} %behind.1.refs_1_), channel_id=1, source_target_pairs={{0,32},{32,64},{64,96},{96,128},{128,160},{160,192},{192,224},{224... | collective-permute-start | bytes 1572872 | tf_op jit(solution)/shard_map/ppermute | solution.py:391
  46.2 1.4 %collective-permute-start.4 = (bf16[2,128,1024]{2,1,0:T(8,128)(2,1)S(1)}, bf16[2,128,1024]{2,1,0:T(8,128)(2,1)}, u32[]{:S(2)}, u32[]{:S(2)}) collective-permute-start(bf16[2,128,1024]{2,1,0:T(8,128)(2,1)S(1)} %bitcast.17), channel_id=1, source_target_pairs={{0,2},{2,0},{1,3},{3,1},{4,6},{6,4},{5,7},{7,5},{8,10},{10,8},{9,1... | collective-permute-start | bytes 1572872 | tf_op jit(solution)/shard_map/ppermute | solution.py:384
  47.6 5.2 %all-to-all-start = ((bf16[8,2,4,32,128]{4,3,2,1,0:T(8,128)(2,1)}), bf16[8,2,4,32,128]{4,3,2,1,0:T(8,128)(2,1)S(1)}, u32[]{:S(2)}, u32[]{:S(2)}) async-start(bf16[8,2,4,32,128]{4,3,2,1,0:T(8,128)(2,1)} %get-tuple-element.7), calls=%async_computation | async-start | bytes 1048576 | tf_op jit(solution)/shard_map/all_to_all | solution.py:394
  52.8 1.0 collective-permute-done.5.refs_2_
  53.8 1.0 collective-permute-start.7
  54.8 10.3 %collective-permute-done.6.refs_3_ = bf16[8,2,4,32,128]{4,3,2,1,0:T(8,128)(2,1)S(1)} collective-permute-done((bf16[8,2,4,32,128]{4,3,2,1,0:T(8,128)(2,1)S(1)}, bf16[8,2,4,32,128]{4,3,2,1,0:T(8,128)(2,1)S(1)}, u32[]{:S(2)}, u32[]{:S(2)}) %collective-permute-start.6) | collective-permute-done | bytes 524320 | tf_op jit(solution)/shard_map/ppermute | solution.py:391
  65.1 0.7 slice.18
  65.7 0.0 collective-permute-start.8
  65.7 0.1 pad_add_fusion.place
  65.8 0.0 all-to-all-done.queries
  65.8 0.0 copy-done.2
  65.8 2.9 %temporal_late.1.refs_6_ = bf16[8,2,128,256]{3,2,1,0:T(8,128)(2,1)} custom-call(s32[3]{0:T(128)S(1)} %pad_add_fusion.place, s32[16]{0:T(128)S(1)} %copy-done.2, bf16[8,2,4,32,128]{4,3,2,1,0:T(8,128)(2,1)S(1)} %all-to-all-done.queries, bf16[8,2,4,32,128]{4,3,2,1,0:T(8,128)(2,1)S(1)} %all-to-all-done.1.refs_0_, bf16[8,2,4,32,128]{4,3,2,1,0:T(8,128)(2,1)S(1)} %behind.1.refs_1_, ...), custom_call_target="tpu_custom_call" | custom-call | flops 1024 | bytes 1024 | tf_op jit(solution)/shard_map/temporal_late/pallas_call | solution.py:189
  68.7 0.0 copy-done
  68.7 0.0 collective-permute-done.7.refs_4_
  68.7 0.0 collective-permute-done.4.far.refs_7_
  68.7 3.4 %collective-permute-done.8.refs_5_ = bf16[2,2,4,32,128]{4,3,2,1,0:T(8,128)(2,1)S(1)} collective-permute-done((bf16[2,2,4,32,128]{4,3,2,1,0:T(8,128)(2,1)}, bf16[2,2,4,32,128]{4,3,2,1,0:T(8,128)(2,1)S(1)}, u32[]{:S(2)}, u32[]{:S(2)}) %collective-permute-start.8) | collective-permute-done | bytes 131104 | tf_op jit(solution)/shard_map/ppermute | solution.py:392
  72.1 2.0 %temporal_early.1 = bf16[8,2,128,256]{3,2,1,0:T(8,128)(2,1)} custom-call(s32[3]{0:T(128)S(1)} %pad_add_fusion.place, s32[16]{0:T(128)S(1)} %copy-done.2, bf16[8,2,4,32,128]{4,3,2,1,0:T(8,128)(2,1)S(1)} %all-to-all-done.queries, bf16[8,2,4,32,128]{4,3,2,1,0:T(8,128)(2,1)S(1)} %all-to-all-done.1.refs_0_, ...), custom_call_target="tpu_custom_call", output_to_operand_aliasing={{}: (9, {})} | custom-call | flops 1024 | bytes 1024 | tf_op jit(solution)/shard_map/temporal_early/pallas_call | solution.py:217
  74.1 6.3 %all-to-all-start.3 = ((bf16[16,128,256]{2,1,0:T(8,128)(2,1)}), bf16[16,128,256]{2,1,0:T(8,128)(2,1)S(1)}, u32[]{:S(2)}, u32[]{:S(2)}) async-start(bf16[16,128,256]{2,1,0:T(8,128)(2,1)} %bitcast.8), calls=%async_computation.3 | async-start | bytes 2097152 | tf_op jit(solution)/shard_map/all_to_all | solution.py:398
  80.4 0.0 copy-start.1
  80.4 1.0 copy-done.1
  81.5 5.4 %project_first.1.partial = f32[2,2,128,1024]{3,2,1,0:T(8,128)S(1)} custom-call(s32[3]{0:T(128)S(1)} %pad_add_fusion.place, bf16[2,128,1024]{2,1,0:T(8,128)(2,1)S(1)} %bitcast.18, bf16[2,128,1024]{2,1,0:T(8,128)(2,1)} %collective-permute-done.4.far.refs_7_, bf16[4096,1024]{1,0:T(8,128)(2,1)} %wo.5, bf16[4096,1024]{1,0:T(8,128)(2,1)} %collective-permute-done.3.after.wo_mate), custom_call_target="tpu_custom_call" | custom-call | flops 1024 | bytes 1024 | tf_op jit(solution)/shard_map/project_first/pallas_call | solution.py:265
  86.9 4.7 %all-to-all-done.3 = bf16[16,128,256]{2,1,0:T(8,128)(2,1)S(1)} async-done(((bf16[16,128,256]{2,1,0:T(8,128)(2,1)}), bf16[16,128,256]{2,1,0:T(8,128)(2,1)S(1)}, u32[]{:S(2)}, u32[]{:S(2)}) %all-to-all-start.3) | async-done | bytes 1048608 | tf_op jit(solution)/shard_map/all_to_all | solution.py:398
  91.6 4.4 %project_next.1 = bf16[128,2048]{1,0:T(8,128)(2,1)S(1)} custom-call(s32[3]{0:T(128)S(1)} %pad_add_fusion.place, f32[2,2,128,1024]{3,2,1,0:T(8,128)S(1)} %project_first.1.partial, bf16[8,2,128,256]{3,2,1,0:T(8,128)(2,1)S(1)} %bitcast.14, bf16[4096,1024]{1,0:T(8,128)(2,1)} %wo.5, bf16[4096,1024]{1,0:T(8,128)(2,1)} %collective-permute-done.3.after.wo_mate), custom_call_target="tpu_custom_call" | custom-call | flops 1024 | bytes 1024 | tf_op jit(solution)/shard_map/project_next/pallas_call | solution.py:297
  95.9 2.1 %collective-permute-start.9 = (bf16[128,2048]{1,0:T(8,128)(2,1)S(1)}, bf16[128,2048]{1,0:T(8,128)(2,1)S(1)}, u32[]{:S(2)}, u32[]{:S(2)}) collective-permute-start(bf16[128,2048]{1,0:T(8,128)(2,1)S(1)} %project_next.1), channel_id=1, source_target_pairs={{0,2},{2,0},{1,3},{3,1},{4,6},{6,4},{5,7},{7,5},{8,10},{10,8},{9,1... | collective-permute-start | bytes 1572872 | tf_op jit(solution)/shard_map/ppermute | solution.py:402
  98.1 5.3 %project_own.1.mixed = bf16[128,4096]{1,0:T(8,128)(2,1)} custom-call(s32[3]{0:T(128)S(1)} %pad_add_fusion.place, f32[2,2,128,1024]{3,2,1,0:T(8,128)S(1)} %project_first.1.partial, bf16[8,2,128,256]{3,2,1,0:T(8,128)(2,1)S(1)} %bitcast.15, bf16[4096,1024]{1,0:T(8,128)(2,1)} %wo.5, bf16[4096,1024]{1,0:T(8,128)(2,1)} %collective-permute-done.3.after.wo_mate), custom_call_target="tpu_custom_call" | custom-call | flops 1024 | bytes 1024 | tf_op jit(solution)/shard_map/project_own/pallas_call | solution.py:297
  103.4 5.4 %collective-permute-done.9.arrived = bf16[128,2048]{1,0:T(8,128)(2,1)S(1)} collective-permute-done((bf16[128,2048]{1,0:T(8,128)(2,1)S(1)}, bf16[128,2048]{1,0:T(8,128)(2,1)S(1)}, u32[]{:S(2)}, u32[]{:S(2)}) %collective-permute-start.9) | collective-permute-done | bytes 524320 | tf_op jit(solution)/shard_map/ppermute | solution.py:402
  108.8 1.4 %put_arrived.1 = bf16[128,4096]{1,0:T(8,128)(2,1)} custom-call(s32[3]{0:T(128)S(1)} %pad_add_fusion.place, bf16[128,4096]{1,0:T(8,128)(2,1)} %project_own.1.mixed, bf16[128,2048]{1,0:T(8,128)(2,1)S(1)} %collective-permute-done.9.arrived), custom_call_target="tpu_custom_call", output_to_operand_aliasing={{}: (1, {})} | custom-call | flops 1024 | bytes 1024 | tf_op jit(solution)/shard_map/put_arrived/pallas_call | solution.py:343
  (2 shorter events, 0.0 us)
Async XLA Ops:
  0.0 37.1 %collective-permute-start.3 = (bf16[4096,1024]{1,0:T(8,128)(2,1)}, bf16[4096,1024]{1,0:T(8,128)(2,1)}, u32[]{:S(2)}, u32[]{:S(2)}) collective-permute-start(bf16[4096,1024]{1,0:T(8,128)(2,1)} %wo.5), channel_id=1, source_target_pairs={{0,1},{1,0},{2,3},{3,2},{4,5},{5,4},{6,7},{7,6},{8,9},{9,8},{10,11... | collective-permute-start | bytes 25165832 | tf_op jit(solution)/shard_map/ppermute | solution.py:377
  1.5 22.0 %collective-permute-start = (bf16[3,4,32,1024]{3,2,1,0:T(8,128)(2,1)S(1)}, bf16[3,4,32,1024]{3,2,1,0:T(8,128)(2,1)}, u32[]{:S(2)}, u32[]{:S(2)}) collective-permute-start(bf16[3,4,32,1024]{3,2,1,0:T(8,128)(2,1)S(1)} %get-tuple-element.9), channel_id=1, source_target_pairs={{0,2},{2,0},{1,3},{3,1},{4,6},{6,4},{5,7},{7,5},{8,10},{10,8},{9,1... | collective-permute-start | bytes 2359304 | tf_op jit(solution)/shard_map/ppermute | solution.py:379
  6.0 24.4 %all-to-all-start.1 = ((bf16[8,2,4,32,128]{4,3,2,1,0:T(8,128)(2,1)}), bf16[8,2,4,32,128]{4,3,2,1,0:T(8,128)(2,1)S(1)}, u32[]{:S(2)}, u32[]{:S(2)}) async-start(bf16[8,2,4,32,128]{4,3,2,1,0:T(8,128)(2,1)} %copy_bitcast_fusion), calls=%async_computation.1 | async-start | bytes 1048576 | tf_op jit(solution)/shard_map/all_to_all | solution.py:373
  11.9 25.2 %collective-permute-start.1 = (bf16[3,4,32,1024]{3,2,1,0:T(8,128)(2,1)S(1)}, bf16[3,4,32,1024]{3,2,1,0:T(8,128)(2,1)}, u32[]{:S(2)}, u32[]{:S(2)}) collective-permute-start(bf16[3,4,32,1024]{3,2,1,0:T(8,128)(2,1)S(1)} %get-tuple-element.10.own), channel_id=1, source_target_pairs={{0,1},{1,0},{2,3},{3,2},{4,5},{5,4},{6,7},{7,6},{8,9},{9,8},{10,11... | collective-permute-start | bytes 2359304 | tf_op jit(solution)/shard_map/ppermute | solution.py:380
  23.6 13.5 %collective-permute-start.2 = (bf16[3,4,32,1024]{3,2,1,0:T(8,128)(2,1)}, bf16[3,4,32,1024]{3,2,1,0:T(8,128)(2,1)}, u32[]{:S(2)}, u32[]{:S(2)}) collective-permute-start(bf16[3,4,32,1024]{3,2,1,0:T(8,128)(2,1)} %collective-permute-done.far), channel_id=1, source_target_pairs={{0,1},{1,0},{2,3},{3,2},{4,5},{5,4},{6,7},{7,6},{8,9},{9,8},{10,11... | collective-permute-start | bytes 2359304 | tf_op jit(solution)/shard_map/ppermute | solution.py:381
  30.3 13.9 %all-to-all-start.2 = ((bf16[8,2,4,32,128]{4,3,2,1,0:T(8,128)(2,1)}), bf16[8,2,4,32,128]{4,3,2,1,0:T(8,128)(2,1)S(1)}, u32[]{:S(2)}, u32[]{:S(2)}) async-start(bf16[8,2,4,32,128]{4,3,2,1,0:T(8,128)(2,1)} %get-tuple-element.8), calls=%async_computation.2 | async-start | bytes 1048576 | tf_op jit(solution)/shard_map/all_to_all | solution.py:373
  35.2 18.7 %collective-permute-start.5 = (bf16[8,2,4,32,128]{4,3,2,1,0:T(8,128)(2,1)S(1)}, bf16[8,2,4,32,128]{4,3,2,1,0:T(8,128)(2,1)S(1)}, u32[]{:S(2)}, u32[]{:S(2)}) collective-permute-start(bf16[8,2,4,32,128]{4,3,2,1,0:T(8,128)(2,1)S(1)} %all-to-all-done.1.refs_0_), channel_id=1, source_target_pairs={{0,32},{32,64},{64,96},{96,128},{128,160},{160,192},{192,224},{224... | collective-permute-start | bytes 1572872 | tf_op jit(solution)/shard_map/ppermute | solution.py:391
  40.5 28.3 %copy-start = (bf16[2,4,32,1024]{3,2,1,0:T(8,128)(2,1)}, bf16[2,4,32,1024]{3,2,1,0:T(8,128)(2,1)S(1)}, u32[]{:S(2)}) copy-start(bf16[2,4,32,1024]{3,2,1,0:T(8,128)(2,1)S(1)} %spatial.1) | copy-start | bytes 1572868
  40.5 25.4 %copy-start.2 = (s32[16]{0:T(128)S(1)}, s32[16]{0:T(128)}, u32[]{:S(2)}) copy-start(s32[16]{0:T(128)} %lengths.3) | copy-start | bytes 196
  44.3 20.8 %collective-permute-start.6 = (bf16[8,2,4,32,128]{4,3,2,1,0:T(8,128)(2,1)S(1)}, bf16[8,2,4,32,128]{4,3,2,1,0:T(8,128)(2,1)S(1)}, u32[]{:S(2)}, u32[]{:S(2)}) collective-permute-start(bf16[8,2,4,32,128]{4,3,2,1,0:T(8,128)(2,1)S(1)} %behind.1.refs_1_), channel_id=1, source_target_pairs={{0,32},{32,64},{64,96},{96,128},{128,160},{160,192},{192,224},{224... | collective-permute-start | bytes 1572872 | tf_op jit(solution)/shard_map/ppermute | solution.py:391
  46.2 22.5 %collective-permute-start.4 = (bf16[2,128,1024]{2,1,0:T(8,128)(2,1)S(1)}, bf16[2,128,1024]{2,1,0:T(8,128)(2,1)}, u32[]{:S(2)}, u32[]{:S(2)}) collective-permute-start(bf16[2,128,1024]{2,1,0:T(8,128)(2,1)S(1)} %bitcast.17), channel_id=1, source_target_pairs={{0,2},{2,0},{1,3},{3,1},{4,6},{6,4},{5,7},{7,5},{8,10},{10,8},{9,1... | collective-permute-start | bytes 1572872 | tf_op jit(solution)/shard_map/ppermute | solution.py:384
  47.6 18.2 %all-to-all-start = ((bf16[8,2,4,32,128]{4,3,2,1,0:T(8,128)(2,1)}), bf16[8,2,4,32,128]{4,3,2,1,0:T(8,128)(2,1)S(1)}, u32[]{:S(2)}, u32[]{:S(2)}) async-start(bf16[8,2,4,32,128]{4,3,2,1,0:T(8,128)(2,1)} %get-tuple-element.7), calls=%async_computation | async-start | bytes 1048576 | tf_op jit(solution)/shard_map/all_to_all | solution.py:394
  53.8 14.9 %collective-permute-start.7 = (bf16[2,2,4,32,128]{4,3,2,1,0:T(8,128)(2,1)S(1)}, bf16[2,2,4,32,128]{4,3,2,1,0:T(8,128)(2,1)S(1)}, u32[]{:S(2)}, u32[]{:S(2)}) collective-permute-start(bf16[2,2,4,32,128]{4,3,2,1,0:T(8,128)(2,1)S(1)} %slice.17), channel_id=1, source_target_pairs={{0,32},{32,64},{64,96},{96,128},{128,160},{160,192},{192,224},{224... | collective-permute-start | bytes 393224 | tf_op jit(solution)/shard_map/ppermute | solution.py:392
  65.7 6.4 %collective-permute-start.8 = (bf16[2,2,4,32,128]{4,3,2,1,0:T(8,128)(2,1)}, bf16[2,2,4,32,128]{4,3,2,1,0:T(8,128)(2,1)S(1)}, u32[]{:S(2)}, u32[]{:S(2)}) collective-permute-start(bf16[2,2,4,32,128]{4,3,2,1,0:T(8,128)(2,1)} %slice.18), channel_id=1, source_target_pairs={{0,32},{32,64},{64,96},{96,128},{128,160},{160,192},{192,224},{224... | collective-permute-start | bytes 393224 | tf_op jit(solution)/shard_map/ppermute | solution.py:392
  74.1 17.4 %all-to-all-start.3 = ((bf16[16,128,256]{2,1,0:T(8,128)(2,1)}), bf16[16,128,256]{2,1,0:T(8,128)(2,1)S(1)}, u32[]{:S(2)}, u32[]{:S(2)}) async-start(bf16[16,128,256]{2,1,0:T(8,128)(2,1)} %bitcast.8), calls=%async_computation.3 | async-start | bytes 2097152 | tf_op jit(solution)/shard_map/all_to_all | solution.py:398
  80.4 1.0 copy-start.1
  95.9 12.9 %collective-permute-start.9 = (bf16[128,2048]{1,0:T(8,128)(2,1)S(1)}, bf16[128,2048]{1,0:T(8,128)(2,1)S(1)}, u32[]{:S(2)}, u32[]{:S(2)}) collective-permute-start(bf16[128,2048]{1,0:T(8,128)(2,1)S(1)} %project_next.1), channel_id=1, source_target_pairs={{0,2},{2,0},{1,3},{3,1},{4,6},{6,4},{5,7},{7,5},{8,10},{10,8},{9,1... | collective-permute-start | bytes 1572872 | tf_op jit(solution)/shard_map/ppermute | solution.py:402

commit v6 on v4

--- a/solution.py
+++ b/solution.py
@@ -57,21 +57,21 @@
     return result[:, :HS] / result[:, HS:]
 
 
-def pack_rest(qkv):
+def pack(qkv):
     _, frames, tok, model_width = qkv.shape
     half = model_width // 2
     groups = tok // GROUP
     step = 2
-
-    def body(qkv, queries, keyvals):
-        for device in range(PLANE):
-            for slot in range(ROUNDS + 2):
-                which, turn = (0, slot) if slot < ROUNDS else (slot - ROUNDS + 1, ROUNDS - 1)
-                target, place = (queries, slot) if slot < ROUNDS else (keyvals, slot - ROUNDS)
-                first = (device * ROUNDS + turn) * HS
-                block = qkv[which, :, :, first : first + HS].astype(F32).reshape(step, groups, GROUP, HS)
-                for group in range(groups):
-                    target[device, place, group] = block[:, group].reshape(step * GROUP, HS).astype(BF16)
+    contents = [[(0, turn) for turn in range(ROUNDS)]] + [[(1, turn), (2, turn)] for turn in range(ROUNDS)]
+
+    def body(qkv, *outs):
+        for out, slots in zip(outs, contents):
+            for device in range(PLANE):
+                for slot, (which, turn) in enumerate(slots):
+                    first = (device * ROUNDS + turn) * HS
+                    block = qkv[which, :, :, first : first + HS].astype(F32).reshape(step, groups, GROUP, HS)
+                    for group in range(groups):
+                        out[device, slot, group] = block[:, group].reshape(step * GROUP, HS).astype(BF16)
 
     rows = jax.ShapeDtypeStruct((PLANE, 2, groups, frames * GROUP, HS), BF16)
     rows_spec = pl.BlockSpec((PLANE, 2, groups, step * GROUP, HS), lambda f: (0, 0, 0, f, 0))
@@ -79,48 +79,49 @@
         body,
         grid=(frames // step,),
         in_specs=[pl.BlockSpec((3, step, tok, half), lambda f: (0, f, 0, 1))],
-        out_specs=[rows_spec] * 2,
-        out_shape=[rows] * 2,
+        out_specs=[rows_spec] * len(contents),
+        out_shape=[rows] * len(contents),
         compiler_params=kernel_params(PACK_VMEM),
         cost_estimate=QUICK,
-        name="pack_rest",
+        name="pack",
     )(qkv)
 
 
-def spatial_attend(own, far, mate_own, mate_far, after):
+def spatial_attend(own, queries_far, keyvals_far, mate_own, mate_far, after):
     _, frames, tok, width = own.shape
 
-    def body(own, far, mate_own, mate_far, after, out):
+    def body(own, queries_far, keyvals_far, mate_own, mate_far, after, out):
         blocks = [(f, slice(head * HS, (head + 1) * HS)) for f in range(frames) for head in range(width // HS)]
 
         def keyvals_of(which, f, cols):
-            return jnp.concatenate([ref[which, f, :, cols] for ref in (own, far, mate_own, mate_far)], axis=0)
+            parts = ((own, 1), (keyvals_far, 0), (mate_own, 1), (mate_far, 0))
+            return jnp.concatenate([ref[skip + which, f, :, cols] for ref, skip in parts], axis=0)
 
         for first in range(0, len(blocks), 8):
             batch = blocks[first : first + 8]
             scores = []
             for f, cols in batch:
-                queries = jnp.concatenate([own[0, f, :, cols], far[0, f, :, cols]], axis=0)
+                queries = jnp.concatenate([own[0, f, :, cols], queries_far[0, f, :, cols]], axis=0)
                 scores.append(
                     lax.dot_general(
-                        queries, keyvals_of(1, f, cols), (((1,), (1,)), ((), ())), preferred_element_type=F32
+                        queries, keyvals_of(0, f, cols), (((1,), (1,)), ((), ())), preferred_element_type=F32
                     )
                 )
             raised = [softmax_parts(block) for block in scores]
-            results = [weighted(block, keyvals_of(2, f, cols)).astype(BF16) for block, (f, cols) in zip(raised, batch)]
+            results = [weighted(block, keyvals_of(1, f, cols)).astype(BF16) for block, (f, cols) in zip(raised, batch)]
             for result, (f, cols) in zip(results, batch):
                 out[0, f, :, cols] = result[:tok]
                 out[1, f, :, cols] = result[tok:]
 
     return pl.pallas_call(
         body,
-        in_specs=[WHOLE] * 4 + [ANYWHERE],
+        in_specs=[WHOLE] * 5 + [ANYWHERE],
         out_specs=WHOLE,
         out_shape=jax.ShapeDtypeStruct((2, frames, tok, width), BF16),
         compiler_params=kernel_params(16),
         cost_estimate=QUICK,
         name="spatial",
-    )(own, far, mate_own, mate_far, after)
+    )(own, queries_far, keyvals_far, mate_own, mate_far, after)
 
 
 def temporal_scores(clips, place, lengths, queries, keyvals, first_query, first_key, bias, batch, store):
@@ -353,31 +354,25 @@
 
 def on_device(qkv, clip_lengths, wo):
     _, frames, tok, model_width = qkv.shape
-    half = model_width // 2
-    quarter = half // 2
+    quarter = model_width // 4
     x_place = lax.axis_index("xh")
     place = jnp.stack([lax.axis_index("z"), x_place, lax.axis_index("c")]).astype(jnp.int32)
 
-    groups = tok // GROUP
-    rows = frames * GROUP
-
-    def by_plane(block, turn):
-        split = block.reshape(block.shape[0], frames, groups, GROUP, PLANE, ROUNDS, HS)[:, :, :, :, :, turn]
-        return split.transpose(4, 0, 2, 1, 3, 5).reshape(PLANE, -1, groups, rows, HS)
-
     onward = [(i, (i + 1) % Z) for i in range(Z)]
-    queries, last_packed = pack_rest(qkv)
-    packed = (by_plane(qkv[1:, :, :, half:], 0), last_packed)
+    queries, *packed = pack(qkv)
     arrived = [lax.all_to_all(block, ("y", "xl"), 0, 0, tiled=True) for block in packed]
 
     own_cols = x_place * quarter
     far_cols = (1 - x_place) * quarter
     wo_mate = lax.ppermute(wo, "c", SWAP)
     own = lax.dynamic_slice(qkv, (0, 0, 0, own_cols), (3, frames, tok, quarter))
-    far = lax.ppermute(lax.dynamic_slice(qkv, (0, 0, 0, far_cols), (3, frames, tok, quarter)), "xh", SWAP)
+    keyvals_far = lax.dynamic_slice(qkv, (1, 0, 0, far_cols), (2, frames, tok, quarter))
+    keyvals_far = lax.ppermute(keyvals_far, "xh", SWAP)
+    queries_far = lax.dynamic_slice(qkv, (0, 0, 0, far_cols), (1, frames, tok, quarter))
+    queries_far = lax.ppermute(behind(queries_far, keyvals_far), "xh", SWAP)
     mate_own = lax.ppermute(own, "c", SWAP)
-    mate_far = lax.ppermute(far, "c", SWAP)
-    near = spatial_attend(own, far, mate_own, mate_far, wo_mate)
+    mate_far = lax.ppermute(keyvals_far, "c", SWAP)
+    near = spatial_attend(own, queries_far, keyvals_far, mate_own, mate_far, wo_mate)
     near = near.reshape(2, frames * tok, quarter)
     far = lax.ppermute(near, "xh", SWAP)
 

time: 111 us -> 111 us (level)
  waiting for transfers between devices: 44.8 us -> 39.7 us
  starting transfers between devices: 32.8 us -> 37.5 us
    ppermute x2, waiting for transfers between devices: 11.3 us -> 6.41 us  [on_device(): before.append(lax.ppermute(got, 'z', onward))]
    ppermute x2, waiting for transfers between devices: 3.41 us -> 0.03 us  [on_device(): before2.append(lax.ppermute(before[-1][PLANE - EARLY:], 'z', onward))]
    all_to_all x1, waiting for transfers between devices: 0.01 us -> 3.37 us  [on_device(): queries = lax.all_to_all(queries, ('y', 'xl'), 0, 0, tiled=True)]
    dynamic_slice x1 -> x3, local copies, waits for them, and re-layouts: 1.53 us -> 3.26 us  [the longest x1 1.21 us: on_device(): own = lax.dynamic_slice(qkv, (0, 0, 0, own_cols), (3, frames, tok, quarter))]
    ppermute x2 -> x3, waiting for transfers between devices: 11.7 us -> 13.2 us  [the longest x1 8.75 us: on_device(): queries_far = lax.ppermute(behind(queries_far, keyvals_far), 'xh', SWAP)]
    ppermute x2 -> x3, starting transfers between devices: 2.21 us -> 3.71 us  [the longest x1 2.21 us: on_device(): keyvals_far = lax.ppermute(keyvals_far, 'xh', SWAP)]
    all_to_all x2, waiting for transfers between devices: 8.26 us -> 6.87 us  [on_device(): lax.all_to_all(block, ('y', 'xl'), 0, 0, tiled=True)]
    slice x1 -> x0, local copies, waits for them, and re-layouts: 1.29 us -> none  [on_device(): packed = (by_plane(qkv[1:, :, :, half:], 0), last_packed)]
  transfers between devices with their start and end apart: 14 -> 15, of which waited for: 8 -> 7; matrix products, arithmetic and copies ran while one was open for 4% -> 4% of each run, Pallas kernels for 17% -> 17%
where the time goes in v6:
time: 111 us; the launch traced here: 109 us
  waiting for transfers between devices  39.7 us (36%)
  starting transfers between devices  37.5 us (34%)
  Pallas kernels  26.8 us (24%)
  local copies, waits for them, and re-layouts  4.99 us (4%)
    all_to_all x2, starting transfers between devices, on_device(): lax.all_to_all(block, ('y', 'xl'), 0, 0, tiled=True)  10.8 us
    pallas_call x2, Pallas kernels, project_last(): pl.pallas_call(body, in_specs=[SMEM] + [WHOLE] * 2 + [IN_HBM] * 2, out_sp...  9.68 us
    ppermute x1, waiting for transfers between devices, on_device(): queries_far = lax.ppermute(behind(queries_far, keyvals_far), 'xh', SWAP)  8.75 us
    all_to_all x1, starting transfers between devices, on_device(): lax.all_to_all(sent, ('y', 'xl', 'xh'), 0, 0, tiled=True)  7.02 us
    all_to_all x2, waiting for transfers between devices, on_device(): lax.all_to_all(block, ('y', 'xl'), 0, 0, tiled=True)  6.87 us
    ppermute x2, waiting for transfers between devices, on_device(): before.append(lax.ppermute(got, 'z', onward))  6.41 us
    all_to_all x1, starting transfers between devices, on_device(): queries = lax.all_to_all(queries, ('y', 'xl'), 0, 0, tiled=True)  5.73 us
    ppermute x1, waiting for transfers between devices, on_device(): arrived = lax.ppermute(for_next, 'xh', SWAP)  5.44 us
  transfers between devices with their start and end apart: 15, of which 7 were waited for; matrix products, arithmetic and copies ran while one was open for 4% of the time, Pallas kernels for 17%

profile of v6, /device:TPU:2, one launch (start us, length us, event | category | flops | bytes accessed | tf_op | source)
XLA Modules:
  0.0 109.2 jit_solution(8221560285099884267)
XLA Ops:
  0.0 0.0 collective-permute-start.4
  0.0 1.1 constant_dynamic-slice_fusion
  1.1 2.2 %collective-permute-start = (bf16[2,4,32,1024]{3,2,1,0:T(8,128)(2,1)S(1)}, bf16[2,4,32,1024]{3,2,1,0:T(8,128)(2,1)S(1)}, u32[]{:S(2)}, u32[]{:S(2)}) collective-permute-start(bf16[2,4,32,1024]{3,2,1,0:T(8,128)(2,1)S(1)} %constant_dynamic-slice_fusion), channel_id=1, source_target_pairs={{0,2},{2,0},{1,3},{3,1},{4,6},{6,4},{5,7},{7,5},{8,10},{10,8},{9,1... | collective-permute-start | bytes 1572872 | tf_op jit(solution)/shard_map/ppermute | solution.py:370
  3.3 2.4 %pack.1 = (bf16[8,2,4,32,128]{4,3,2,1,0:T(8,128)(2,1)}, bf16[8,2,4,32,128]{4,3,2,1,0:T(8,128)(2,1)}, bf16[8,2,4,32,128]{4,3,2,1,0:T(8,128)(2,1)}) custom-call(bf16[3,4,32,4096]{3,2,1,0:T(8,128)(2,1)} %qkv.1), custom_call_target="tpu_custom_call" | custom-call | flops 1024 | bytes 1024 | tf_op jit(solution)/shard_map/pack/pallas_call | solution.py:78
  5.7 5.9 %all-to-all-start.1 = ((bf16[8,2,4,32,128]{4,3,2,1,0:T(8,128)(2,1)}), bf16[8,2,4,32,128]{4,3,2,1,0:T(8,128)(2,1)S(1)}, u32[]{:S(2)}, u32[]{:S(2)}) async-start(bf16[8,2,4,32,128]{4,3,2,1,0:T(8,128)(2,1)} %get-tuple-element.9), calls=%async_computation.1 | async-start | bytes 1048576 | tf_op jit(solution)/shard_map/all_to_all | solution.py:363
  11.7 1.2 %constant_dynamic-slice_fusion.2.own = bf16[3,4,32,1024]{3,2,1,0:T(8,128)(2,1)S(1)} fusion(bf16[3,4,32,4096]{3,2,1,0:T(8,128)(2,1)} %qkv.1, s32[]{:T(128)S(6)} %select_n.7), kind=kLoop, calls=%fused_computation.2 | loop fusion | bytes 1572868 | tf_op jit(solution)/shard_map/dynamic_slice | solution.py:368
  12.9 0.1 collective-permute-start.2
  13.0 4.4 %collective-permute-done.refs_1_.keyvals_far = bf16[2,4,32,1024]{3,2,1,0:T(8,128)(2,1)S(1)} collective-permute-done((bf16[2,4,32,1024]{3,2,1,0:T(8,128)(2,1)S(1)}, bf16[2,4,32,1024]{3,2,1,0:T(8,128)(2,1)S(1)}, u32[]{:S(2)}, u32[]{:S(2)}) %collective-permute-start) | collective-permute-done | bytes 524320 | tf_op jit(solution)/shard_map/ppermute | solution.py:370
  17.4 0.0 collective-permute-start.3
  17.4 6.9 %all-to-all-done.1.refs_0_ = bf16[8,2,4,32,128]{4,3,2,1,0:T(8,128)(2,1)S(1)} async-done(((bf16[8,2,4,32,128]{4,3,2,1,0:T(8,128)(2,1)}), bf16[8,2,4,32,128]{4,3,2,1,0:T(8,128)(2,1)S(1)}, u32[]{:S(2)}, u32[]{:S(2)}) %all-to-all-start.1) | async-done | bytes 524320 | tf_op jit(solution)/shard_map/all_to_all | solution.py:363
  24.3 4.8 %all-to-all-start.2 = ((bf16[8,2,4,32,128]{4,3,2,1,0:T(8,128)(2,1)}), bf16[8,2,4,32,128]{4,3,2,1,0:T(8,128)(2,1)S(1)}, u32[]{:S(2)}, u32[]{:S(2)}) async-start(bf16[8,2,4,32,128]{4,3,2,1,0:T(8,128)(2,1)} %get-tuple-element.10), calls=%async_computation.2 | async-start | bytes 1048576 | tf_op jit(solution)/shard_map/all_to_all | solution.py:363
  29.1 1.0 constant_dynamic-slice_fusion.1.refs_0_
  30.1 1.5 %collective-permute-start.1 = (bf16[1,4,32,1024]{3,2,1,0:T(8,128)(2,1)S(1)}, bf16[1,4,32,1024]{3,2,1,0:T(8,128)(2,1)S(1)}, u32[]{:S(2)}, u32[]{:S(2)}) collective-permute-start(bf16[1,4,32,1024]{3,2,1,0:T(8,128)(2,1)S(1)} %behind.2), channel_id=1, source_target_pairs={{0,2},{2,0},{1,3},{3,1},{4,6},{6,4},{5,7},{7,5},{8,10},{10,8},{9,1... | collective-permute-start | bytes 786440 | tf_op jit(solution)/shard_map/ppermute | solution.py:372
  31.6 1.9 %collective-permute-start.6 = (bf16[8,2,4,32,128]{4,3,2,1,0:T(8,128)(2,1)S(1)}, bf16[8,2,4,32,128]{4,3,2,1,0:T(8,128)(2,1)S(1)}, u32[]{:S(2)}, u32[]{:S(2)}) collective-permute-start(bf16[8,2,4,32,128]{4,3,2,1,0:T(8,128)(2,1)S(1)} %all-to-all-done.1.refs_0_), channel_id=1, source_target_pairs={{0,32},{32,64},{64,96},{96,128},{128,160},{160,192},{192,224},{224... | collective-permute-start | bytes 1572872 | tf_op jit(solution)/shard_map/ppermute | solution.py:384
  33.5 8.8 %collective-permute-done.1.queries_far = bf16[1,4,32,1024]{3,2,1,0:T(8,128)(2,1)S(1)} collective-permute-done((bf16[1,4,32,1024]{3,2,1,0:T(8,128)(2,1)S(1)}, bf16[1,4,32,1024]{3,2,1,0:T(8,128)(2,1)S(1)}, u32[]{:S(2)}, u32[]{:S(2)}) %collective-permute-start.1) | collective-permute-done | bytes 262176 | tf_op jit(solution)/shard_map/ppermute | solution.py:372
  42.2 0.0 collective-permute-done.2.mate_own
  42.2 0.0 collective-permute-done.3.mate_far
  42.3 0.0 collective-permute-done.4.after.wo_mate
  42.3 3.0 %spatial.1 = bf16[2,4,32,1024]{3,2,1,0:T(8,128)(2,1)S(1)} custom-call(bf16[3,4,32,1024]{3,2,1,0:T(8,128)(2,1)S(1)} %constant_dynamic-slice_fusion.2.own, bf16[1,4,32,1024]{3,2,1,0:T(8,128)(2,1)S(1)} %collective-permute-done.1.queries_far, bf16[2,4,32,1024]{3,2,1,0:T(8,128)(2,1)S(1)} %collective-permute-done.refs_1_.keyvals_far, ...), custom_call_target="tpu_custom_call" | custom-call | flops 1024 | bytes 1024 | tf_op jit(solution)/shard_map/spatial/pallas_call | solution.py:116
  45.3 0.0 copy-start
  45.3 0.0 copy-start.2
  45.3 0.0 all-to-all-done.2.refs_0_
  45.3 2.0 %collective-permute-start.7 = (bf16[8,2,4,32,128]{4,3,2,1,0:T(8,128)(2,1)S(1)}, bf16[8,2,4,32,128]{4,3,2,1,0:T(8,128)(2,1)S(1)}, u32[]{:S(2)}, u32[]{:S(2)}) collective-permute-start(bf16[8,2,4,32,128]{4,3,2,1,0:T(8,128)(2,1)S(1)} %behind.3.refs_1_), channel_id=1, source_target_pairs={{0,32},{32,64},{64,96},{96,128},{128,160},{160,192},{192,224},{224... | collective-permute-start | bytes 1572872 | tf_op jit(solution)/shard_map/ppermute | solution.py:384
  47.3 2.1 %collective-permute-start.5 = (bf16[2,128,1024]{2,1,0:T(8,128)(2,1)S(1)}, bf16[2,128,1024]{2,1,0:T(8,128)(2,1)}, u32[]{:S(2)}, u32[]{:S(2)}) collective-permute-start(bf16[2,128,1024]{2,1,0:T(8,128)(2,1)S(1)} %bitcast.10), channel_id=1, source_target_pairs={{0,2},{2,0},{1,3},{3,1},{4,6},{6,4},{5,7},{7,5},{8,10},{10,8},{9,1... | collective-permute-start | bytes 1572872 | tf_op jit(solution)/shard_map/ppermute | solution.py:377
  49.5 5.7 %all-to-all-start = ((bf16[8,2,4,32,128]{4,3,2,1,0:T(8,128)(2,1)}), bf16[8,2,4,32,128]{4,3,2,1,0:T(8,128)(2,1)S(1)}, u32[]{:S(2)}, u32[]{:S(2)}) async-start(bf16[8,2,4,32,128]{4,3,2,1,0:T(8,128)(2,1)} %get-tuple-element.8), calls=%async_computation | async-start | bytes 1048576 | tf_op jit(solution)/shard_map/all_to_all | solution.py:387
  55.2 0.0 collective-permute-done.6.refs_2_
  55.2 2.0 %collective-permute-start.8 = (bf16[2,2,4,32,128]{4,3,2,1,0:T(8,128)(2,1)S(1)}, bf16[2,2,4,32,128]{4,3,2,1,0:T(8,128)(2,1)S(1)}, u32[]{:S(2)}, u32[]{:S(2)}) collective-permute-start(bf16[2,2,4,32,128]{4,3,2,1,0:T(8,128)(2,1)S(1)} %slice.8), channel_id=1, source_target_pairs={{0,32},{32,64},{64,96},{96,128},{128,160},{160,192},{192,224},{224... | collective-permute-start | bytes 393224 | tf_op jit(solution)/shard_map/ppermute | solution.py:385
  57.2 6.4 %collective-permute-done.7.refs_3_ = bf16[8,2,4,32,128]{4,3,2,1,0:T(8,128)(2,1)S(1)} collective-permute-done((bf16[8,2,4,32,128]{4,3,2,1,0:T(8,128)(2,1)S(1)}, bf16[8,2,4,32,128]{4,3,2,1,0:T(8,128)(2,1)S(1)}, u32[]{:S(2)}, u32[]{:S(2)}) %collective-permute-start.7) | collective-permute-done | bytes 524320 | tf_op jit(solution)/shard_map/ppermute | solution.py:384
  63.6 0.7 slice.9
  64.3 0.0 collective-permute-start.9
  64.3 0.1 pad_add_fusion.place
  64.3 3.4 %all-to-all-done.queries = bf16[8,2,4,32,128]{4,3,2,1,0:T(8,128)(2,1)S(1)} async-done(((bf16[8,2,4,32,128]{4,3,2,1,0:T(8,128)(2,1)}), bf16[8,2,4,32,128]{4,3,2,1,0:T(8,128)(2,1)S(1)}, u32[]{:S(2)}, u32[]{:S(2)}) %all-to-all-start) | async-done | bytes 524320 | tf_op jit(solution)/shard_map/all_to_all | solution.py:387
  67.7 0.0 copy-done.2
  67.7 2.9 %temporal_late.1.refs_6_ = bf16[8,2,128,256]{3,2,1,0:T(8,128)(2,1)} custom-call(s32[3]{0:T(128)S(1)} %pad_add_fusion.place, s32[16]{0:T(128)S(1)} %copy-done.2, bf16[8,2,4,32,128]{4,3,2,1,0:T(8,128)(2,1)S(1)} %all-to-all-done.queries, bf16[8,2,4,32,128]{4,3,2,1,0:T(8,128)(2,1)S(1)} %all-to-all-done.1.refs_0_, bf16[8,2,4,32,128]{4,3,2,1,0:T(8,128)(2,1)S(1)} %behind.3.refs_1_, ...), custom_call_target="tpu_custom_call" | custom-call | flops 1024 | bytes 1024 | tf_op jit(solution)/shard_map/temporal_late/pallas_call | solution.py:190
  70.6 0.0 copy-done
  70.6 0.0 collective-permute-done.8.refs_4_
  70.6 0.0 collective-permute-done.5.far.refs_7_
  70.6 0.0 collective-permute-done.9.refs_5_
  70.7 2.0 %temporal_early.1 = bf16[8,2,128,256]{3,2,1,0:T(8,128)(2,1)} custom-call(s32[3]{0:T(128)S(1)} %pad_add_fusion.place, s32[16]{0:T(128)S(1)} %copy-done.2, bf16[8,2,4,32,128]{4,3,2,1,0:T(8,128)(2,1)S(1)} %all-to-all-done.queries, bf16[8,2,4,32,128]{4,3,2,1,0:T(8,128)(2,1)S(1)} %all-to-all-done.1.refs_0_, ...), custom_call_target="tpu_custom_call", output_to_operand_aliasing={{}: (9, {})} | custom-call | flops 1024 | bytes 1024 | tf_op jit(solution)/shard_map/temporal_early/pallas_call | solution.py:218
  72.7 7.0 %all-to-all-start.3 = ((bf16[16,128,256]{2,1,0:T(8,128)(2,1)}), bf16[16,128,256]{2,1,0:T(8,128)(2,1)S(1)}, u32[]{:S(2)}, u32[]{:S(2)}) async-start(bf16[16,128,256]{2,1,0:T(8,128)(2,1)} %bitcast.4), calls=%async_computation.3 | async-start | bytes 2097152 | tf_op jit(solution)/shard_map/all_to_all | solution.py:391
  79.7 0.0 copy-start.1
  79.7 1.0 copy-done.1
  80.7 5.4 %project_first.1.partial = f32[2,2,128,1024]{3,2,1,0:T(8,128)S(1)} custom-call(s32[3]{0:T(128)S(1)} %pad_add_fusion.place, bf16[2,128,1024]{2,1,0:T(8,128)(2,1)S(1)} %bitcast.11, bf16[2,128,1024]{2,1,0:T(8,128)(2,1)} %collective-permute-done.5.far.refs_7_, bf16[4096,1024]{1,0:T(8,128)(2,1)} %wo.5, bf16[4096,1024]{1,0:T(8,128)(2,1)} %collective-permute-done.4.after.wo_mate), custom_call_target="tpu_custom_call" | custom-call | flops 1024 | bytes 1024 | tf_op jit(solution)/shard_map/project_first/pallas_call | solution.py:266
  86.1 4.4 %all-to-all-done.3 = bf16[16,128,256]{2,1,0:T(8,128)(2,1)S(1)} async-done(((bf16[16,128,256]{2,1,0:T(8,128)(2,1)}), bf16[16,128,256]{2,1,0:T(8,128)(2,1)S(1)}, u32[]{:S(2)}, u32[]{:S(2)}) %all-to-all-start.3) | async-done | bytes 1048608 | tf_op jit(solution)/shard_map/all_to_all | solution.py:391
  90.5 4.4 %project_next.1 = bf16[128,2048]{1,0:T(8,128)(2,1)S(1)} custom-call(s32[3]{0:T(128)S(1)} %pad_add_fusion.place, f32[2,2,128,1024]{3,2,1,0:T(8,128)S(1)} %project_first.1.partial, bf16[8,2,128,256]{3,2,1,0:T(8,128)(2,1)S(1)} %bitcast.7, bf16[4096,1024]{1,0:T(8,128)(2,1)} %wo.5, bf16[4096,1024]{1,0:T(8,128)(2,1)} %collective-permute-done.4.after.wo_mate), custom_call_target="tpu_custom_call" | custom-call | flops 1024 | bytes 1024 | tf_op jit(solution)/shard_map/project_next/pallas_call | solution.py:298
  94.9 2.1 %collective-permute-start.10 = (bf16[128,2048]{1,0:T(8,128)(2,1)S(1)}, bf16[128,2048]{1,0:T(8,128)(2,1)S(1)}, u32[]{:S(2)}, u32[]{:S(2)}) collective-permute-start(bf16[128,2048]{1,0:T(8,128)(2,1)S(1)} %project_next.1), channel_id=1, source_target_pairs={{0,2},{2,0},{1,3},{3,1},{4,6},{6,4},{5,7},{7,5},{8,10},{10,8},{9,1... | collective-permute-start | bytes 1572872 | tf_op jit(solution)/shard_map/ppermute | solution.py:395
  97.0 5.3 %project_own.1.mixed = bf16[128,4096]{1,0:T(8,128)(2,1)} custom-call(s32[3]{0:T(128)S(1)} %pad_add_fusion.place, f32[2,2,128,1024]{3,2,1,0:T(8,128)S(1)} %project_first.1.partial, bf16[8,2,128,256]{3,2,1,0:T(8,128)(2,1)S(1)} %bitcast.8, bf16[4096,1024]{1,0:T(8,128)(2,1)} %wo.5, bf16[4096,1024]{1,0:T(8,128)(2,1)} %collective-permute-done.4.after.wo_mate), custom_call_target="tpu_custom_call" | custom-call | flops 1024 | bytes 1024 | tf_op jit(solution)/shard_map/project_own/pallas_call | solution.py:298
  102.3 5.4 %collective-permute-done.10.arrived = bf16[128,2048]{1,0:T(8,128)(2,1)S(1)} collective-permute-done((bf16[128,2048]{1,0:T(8,128)(2,1)S(1)}, bf16[128,2048]{1,0:T(8,128)(2,1)S(1)}, u32[]{:S(2)}, u32[]{:S(2)}) %collective-permute-start.10) | collective-permute-done | bytes 524320 | tf_op jit(solution)/shard_map/ppermute | solution.py:395
  107.8 1.4 %put_arrived.1 = bf16[128,4096]{1,0:T(8,128)(2,1)} custom-call(s32[3]{0:T(128)S(1)} %pad_add_fusion.place, bf16[128,4096]{1,0:T(8,128)(2,1)} %project_own.1.mixed, bf16[128,2048]{1,0:T(8,128)(2,1)S(1)} %collective-permute-done.10.arrived), custom_call_target="tpu_custom_call", output_to_operand_aliasing={{}: (1, {})} | custom-call | flops 1024 | bytes 1024 | tf_op jit(solution)/shard_map/put_arrived/pallas_call | solution.py:339
  (3 shorter events, 0.0 us)
Async XLA Ops:
  0.0 42.3 %collective-permute-start.4 = (bf16[4096,1024]{1,0:T(8,128)(2,1)}, bf16[4096,1024]{1,0:T(8,128)(2,1)}, u32[]{:S(2)}, u32[]{:S(2)}) collective-permute-start(bf16[4096,1024]{1,0:T(8,128)(2,1)} %wo.5), channel_id=1, source_target_pairs={{0,1},{1,0},{2,3},{3,2},{4,5},{5,4},{6,7},{7,6},{8,9},{9,8},{10,11... | collective-permute-start | bytes 25165832 | tf_op jit(solution)/shard_map/ppermute | solution.py:367
  1.1 16.3 %collective-permute-start = (bf16[2,4,32,1024]{3,2,1,0:T(8,128)(2,1)S(1)}, bf16[2,4,32,1024]{3,2,1,0:T(8,128)(2,1)S(1)}, u32[]{:S(2)}, u32[]{:S(2)}) collective-permute-start(bf16[2,4,32,1024]{3,2,1,0:T(8,128)(2,1)S(1)} %constant_dynamic-slice_fusion), channel_id=1, source_target_pairs={{0,2},{2,0},{1,3},{3,1},{4,6},{6,4},{5,7},{7,5},{8,10},{10,8},{9,1... | collective-permute-start | bytes 1572872 | tf_op jit(solution)/shard_map/ppermute | solution.py:370
  5.7 18.5 %all-to-all-start.1 = ((bf16[8,2,4,32,128]{4,3,2,1,0:T(8,128)(2,1)}), bf16[8,2,4,32,128]{4,3,2,1,0:T(8,128)(2,1)S(1)}, u32[]{:S(2)}, u32[]{:S(2)}) async-start(bf16[8,2,4,32,128]{4,3,2,1,0:T(8,128)(2,1)} %get-tuple-element.9), calls=%async_computation.1 | async-start | bytes 1048576 | tf_op jit(solution)/shard_map/all_to_all | solution.py:363
  12.9 29.4 %collective-permute-start.2 = (bf16[3,4,32,1024]{3,2,1,0:T(8,128)(2,1)S(1)}, bf16[3,4,32,1024]{3,2,1,0:T(8,128)(2,1)}, u32[]{:S(2)}, u32[]{:S(2)}) collective-permute-start(bf16[3,4,32,1024]{3,2,1,0:T(8,128)(2,1)S(1)} %constant_dynamic-slice_fusion.2.own), channel_id=1, source_target_pairs={{0,1},{1,0},{2,3},{3,2},{4,5},{5,4},{6,7},{7,6},{8,9},{9,8},{10,11... | collective-permute-start | bytes 2359304 | tf_op jit(solution)/shard_map/ppermute | solution.py:373
  17.4 24.8 %collective-permute-start.3 = (bf16[2,4,32,1024]{3,2,1,0:T(8,128)(2,1)S(1)}, bf16[2,4,32,1024]{3,2,1,0:T(8,128)(2,1)}, u32[]{:S(2)}, u32[]{:S(2)}) collective-permute-start(bf16[2,4,32,1024]{3,2,1,0:T(8,128)(2,1)S(1)} %collective-permute-done.refs_1_.keyvals_far), channel_id=1, source_target_pairs={{0,1},{1,0},{2,3},{3,2},{4,5},{5,4},{6,7},{7,6},{8,9},{9,8},{10,11... | collective-permute-start | bytes 1572872 | tf_op jit(solution)/shard_map/ppermute | solution.py:374
  24.3 21.0 %all-to-all-start.2 = ((bf16[8,2,4,32,128]{4,3,2,1,0:T(8,128)(2,1)}), bf16[8,2,4,32,128]{4,3,2,1,0:T(8,128)(2,1)S(1)}, u32[]{:S(2)}, u32[]{:S(2)}) async-start(bf16[8,2,4,32,128]{4,3,2,1,0:T(8,128)(2,1)} %get-tuple-element.10), calls=%async_computation.2 | async-start | bytes 1048576 | tf_op jit(solution)/shard_map/all_to_all | solution.py:363
  30.1 12.2 %collective-permute-start.1 = (bf16[1,4,32,1024]{3,2,1,0:T(8,128)(2,1)S(1)}, bf16[1,4,32,1024]{3,2,1,0:T(8,128)(2,1)S(1)}, u32[]{:S(2)}, u32[]{:S(2)}) collective-permute-start(bf16[1,4,32,1024]{3,2,1,0:T(8,128)(2,1)S(1)} %behind.2), channel_id=1, source_target_pairs={{0,2},{2,0},{1,3},{3,1},{4,6},{6,4},{5,7},{7,5},{8,10},{10,8},{9,1... | collective-permute-start | bytes 786440 | tf_op jit(solution)/shard_map/ppermute | solution.py:372
  31.6 23.6 %collective-permute-start.6 = (bf16[8,2,4,32,128]{4,3,2,1,0:T(8,128)(2,1)S(1)}, bf16[8,2,4,32,128]{4,3,2,1,0:T(8,128)(2,1)S(1)}, u32[]{:S(2)}, u32[]{:S(2)}) collective-permute-start(bf16[8,2,4,32,128]{4,3,2,1,0:T(8,128)(2,1)S(1)} %all-to-all-done.1.refs_0_), channel_id=1, source_target_pairs={{0,32},{32,64},{64,96},{96,128},{128,160},{160,192},{192,224},{224... | collective-permute-start | bytes 1572872 | tf_op jit(solution)/shard_map/ppermute | solution.py:384
  45.3 25.3 %copy-start = (bf16[2,4,32,1024]{3,2,1,0:T(8,128)(2,1)}, bf16[2,4,32,1024]{3,2,1,0:T(8,128)(2,1)S(1)}, u32[]{:S(2)}) copy-start(bf16[2,4,32,1024]{3,2,1,0:T(8,128)(2,1)S(1)} %spatial.1) | copy-start | bytes 1572868
  45.3 22.4 %copy-start.2 = (s32[16]{0:T(128)S(1)}, s32[16]{0:T(128)}, u32[]{:S(2)}) copy-start(s32[16]{0:T(128)} %lengths.3) | copy-start | bytes 196
  45.3 18.3 %collective-permute-start.7 = (bf16[8,2,4,32,128]{4,3,2,1,0:T(8,128)(2,1)S(1)}, bf16[8,2,4,32,128]{4,3,2,1,0:T(8,128)(2,1)S(1)}, u32[]{:S(2)}, u32[]{:S(2)}) collective-permute-start(bf16[8,2,4,32,128]{4,3,2,1,0:T(8,128)(2,1)S(1)} %behind.3.refs_1_), channel_id=1, source_target_pairs={{0,32},{32,64},{64,96},{96,128},{128,160},{160,192},{192,224},{224... | collective-permute-start | bytes 1572872 | tf_op jit(solution)/shard_map/ppermute | solution.py:384
  47.3 23.3 %collective-permute-start.5 = (bf16[2,128,1024]{2,1,0:T(8,128)(2,1)S(1)}, bf16[2,128,1024]{2,1,0:T(8,128)(2,1)}, u32[]{:S(2)}, u32[]{:S(2)}) collective-permute-start(bf16[2,128,1024]{2,1,0:T(8,128)(2,1)S(1)} %bitcast.10), channel_id=1, source_target_pairs={{0,2},{2,0},{1,3},{3,1},{4,6},{6,4},{5,7},{7,5},{8,10},{10,8},{9,1... | collective-permute-start | bytes 1572872 | tf_op jit(solution)/shard_map/ppermute | solution.py:377
  49.5 18.3 %all-to-all-start = ((bf16[8,2,4,32,128]{4,3,2,1,0:T(8,128)(2,1)}), bf16[8,2,4,32,128]{4,3,2,1,0:T(8,128)(2,1)S(1)}, u32[]{:S(2)}, u32[]{:S(2)}) async-start(bf16[8,2,4,32,128]{4,3,2,1,0:T(8,128)(2,1)} %get-tuple-element.8), calls=%async_computation | async-start | bytes 1048576 | tf_op jit(solution)/shard_map/all_to_all | solution.py:387
  55.2 15.4 %collective-permute-start.8 = (bf16[2,2,4,32,128]{4,3,2,1,0:T(8,128)(2,1)S(1)}, bf16[2,2,4,32,128]{4,3,2,1,0:T(8,128)(2,1)S(1)}, u32[]{:S(2)}, u32[]{:S(2)}) collective-permute-start(bf16[2,2,4,32,128]{4,3,2,1,0:T(8,128)(2,1)S(1)} %slice.8), channel_id=1, source_target_pairs={{0,32},{32,64},{64,96},{96,128},{128,160},{160,192},{192,224},{224... | collective-permute-start | bytes 393224 | tf_op jit(solution)/shard_map/ppermute | solution.py:385
  64.3 6.4 %collective-permute-start.9 = (bf16[2,2,4,32,128]{4,3,2,1,0:T(8,128)(2,1)}, bf16[2,2,4,32,128]{4,3,2,1,0:T(8,128)(2,1)S(1)}, u32[]{:S(2)}, u32[]{:S(2)}) collective-permute-start(bf16[2,2,4,32,128]{4,3,2,1,0:T(8,128)(2,1)} %slice.9), channel_id=1, source_target_pairs={{0,32},{32,64},{64,96},{96,128},{128,160},{160,192},{192,224},{224... | collective-permute-start | bytes 393224 | tf_op jit(solution)/shard_map/ppermute | solution.py:385
  72.7 17.8 %all-to-all-start.3 = ((bf16[16,128,256]{2,1,0:T(8,128)(2,1)}), bf16[16,128,256]{2,1,0:T(8,128)(2,1)S(1)}, u32[]{:S(2)}, u32[]{:S(2)}) async-start(bf16[16,128,256]{2,1,0:T(8,128)(2,1)} %bitcast.4), calls=%async_computation.3 | async-start | bytes 2097152 | tf_op jit(solution)/shard_map/all_to_all | solution.py:391
  79.7 1.0 copy-start.1
  94.9 12.9 %collective-permute-start.10 = (bf16[128,2048]{1,0:T(8,128)(2,1)S(1)}, bf16[128,2048]{1,0:T(8,128)(2,1)S(1)}, u32[]{:S(2)}, u32[]{:S(2)}) collective-permute-start(bf16[128,2048]{1,0:T(8,128)(2,1)S(1)} %project_next.1), channel_id=1, source_target_pairs={{0,2},{2,0},{1,3},{3,1},{4,6},{6,4},{5,7},{7,5},{8,10},{10,8},{9,1... | collective-permute-start | bytes 1572872 | tf_op jit(solution)/shard_map/ppermute | solution.py:395
